TPU v7x, 32 devices: a whole 2x2x4 slice. The times are simulated.
32 devices in a mesh: dp: 4 (over y, x), mp: 8 (over z, core).
Axes of the slice: x: 2, y: 2, z: 4, core: 2. Of those that a mesh axis runs over, the one named last changes fastest.
Arguments:
- inputs: bfloat16 [4, 2304, 1024], P('dp', 'mp'), may hold values from -6 to 6
- resets: int32 [4, 1024], P('dp'), may hold values from 0 to 1
- owners: int32 [57], replicated, may hold values from 0 to 3, as said below
- kernel: float32 [96, 2304, 256], P('dp', 'mp'), may hold values from -0.09375 to 0.09375
- kernel_first: float32 [96, 2304, 256], P('dp', 'mp'), may hold values from -0.00011799647 to 0.00011799647
- kernel_second: float32 [96, 2304, 256], P('dp', 'mp'), may hold values from 3.1389873e-11 to 1.255595e-10
- bias_rows: float32 [12, 2304], P('dp', 'mp'), may hold values from -0.18 to 0.18
- bias_first: float32 [12, 2304], P('dp', 'mp'), may hold values from -0.00011799647 to 0.00011799647
- bias_second: float32 [12, 2304], P('dp', 'mp'), may hold values from 3.1389873e-11 to 1.255595e-10
- cotangent: bfloat16 [4, 2304, 1024], P('dp', 'mp'), may hold values from -15 to 15
Outputs:
- outputs: bfloat16 [4, 2304, 1024], P('dp', 'mp')
- input_grads: bfloat16 [4, 2304, 1024], P('dp', 'mp')
- kernel_new: float32 [96, 2304, 256], P('dp', 'mp')
- kernel_first_new: float32 [96, 2304, 256], P('dp', 'mp')
- kernel_second_new: float32 [96, 2304, 256], P('dp', 'mp')
- bias_new: float32 [12, 2304], P('dp', 'mp')
- bias_first_new: float32 [12, 2304], P('dp', 'mp')
- bias_second_new: float32 [12, 2304], P('dp', 'mp')
- grad_norm: float32 [], replicated
Inputs may be any that keep to these rules, and one draw needn't show every extreme that they name: Entries 0 to 53 name the dp index owning each kernel block, the last 3 the owners of the three gates' biases. Each dp index owns at most 24 kernel blocks, and one owns exactly 24.
All inputs are finite; a program needn't handle non-finite values.
Results may differ from a plain program's by a relative error of at most 0.0065.
Values may be sent and summed in bfloat16 or wider, within the bound.
A program may use at most 256 MiB of HBM per device.

v0:
```python
import jax
import jax.numpy as jnp
from jax import lax
from jax.sharding import PartitionSpec as P

D = 2304
STEP = 10


def earlier_count(owned):
    number = owned.shape[0]
    places = jnp.arange(number, dtype=jnp.int32)
    earlier = (owned[:, None] == owned[None, :]) & (places[None, :] < places[:, None])
    return jnp.sum(earlier.astype(jnp.int32), axis=1)


def slot_sources(slot, count):
    places = jnp.arange(slot.shape[0], dtype=jnp.int32)
    hits = slot[None, :] == jnp.arange(count, dtype=jnp.int32)[:, None]
    source = jnp.sum(jnp.where(hits, places[None, :], 0), axis=1)
    return (source, jnp.any(hits, axis=1).astype(jnp.float32))


def shift_later(values):
    return jnp.pad(values, ((0, 0), (0, 0), (1, 0)))[:, :, :-1]


def shift_earlier(values):
    return jnp.pad(values, ((0, 0), (0, 0), (0, 1)))[:, :, 1:]


def combine(earlier, later):
    return (earlier[0] * later[0], later[0] * earlier[1] + later[1])


def pooled(preact, keeping):
    channels = preact.shape[1] // 3
    candidate = jnp.tanh(preact[:, :channels])
    forget = jax.nn.sigmoid(preact[:, channels : 2 * channels])
    output_gate = jax.nn.sigmoid(preact[:, 2 * channels :])
    decay = forget * keeping[:, None, :]
    _, cells = lax.associative_scan(combine, (decay, (1.0 - forget) * candidate), axis=2)
    return output_gate * cells


def adam_step(weights, first, second, grad, decay_rate):
    rate = (2.0 * D) ** (-0.5)
    first_new = 0.9 * first + 0.1 * grad
    second_new = 0.999 * second + 0.001 * grad * grad
    first_hat = first_new / (1.0 - 0.9**STEP)
    second_hat = second_new / (1.0 - 0.999**STEP)
    weights_new = weights - rate * (
        first_hat / (jnp.sqrt(second_hat) + 1e-08) + decay_rate * weights
    )
    return (weights_new, first_new, second_new)


def shards(
    inputs,
    resets,
    owners,
    kernel,
    kernel_first,
    kernel_second,
    bias_rows,
    bias_first,
    bias_second,
    cotangent,
):
    streams, local_width, length = inputs.shape
    slots_own, _, block_rows = kernel.shape
    block_count = owners.shape[0] - 3
    dp_size = lax.axis_size("dp")
    dp_index = lax.axis_index("dp")
    kernel_owner = owners[:block_count]
    bias_owner = owners[block_count:]
    kernel_slot = kernel_owner * slots_own + earlier_count(kernel_owner)
    bias_slot = bias_owner * 3 + earlier_count(bias_owner)
    all_kernel, all_bias = (
        lax.all_gather(kernel.astype(jnp.bfloat16), "dp", axis=0, tiled=True),
        lax.all_gather(bias_rows.astype(jnp.bfloat16), "dp", axis=0, tiled=True),
    )
    per_gate = block_count // 3
    double_width = per_gate * block_rows
    full_width = double_width // 2
    gate_cols = 3 * local_width
    arranged = (
        all_kernel[kernel_slot]
        .reshape(3, per_gate, local_width, block_rows)
        .transpose(0, 2, 1, 3)
        .reshape(gate_cols, double_width)
    )
    paired_t = jnp.concatenate([arranged[:, :full_width], arranged[:, full_width:]], axis=0)
    bias_vec = all_bias[bias_slot].astype(jnp.float32).reshape(gate_cols)
    rows = paired_t
    projected = jnp.einsum(
        "ok,skl->sol",
        rows,
        lax.all_gather(inputs, "mp", axis=1, tiled=True),
        preferred_element_type=jnp.float32,
    )
    preact = (
        projected[:, :gate_cols] + shift_later(projected[:, gate_cols:]) + bias_vec[None, :, None]
    )
    keeping = (1 - resets).astype(jnp.float32)
    result, pullback = jax.vjp(lambda values: pooled(values, keeping), preact)
    pre_grad = pullback(cotangent.astype(jnp.float32))[0].astype(jnp.bfloat16)
    joined = jnp.concatenate([pre_grad, shift_earlier(pre_grad)], axis=1)
    bias_grad = jnp.sum(pre_grad.astype(jnp.float32), axis=(0, 2)).reshape(3, local_width)
    pair_grad = jnp.einsum(
        "sol,skl->ok",
        joined,
        lax.all_gather(inputs, "mp", axis=1, tiled=True),
        preferred_element_type=jnp.float32,
    )
    rows = paired_t
    term_rows = lax.psum_scatter(
        jnp.einsum("ok,sol->ksl", rows, joined, preferred_element_type=jnp.float32),
        "mp",
        scatter_dimension=0,
        tiled=True,
    )
    input_grads = jnp.transpose(term_rows.astype(jnp.bfloat16), (1, 0, 2))
    block_grad = pair_grad.reshape(2, 3, local_width, full_width).transpose(1, 2, 0, 3)
    block_grad = (
        block_grad.reshape(3, local_width, per_gate, block_rows)
        .transpose(0, 2, 1, 3)
        .reshape(block_count, local_width, block_rows)
    )
    kernel_source, kernel_valid = slot_sources(kernel_slot, dp_size * slots_own)
    bias_source, bias_valid = slot_sources(bias_slot, dp_size * 3)
    own_kernel_valid = lax.dynamic_slice_in_dim(kernel_valid, dp_index * slots_own, slots_own)
    own_bias_valid = lax.dynamic_slice_in_dim(bias_valid, dp_index * 3, 3)
    total_kernel, total_bias = lax.psum((block_grad, bias_grad), "dp")
    own_kernel_source = lax.dynamic_slice_in_dim(kernel_source, dp_index * slots_own, slots_own)
    own_bias_source = lax.dynamic_slice_in_dim(bias_source, dp_index * 3, 3)
    own_kernel = total_kernel[own_kernel_source] * own_kernel_valid[:, None, None]
    own_bias = total_bias[own_bias_source] * own_bias_valid[:, None]
    squares = jnp.sum(own_kernel * own_kernel) + jnp.sum(own_bias * own_bias)
    grad_norm = jnp.sqrt(lax.psum(squares, ("dp", "mp")))
    factor = 1.0 / jnp.maximum(grad_norm, 1.0)
    kernel_w, kernel_m, kernel_v = adam_step(
        kernel, kernel_first, kernel_second, own_kernel * factor, 0.1
    )
    bias_w, bias_m, bias_v = adam_step(bias_rows, bias_first, bias_second, own_bias * factor, 0.0)
    kernel_mask = own_kernel_valid[:, None, None] > 0.5
    bias_mask = own_bias_valid[:, None] > 0.5
    return (
        result.astype(jnp.bfloat16),
        input_grads,
        jnp.where(kernel_mask, kernel_w, 0.0),
        jnp.where(kernel_mask, kernel_m, 0.0),
        jnp.where(kernel_mask, kernel_v, 0.0),
        jnp.where(bias_mask, bias_w, 0.0),
        jnp.where(bias_mask, bias_m, 0.0),
        jnp.where(bias_mask, bias_v, 0.0),
        grad_norm,
    )


def solution(mesh):
    placed = (
        P("dp", "mp", None),
        P("dp", None),
        P(),
        P("dp", "mp", None),
        P("dp", "mp", None),
        P("dp", "mp", None),
        P("dp", "mp"),
        P("dp", "mp"),
        P("dp", "mp"),
        P("dp", "mp", None),
    )
    return jax.shard_map(
        shards,
        mesh=mesh,
        in_specs=placed,
        out_specs=(
            P("dp", "mp", None),
            P("dp", "mp", None),
            P("dp", "mp", None),
            P("dp", "mp", None),
            P("dp", "mp", None),
            P("dp", "mp"),
            P("dp", "mp"),
            P("dp", "mp"),
            P(),
        ),
        check_vma=False,
    )
```

profile of v0, /device:TPU:0, one launch (start us, length us, event | category | flops | bytes accessed | tf_op | source)
XLA Modules:
  0.0 1835.0 jit_solution(1816470998600047845)
XLA Ops:
  13.4 9.6 all-gather
  25.2 125.8 %all-gather.4.cloned.1.call-done = bf16[96,288,256]{2,1,0:T(8,128)(2,1)} async-done(((bf16[24,288,256]{2,1,0:T(8,128)(2,1)}), bf16[96,288,256]{2,1,0:T(8,128)(2,1)}) %all-gather.4.cloned.1.call-update) | async-done | bytes 14155792 | tf_op jit(solution)/shard_map/all_gather | solution.py:80
  151.0 10.8 gather_fusion
  161.9 12.1 copy.43
  174.0 10.2 copy.65
  189.9 14.5 all-gather.6.cloned.1.call-done
  204.4 12.2 fusion.4
  220.1 24.4 %slice.350 = f32[1,288,511]{2,1,0:T(8,128)} slice(f32[1,288,1024]{2,1,0:T(8,128)} %get-tuple-element.47), slice={[0:1:1], [0:288:1], [2:1024:2]} | slice | bytes 1177344 | tf_op jit(solution)/shard_map/jvp()/slice | solution.py:42
  244.5 24.5 %slice.355 = f32[1,288,512]{2,1,0:T(8,128)} slice(f32[1,288,1024]{2,1,0:T(8,128)} %get-tuple-element.47), slice={[0:1:1], [0:288:1], [0:1023:2]} | slice | bytes 1179648 | tf_op jit(solution)/shard_map/jvp()/slice | solution.py:42
  269.0 24.5 %slice.351 = f32[1,288,512]{2,1,0:T(8,128)} slice(f32[1,288,1024]{2,1,0:T(8,128)} %get-tuple-element.47), slice={[0:1:1], [0:288:1], [1:1024:2]} | slice | bytes 1179648 | tf_op jit(solution)/shard_map/jvp()/slice | solution.py:42
  293.4 24.8 %slice.423 = f32[1,288,511]{2,1,0:T(8,128)} slice(f32[1,288,1024]{2,1,0:T(8,128)} %get-tuple-element.48), slice={[0:1:1], [0:288:1], [2:1024:2]} | slice | bytes 1177344 | tf_op jit(solution)/shard_map/jvp()/slice | solution.py:42
  318.3 24.5 %slice.353 = f32[1,288,512]{2,1,0:T(8,128)} slice(f32[1,288,1024]{2,1,0:T(8,128)} %get-tuple-element.48), slice={[0:1:1], [0:288:1], [1:1024:2]} | slice | bytes 1179648 | tf_op jit(solution)/shard_map/jvp()/slice | solution.py:42
  342.8 24.5 %slice.352 = f32[1,288,512]{2,1,0:T(8,128)} slice(f32[1,288,1024]{2,1,0:T(8,128)} %get-tuple-element.48), slice={[0:1:1], [0:288:1], [0:1023:2]} | slice | bytes 1179648 | tf_op jit(solution)/shard_map/jvp()/slice | solution.py:42
  370.1 13.0 slice.361
  383.1 13.2 slice.357
  396.3 13.0 slice.359
  409.3 13.0 slice.358
  430.9 6.7 slice.367
  437.6 6.5 slice.363
  450.6 6.5 slice.365
  457.1 6.5 slice.364
  566.6 13.1 slice.421
  579.8 13.0 slice.356
  673.0 7.2 pad.402
  680.2 7.2 pad.403
  689.3 12.3 pad.405
  704.7 12.3 pad.404
  722.1 24.4 %pad.406 = f32[1,288,1024]{2,1,0:T(8,128)} pad(f32[1,288,512]{2,1,0:T(8,128)} %pad_maximum_fusion.6, f32[]{:T(128)} %constant.26.clone.1), padding=0_0_0x0_0_0x0_1_1 | pad | bytes 1769476 | tf_op jit(solution)/shard_map/jvp()/pad | solution.py:42
  746.5 24.2 %pad.407 = f32[1,288,1024]{2,1,0:T(8,128)} pad(f32[1,288,512]{2,1,0:T(8,128)} %add.413, f32[]{:T(128)} %constant.26.clone.1), padding=0_0_0x0_0_0x1_0_1 | pad | bytes 1769476 | tf_op jit(solution)/shard_map/jvp()/pad | solution.py:42
  776.1 24.5 %slice.425 = f32[1,288,512]{2,1,0:T(8,128)} slice(f32[1,288,1023]{2,1,0:T(8,128)} %get-tuple-element.51), slice={[0:1:1], [0:288:1], [0:1023:2]} | slice | bytes 1179648 | tf_op jit(solution)/shard_map/transpose(jvp())/slice | solution.py:42
  800.5 24.5 %slice.424 = f32[1,288,512]{2,1,0:T(8,128)} slice(f32[1,288,1023]{2,1,0:T(8,128)} %get-tuple-element.50), slice={[0:1:1], [0:288:1], [0:1023:2]} | slice | bytes 1179648 | tf_op jit(solution)/shard_map/transpose(jvp())/slice | solution.py:42
  829.3 13.0 slice.427
  842.3 13.2 slice.426
  859.6 6.5 slice.429
  866.1 6.5 slice.428
  1064.5 7.2 pad.470
  1071.7 7.2 pad.499
  1078.9 7.2 pad.478
  1086.1 7.3 pad.498
  1093.4 7.2 pad.471
  1100.6 7.2 pad.421
  1112.1 12.4 pad.472
  1126.1 12.3 pad.501
  1138.3 12.3 pad.477
  1150.6 12.3 pad.500
  1163.0 12.4 pad.473
  1175.4 12.3 pad.416
  1193.7 24.4 %pad.474 = f32[1,288,1024]{2,1,0:T(8,128)} pad(f32[1,288,512]{2,1,0:T(8,128)} %copy-done.1, f32[]{:T(128)} %constant.26.clone.1), padding=0_0_0x0_0_0x1_0_1 | pad | bytes 1769476 | tf_op jit(solution)/shard_map/transpose(jvp())/pad | solution.py:42
  1219.7 24.3 %pad.503 = f32[1,288,1024]{2,1,0:T(8,128)} pad(f32[1,288,512]{2,1,0:T(8,128)} %get-tuple-element.49, f32[]{:T(128)} %constant.26.clone.1), padding=0_0_0x0_0_0x0_1_1 | pad | bytes 1769476 | tf_op jit(solution)/shard_map/transpose(jvp())/pad | solution.py:42
  1244.0 24.4 %pad.476 = f32[1,288,1024]{2,1,0:T(8,128)} pad(f32[1,288,511]{2,1,0:T(8,128)} %get-tuple-element.55, f32[]{:T(128)} %constant.26.clone.1), padding=0_0_0x0_0_0x2_1_1 | pad | bytes 1768324 | tf_op jit(solution)/shard_map/transpose(jvp())/pad | solution.py:42
  1268.4 24.2 %pad.502 = f32[1,288,1024]{2,1,0:T(8,128)} pad(f32[1,288,512]{2,1,0:T(8,128)} %get-tuple-element.17, f32[]{:T(128)} %constant.26.clone.1), padding=0_0_0x0_0_0x1_0_1 | pad | bytes 1769476 | tf_op jit(solution)/shard_map/transpose(jvp())/pad | solution.py:42
  1292.6 24.5 %pad.475 = f32[1,288,1024]{2,1,0:T(8,128)} pad(f32[1,288,512]{2,1,0:T(8,128)} %mul.485, f32[]{:T(128)} %constant.26.clone.1), padding=0_0_0x0_0_0x0_1_1 | pad | bytes 1769476 | tf_op jit(solution)/shard_map/transpose(jvp())/pad | solution.py:42
  1317.1 24.1 %pad.411 = f32[1,288,1024]{2,1,0:T(8,128)} pad(f32[1,288,511]{2,1,0:T(8,128)} %get-tuple-element.53, f32[]{:T(128)} %constant.26.clone.1), padding=0_0_0x0_0_0x2_1_1 | pad | bytes 1768324 | tf_op jit(solution)/shard_map/transpose(jvp())/pad | solution.py:42
  1349.0 11.4 convolution_bitcast_fusion
  1360.4 27.9 %copy.56 = f32[3,288,2,2304]{3,2,1,0:T(2,128)} copy(f32[3,288,2,2304]{3,1,0,2:T(8,128)} %convolution_bitcast_fusion) | data formatting | bytes 31850496 | tf_op jit(solution)/shard_map/transpose | solution.py:124
  1388.3 22.5 %reshape.74 = f32[3,288,18,256]{3,2,1,0:T(8,128)} reshape(f32[3,288,2,2304]{3,2,1,0:T(2,128)} %copy.56) | data formatting | bytes 31850496 | tf_op jit(solution)/shard_map/reshape | solution.py:126
  1410.8 16.3 copy.57
  1427.2 13.3 convolution_bitcast_fusion.1
  1441.9 10.4 psum.22
  1453.6 266.9 %all-reduce.102.cloned.1.call-done = f32[54,288,256]{2,1,0:T(8,128)} async-done(((f32[54,288,256]{2,1,0:T(8,128)}), f32[54,288,256]{2,1,0:T(8,128)}) %all-reduce.102.cloned.1.call-update) | async-done | bytes 15925264 | tf_op jit(solution)/shard_map/psum | solution.py:134
  1720.5 9.5 gather_fusion.2
  1737.2 42.6 %psum.23 = f32[]{:T(128)} all-reduce(f32[]{:T(128)S(6)} %add.421), channel_id=1, replica_groups=mesh['dp'=4,'mp'=8] {'dp','mp'}, use_global_device_ids=true, to_apply=%region_12.13 | all-reduce | flops 1 | bytes 8 | tf_op jit(solution)/shard_map/psum | solution.py:140
  1781.2 18.2 broadcast_select_fusion
  1799.4 25.3 %reduce-scatter.2.cloned.1.call-done = f32[288,1,1024]{2,0,1:T(8,128)} async-done(((f32[2304,1,1024]{2,0,1:T(8,128)}), f32[288,1,1024]{2,0,1:T(8,128)}) %reduce-scatter.2.cloned.1.call-update) | async-done | bytes 1179664 | tf_op jit(solution)/shard_map/reduce_scatter | solution.py:117
  (305 shorter events, 466.9 us)
Async XLA Ops:
  7.2 143.9 %all-gather.4.cloned.1.call-start = ((), (), s32[]{:S(2)}) async-start(), calls=%async_computation.1 | async-start | bytes 17694720 | tf_op jit(solution)/shard_map/all_gather | solution.py:80
  12.5 0.8 copy-start.18
  12.5 10.5 copy-start.23
  12.5 12.7 copy-start.22
  12.5 191.9 %all-gather.6.cloned.1.call-start = ((), (), s32[]{:S(2)}) async-start(), calls=%async_computation.2 | async-start | bytes 5308416 | tf_op jit(solution)/shard_map/all_gather | solution.py:99
  13.3 1707.2 %all-reduce.102.cloned.1.call-start = ((), (), s32[]{:S(2)}) async-start(), calls=%async_computation.4 | async-start | bytes 31850496 | tf_op jit(solution)/shard_map/psum | solution.py:134
  542.4 0.7 copy-start.9
  544.2 2.1 copy-start.6
  544.2 2.1 copy-start.7
  717.0 4.0 copy-start.17
  825.0 3.0 copy-start.8
  911.1 17.0 copy-start.24
  923.8 6.9 copy-start.4
  930.0 0.7 copy-start.10
  943.2 0.6 copy-start.11
  962.2 0.6 copy-start.12
  982.2 0.7 copy-start.13
  1003.9 0.7 copy-start.14
  1029.4 0.7 copy-start.15
  1062.2 0.7 copy-start.16
  1107.8 3.5 copy-start.2
  1110.6 0.7 copy-start.5
  1187.7 5.1 copy-start
  1191.9 0.8 copy-start.1
  1345.4 1.3 copy-start.3
  1346.7 2.2 slice-start
  1347.0 2.1 slice-start.1
  1427.1 397.6 %reduce-scatter.2.cloned.1.call-start = ((), (), s32[]{:S(2)}) async-start(), calls=%async_computation.3 | async-start | bytes 10616832 | tf_op jit(solution)/shard_map/reduce_scatter | solution.py:117
  1440.4 0.7 copy-start.26
  1440.4 0.8 copy-start.25
  1730.0 50.5 %copy-start.19 = (f32[3,288]{1,0:T(4,128)S(1)}, f32[3,288]{1,0:T(4,128)}, u32[]{:S(2)}) copy-start(f32[3,288]{1,0:T(4,128)} %param.16) | copy-start | bytes 10372
  1730.0 50.5 %copy-start.20 = (f32[3,288]{1,0:T(4,128)S(1)}, f32[3,288]{1,0:T(4,128)}, u32[]{:S(2)}) copy-start(f32[3,288]{1,0:T(4,128)} %param.18) | copy-start | bytes 10372
  1730.0 50.5 %copy-start.21 = (f32[3,288]{1,0:T(4,128)S(1)}, f32[3,288]{1,0:T(4,128)}, u32[]{:S(2)}) copy-start(f32[3,288]{1,0:T(4,128)} %param.17) | copy-start | bytes 10372
Sparse Core Ops, SparseCore 0:
  12.7 138.3 all-gather.3
  152.7 51.6 all-gather.5
  1427.3 293.2 all-reduce.101
  1722.8 101.9 reduce-scatter.1
where the time goes:
time: 1850 us; the launch traced here: 1840 us
  local copies, waits for them, and re-layouts  1120 us (61%)
  waiting for transfers between devices  433 us (23%)
  other arithmetic  167 us (9%)
  blocking collectives  62.6 us (3%)
  matrix products  36.8 us (2%)
    pad x79, local copies, waits for them, and re-layouts, pooled(): lax.associative_scan(combine, (decay, (1.0 - forget) * candidate), axis=2)  502 us
    slice x73, local copies, waits for them, and re-layouts, pooled(): lax.associative_scan(combine, (decay, (1.0 - forget) * candidate), axis=2)  471 us
    psum x1, waiting for transfers between devices, shards(): total_kernel, total_bias = lax.psum((block_grad, bias_grad), 'dp')  267 us
    all_gather x1, waiting for transfers between devices, shards(): lax.all_gather(kernel.astype(jnp.bfloat16), 'dp', axis=0, tiled=True)  126 us
    psum x1, blocking collectives, shards(): grad_norm = jnp.sqrt(lax.psum(squares, ('dp', 'mp')))  42.6 us
  transfers between devices with their start and end apart: 4, of which 4 were waited for; matrix products, arithmetic and copies ran while one was open for 5% of the time, Pallas kernels for 0%

commit v1 on v0

--- a/solution.py
+++ b/solution.py
@@ -1,6 +1,8 @@
 import jax
 import jax.numpy as jnp
 from jax import lax
+from jax.experimental import pallas as pl
+from jax.experimental.pallas import tpu as pltpu
 from jax.sharding import PartitionSpec as P
 
 D = 2304
@@ -158,6 +160,824 @@
     )
 
 
+MESH_ID = pl.DeviceIdType.MESH
+LANES = 128
+CHUNKS = 4
+
+
+def place():
+    dp, mp = lax.axis_index("dp"), lax.axis_index("mp")
+    return dp // 2, lax.rem(dp, 2), mp // 2, lax.rem(mp, 2)
+
+
+def partners(y, x, z, c):
+    dp, mp = y * 2 + x, z * 2 + c
+    return {
+        "x": (y * 2 + 1 - x, mp),
+        "y": ((1 - y) * 2 + x, mp),
+        "xy": ((1 - y) * 2 + 1 - x, mp),
+        "core": (dp, z * 2 + 1 - c),
+        "up": (dp, mp + 2),
+        "down": (dp, mp - 2),
+    }
+
+
+def greet(who, names, z, depth):
+    barrier = pltpu.get_barrier_semaphore()
+    for name in names:
+        pl.semaphore_signal(barrier, inc=1, device_id=who[name], device_id_type=MESH_ID)
+
+    @pl.when(z < depth - 1)
+    def _():
+        pl.semaphore_signal(barrier, inc=1, device_id=who["up"], device_id_type=MESH_ID)
+
+    @pl.when(z > 0)
+    def _():
+        pl.semaphore_signal(barrier, inc=1, device_id=who["down"], device_id_type=MESH_ID)
+
+    both = (z < depth - 1).astype(jnp.int32) + (z > 0).astype(jnp.int32)
+    pl.semaphore_wait(barrier, len(names) + both)
+
+
+class Sends:
+    def __init__(self, sems):
+        self.sems, self.number, self.made = sems, 0, []
+
+    def start(self, src, dst, recv, device, when=None):
+        slot = self.number
+        self.number += 1
+
+        def build():
+            return pltpu.make_async_remote_copy(
+                src_ref=src(),
+                dst_ref=dst(),
+                send_sem=self.sems.at[slot],
+                recv_sem=recv,
+                device_id=device,
+                device_id_type=MESH_ID,
+            )
+
+        def go():
+            build().start()
+
+        if when is None:
+            go()
+        else:
+            pl.when(when)(go)
+        self.made.append((build, when))
+
+    def finish(self):
+        for build, when in self.made:
+            if when is None:
+                build().wait_send()
+            else:
+                pl.when(when)(lambda build=build: build().wait_send())
+
+
+def landed(ref, sem, device):
+    pltpu.make_async_remote_copy(
+        src_ref=ref, dst_ref=ref, send_sem=sem, recv_sem=sem, device_id=device, device_id_type=MESH_ID
+    ).wait_recv()
+
+
+def gather_kernel(
+    w_ref, x_ref, cot_ref, res_ref, bias_ref,
+    wg, xg, cg, rg, bg,
+    wf, wb, load_sem, own_sem, send_sem, w_sem, x_sem, c_sem, r_sem, b_sem,
+):
+    y, x, z, c = place()
+    dp, mp = y * 2 + x, z * 2 + c
+    who = partners(y, x, z, c)
+    slots, width, _ = w_ref.shape
+    half = width // 2
+    depth = xg.shape[1] // width // 2
+    rows = slots // CHUNKS
+
+    def part(index):
+        return pl.ds(pl.multiple_of(index * half, half), half)
+
+    def rows_of(index):
+        return pl.ds(pl.multiple_of(index * width, width), width)
+
+    loads = [
+        pltpu.make_async_copy(
+            w_ref.at[pl.ds(i * rows, rows)], wf.at[pl.ds(i * rows, rows)], load_sem.at[i]
+        )
+        for i in range(CHUNKS)
+    ]
+    for load in loads:
+        load.start()
+    own = [
+        pltpu.make_async_copy(x_ref, xg.at[x, rows_of(mp)], own_sem.at[0]),
+        pltpu.make_async_copy(cot_ref.at[part(x)], cg.at[x], own_sem.at[1]),
+        pltpu.make_async_copy(res_ref, rg.at[x], own_sem.at[2]),
+        pltpu.make_async_copy(bias_ref, bg.at[dp], own_sem.at[3]),
+    ]
+    for copy in own:
+        copy.start()
+    greet(who, ("x", "y", "xy", "core"), z, depth)
+    sends = Sends(send_sem)
+
+    def spread(stream, place_z, src, up, down, core=True):
+        number = place_z * 2 + c
+
+        def dst():
+            return xg.at[stream, rows_of(number)]
+
+        recv = x_sem.at[stream, number]
+        if up is not False:
+            sends.start(src, dst, recv, who["up"], up)
+        if down is not False:
+            sends.start(src, dst, recv, who["down"], down)
+        sends.start(src, dst, recv, who["core"], core)
+
+    spread(x, z, lambda: x_ref, z < depth - 1, z > 0, None)
+    sends.start(lambda: x_ref, lambda: xg.at[x, rows_of(mp)], x_sem.at[x, mp], who["x"])
+    for name in ("x", "y", "xy"):
+        sends.start(lambda: bias_ref, lambda: bg.at[dp], b_sem.at[dp], who[name])
+    sends.start(lambda: res_ref, lambda: rg.at[x], r_sem, who["x"])
+    for i in range(CHUNKS):
+        loads[i].wait()
+
+        def cast(r, _, i=i):
+            wb[i * rows + r] = wf[i * rows + r].astype(jnp.bfloat16)
+            return 0
+
+        lax.fori_loop(0, rows, cast, 0)
+
+        def dst(i=i):
+            return wg.at[pl.ds(dp * slots + i * rows, rows)]
+
+        sends.start(lambda i=i: wb.at[pl.ds(i * rows, rows), part(x)], dst, w_sem.at[dp, i], who["y"])
+        sends.start(
+            lambda i=i: wb.at[pl.ds(i * rows, rows), part(1 - x)], dst, w_sem.at[dp, i], who["x"]
+        )
+        copy = pltpu.make_async_copy(wb.at[pl.ds(i * rows, rows), part(x)], dst(), own_sem.at[4 + i])
+        copy.start()
+        own.append(copy)
+    sends.start(lambda: cot_ref.at[part(1 - x)], lambda: cg.at[x], c_sem, who["x"])
+
+    def along_z(stream, d):
+        @pl.when(z >= d)
+        def _():
+            landed(xg.at[stream, rows_of((z - d) * 2 + c)], x_sem.at[stream, (z - d) * 2 + c], who["down"])
+
+        src = lambda: xg.at[stream, rows_of((z - d) * 2 + c)]
+        spread(stream, z - d, src, (z >= d) & (z < depth - 1), False, z >= d)
+
+        @pl.when(z + d < depth)
+        def _():
+            landed(xg.at[stream, rows_of((z + d) * 2 + c)], x_sem.at[stream, (z + d) * 2 + c], who["up"])
+
+        src = lambda: xg.at[stream, rows_of((z + d) * 2 + c)]
+        spread(stream, z + d, src, False, (z + d < depth) & (z > 0), z + d < depth)
+
+    def pass_on(i):
+        def ref():
+            return wg.at[pl.ds((y * 2 + 1 - x) * slots + i * rows, rows)]
+
+        sem = w_sem.at[y * 2 + 1 - x, i]
+        landed(ref(), sem, who["x"])
+        sends.start(ref, ref, sem, who["y"])
+
+    def other_stream():
+        ref = lambda: xg.at[1 - x, rows_of(mp)]
+        landed(ref(), x_sem.at[1 - x, mp], who["x"])
+        spread(1 - x, z, ref, z < depth - 1, z > 0, None)
+
+    steps = [lambda d=d: along_z(x, d) for d in range(1, depth)]
+    steps += [lambda d=d: along_z(1 - x, d) for d in range(1, depth)]
+    steps.insert(1, other_stream)
+    after = [2, 4, 5, 7]
+    for i in range(CHUNKS):
+        steps.insert(min(after[i] + 1, len(steps)), lambda i=i: pass_on(i))
+    for step in steps:
+        step()
+    for source in ((1 - y) * 2 + x, (1 - y) * 2 + 1 - x):
+        for i in range(CHUNKS):
+            landed(wg.at[pl.ds(source * slots + i * rows, rows)], w_sem.at[source, i], who["y"])
+    for stream in (x, 1 - x):
+        for k in range(depth):
+            number = k * 2 + 1 - c
+            landed(xg.at[stream, rows_of(number)], x_sem.at[stream, number], who["core"])
+    landed(cg.at[1 - x], c_sem, who["x"])
+    landed(rg.at[1 - x], r_sem, who["x"])
+    for source in (y * 2 + 1 - x, (1 - y) * 2 + x, (1 - y) * 2 + 1 - x):
+        landed(bg.at[source], b_sem.at[source], who["x"])
+    for copy in own:
+        copy.wait()
+    sends.finish()
+
+
+def slot_table(owners, slot, count, blocks, slots):
+    for d in range(4):
+        count[d] = 0
+
+    def one(i, _):
+        owner = owners[i]
+        slot[i] = owner * slots + count[owner]
+        count[owner] = count[owner] + 1
+        return 0
+
+    lax.fori_loop(0, blocks, one, 0)
+
+
+def bias_rank(owners, blocks, g):
+    owner = owners[blocks + g]
+    rank = jnp.int32(0)
+    for h in range(g):
+        rank += (owners[blocks + h] == owner).astype(jnp.int32)
+    return owner, rank
+
+
+def scan_later(a, b, length):
+    d = 1
+    while d < length:
+        b = b + a * pltpu.roll(b, d, 1)
+        if 2 * d < length:
+            a = a * pltpu.roll(a, d, 1)
+        d *= 2
+    return b
+
+
+def scan_earlier(a, b, length):
+    d = 1
+    while d < length:
+        b = b + a * pltpu.roll(b, length - d, 1)
+        if 2 * d < length:
+            a = a * pltpu.roll(a, length - d, 1)
+        d *= 2
+    return b
+
+
+def layer_kernel(
+    owners, wg, xg, cg, rg, bg,
+    h_out, gs, j_out, w_out, bgrad,
+    slot, count, wv, xv, p, joined, gb, bcol, w_sem, x_sem, o_sem,
+):
+    half, block_rows = wg.shape[1], wg.shape[2]
+    slots = wg.shape[0] // 4
+    streams, full, length = xg.shape
+    per_half = full // block_rows
+    blocks = 6 * per_half
+    x = lax.rem(lax.axis_index("dp"), 2)
+    x_loads = [pltpu.make_async_copy(xg.at[s], xv.at[s], x_sem.at[s]) for s in range(2)]
+    slot_table(owners, slot, count, blocks, slots)
+    for h in range(2):
+        for g in range(3):
+
+            def fetch(k, _, h=h, g=g):
+                pltpu.make_async_copy(
+                    wg.at[slot[g * 2 * per_half + h * per_half + k]],
+                    wv.at[
+                        pl.ds((h * 3 + g) * half, half),
+                        pl.ds(pl.multiple_of(k * block_rows, block_rows), block_rows),
+                    ],
+                    w_sem,
+                ).start()
+                return 0
+
+            lax.fori_loop(0, per_half, fetch, 0)
+    for load in x_loads:
+        load.start()
+    lane_of = lax.broadcasted_iota(jnp.int32, (half, 2 * half), 1)
+    row_of = lax.broadcasted_iota(jnp.int32, (half, 2 * half), 0)
+    diagonal = lane_of == row_of + x * half
+    for g in range(3):
+        owner, rank = bias_rank(owners, blocks, g)
+        held = bg[owner]
+        line = jnp.zeros((1, 2 * half), jnp.float32)
+        for r in range(3):
+            line = jnp.where(rank == r, held[r : r + 1], line)
+        line = line.astype(jnp.bfloat16).astype(jnp.float32)
+        column = jnp.sum(jnp.where(diagonal, line, 0.0), axis=1, keepdims=True)
+        bcol[pl.ds(g * half, half), :] = jnp.broadcast_to(column, (half, LANES))
+    bgrad[...] = jnp.zeros_like(bgrad)
+    pltpu.make_async_copy(wv, wv, w_sem).wait()
+    w_back = pltpu.make_async_copy(wv, w_out, o_sem.at[0])
+    w_back.start()
+    tile = 16
+    moment = lax.broadcasted_iota(jnp.int32, (tile, length), 1)
+    lane = lax.broadcasted_iota(jnp.int32, (tile, LANES), 1)
+    for s in range(2):
+        x_loads[s].wait()
+
+        def project(n, _, s=s):
+            columns = pl.ds(pl.multiple_of(n * 256, 256), 256)
+            p[:, columns] = jnp.dot(wv[...], xv[s, :, columns], preferred_element_type=jnp.float32)
+            return 0
+
+        lax.fori_loop(0, length // 256, project, 0)
+        keep = 1.0 - jnp.broadcast_to(rg[s], (tile, length)).astype(jnp.float32)
+        keep = jnp.where(moment == 0, 0.0, keep)
+
+        def gates(i, _, s=s, keep=keep):
+            base = pl.multiple_of(i * tile, tile)
+
+            def pre(g):
+                now = p[pl.ds(g * half + base, tile), :]
+                before = pltpu.roll(p[pl.ds((3 + g) * half + base, tile), :], 1, 1)
+                return (
+                    now
+                    + jnp.where(moment == 0, 0.0, before)
+                    + bcol[pl.ds(g * half + base, tile), :][:, :1]
+                )
+
+            cand = jnp.tanh(pre(0))
+            forget = jax.nn.sigmoid(pre(1))
+            gate = jax.nn.sigmoid(pre(2))
+            decay = forget * keep
+            cells = scan_later(decay, (1.0 - forget) * cand, length)
+            h_out[s, pl.ds(base, tile), :] = (gate * cells).astype(jnp.bfloat16)
+            dh = cg[s, pl.ds(base, tile), :].astype(jnp.float32)
+            dc = scan_earlier(pltpu.roll(decay, length - 1, 1), dh * gate, length)
+            d_gate = dh * cells * gate * (1.0 - gate)
+            d_cand = dc * (1.0 - forget) * (1.0 - cand * cand)
+            d_forget = (
+                dc * (keep * pltpu.roll(cells, 1, 1) - cand) * forget * (1.0 - forget)
+            )
+            total = bgrad[pl.ds(base, tile), :]
+            for g, value in enumerate((d_cand, d_forget, d_gate)):
+                value = value.astype(jnp.bfloat16)
+                wide = value.astype(jnp.float32)
+                joined[pl.ds(g * half + base, tile), pl.ds(s * length, length)] = value
+                ahead = jnp.where(moment == length - 1, 0.0, pltpu.roll(wide, length - 1, 1))
+                joined[pl.ds((3 + g) * half + base, tile), pl.ds(s * length, length)] = ahead.astype(
+                    jnp.bfloat16
+                )
+                total += jnp.where(lane == g, jnp.sum(wide, axis=1, keepdims=True), 0.0)
+            bgrad[pl.ds(base, tile), :] = total
+            return 0
+
+        lax.fori_loop(0, half // tile, gates, 0)
+    j_back = pltpu.make_async_copy(joined, j_out, o_sem.at[1])
+    j_back.start()
+
+    def weight_grad(k, _):
+        rows = pl.ds(pl.multiple_of(k * block_rows, block_rows), block_rows)
+        both = (((1,), (1,)), ((), ()))
+        total = lax.dot_general(
+            joined[:, pl.ds(0, length)], xv[0, rows, :], both, preferred_element_type=jnp.float32
+        )
+        total += lax.dot_general(
+            joined[:, pl.ds(length, length)], xv[1, rows, :], both, preferred_element_type=jnp.float32
+        )
+        gb[k] = total.astype(jnp.bfloat16)
+        for h in range(2):
+            for g in range(3):
+                pltpu.make_async_copy(
+                    gb.at[k, pl.ds((h * 3 + g) * half, half)],
+                    gs.at[slot[g * 2 * per_half + h * per_half + k]],
+                    w_sem,
+                ).start()
+        return 0
+
+    lax.fori_loop(0, per_half, weight_grad, 0)
+    pltpu.make_async_copy(gb, gb, w_sem).wait()
+    w_back.wait()
+    j_back.wait()
+
+
+def reduce_kernel(
+    owners, gs, w_hbm, j_hbm, h_in, bgrad,
+    gt, h_out, ig_out, bt, norm,
+    wv, jv, ig, up_got, down_got, core_got, x_got, y_got, y_own, x_give, b_got, squares, s_got,
+    load_sem, own_sem, send_sem, y_sem, x_sem, core_sem, up_sem, down_sem, ix_sem, h_sem, b_sem, s_sem,
+):
+    y, x, z, c = place()
+    who = partners(y, x, z, c)
+    slots, width, block_rows = gt.shape
+    half = width // 2
+    length = h_out.shape[1]
+    full = w_hbm.shape[1]
+    depth = full // width // 2
+    rows = slots // CHUNKS
+    blocks = 6 * (full // block_rows)
+    tile = 16
+
+    def part(index):
+        return pl.ds(pl.multiple_of(index * half, half), half)
+
+    def rows_of(place_z, core):
+        return pl.ds(pl.multiple_of((place_z * 2 + core) * width, width), width)
+
+    loads = [
+        pltpu.make_async_copy(w_hbm, wv, load_sem.at[0]),
+        pltpu.make_async_copy(j_hbm, jv, load_sem.at[1]),
+    ]
+    for load in loads:
+        load.start()
+    owner_x = (1 - x, x)
+    own_loads = []
+    for q in range(2):
+        copy = pltpu.make_async_copy(
+            gs.at[pl.ds((y * 2 + owner_x[q]) * slots, slots)], y_own.at[q], load_sem.at[2 + q]
+        )
+        copy.start()
+        own_loads.append(copy)
+    h_own = pltpu.make_async_copy(h_in.at[x], h_out.at[part(x)], own_sem.at[0])
+    h_own.start()
+    greet_extra = jnp.bitwise_xor(z, 2) * 2 + c
+    barrier = pltpu.get_barrier_semaphore()
+    flip_near = (y * 2 + x, jnp.bitwise_xor(z, 1) * 2 + c)
+    flip_far = (y * 2 + x, greet_extra)
+    pl.semaphore_signal(barrier, inc=1, device_id=flip_near, device_id_type=MESH_ID)
+    pl.semaphore_signal(barrier, inc=1, device_id=flip_far, device_id_type=MESH_ID)
+    for name in ("x", "y", "core"):
+        pl.semaphore_signal(barrier, inc=1, device_id=who[name], device_id_type=MESH_ID)
+
+    @pl.when(z < depth - 1)
+    def _():
+        pl.semaphore_signal(barrier, inc=1, device_id=who["up"], device_id_type=MESH_ID)
+
+    @pl.when(z > 0)
+    def _():
+        pl.semaphore_signal(barrier, inc=1, device_id=who["down"], device_id_type=MESH_ID)
+
+    both = (z < depth - 1).astype(jnp.int32) + (z > 0).astype(jnp.int32)
+    pl.semaphore_wait(barrier, 5 + both)
+
+    sends = Sends(send_sem)
+    sends.start(lambda: bgrad, lambda: b_got.at[0], b_sem.at[0], who["y"])
+    for q in range(2):
+        for i in range(CHUNKS):
+            sends.start(
+                lambda q=q, i=i: gs.at[
+                    pl.ds(((1 - y) * 2 + owner_x[q]) * slots + i * rows, rows)
+                ],
+                lambda q=q, i=i: y_got.at[q, pl.ds(i * rows, rows)],
+                y_sem.at[q, i],
+                who["y"],
+            )
+    sends.start(lambda: h_in.at[1 - x], lambda: h_out.at[part(x)], h_sem, who["x"])
+    for load in loads:
+        load.wait()
+    streams = (1 - x, x)
+    for q in range(2):
+
+        def input_grad(k, _, q=q):
+            columns = pl.ds(pl.multiple_of(k * 256, 256), 256)
+            lanes = pl.ds(pl.multiple_of(streams[q] * length, length), length)
+            ig[q, columns, :] = lax.dot_general(
+                wv[:, columns],
+                jv[:, lanes],
+                (((0,), (0,)), ((), ())),
+                preferred_element_type=jnp.float32,
+            ).astype(jnp.bfloat16)
+            return 0
+
+        lax.fori_loop(0, full // 256, input_grad, 0)
+        for k in range(depth):
+            sends.start(
+                lambda q=q, k=k: ig.at[q, rows_of(k, 1 - c)],
+                lambda q=q, k=k: core_got.at[q, k],
+                core_sem.at[q, k],
+                who["core"],
+            )
+
+    def add_tiles(dst, refs):
+        def one(i, _):
+            at = pl.ds(pl.multiple_of(i * tile, tile), tile)
+            total = refs[0][at, :].astype(jnp.float32)
+            for ref in refs[1:]:
+                total += ref[at, :].astype(jnp.float32)
+            dst[at, :] = total.astype(jnp.bfloat16)
+            return 0
+
+        lax.fori_loop(0, width // tile, one, 0)
+
+    def chip_sum(q, k):
+        landed(core_got.at[q, k], core_sem.at[q, k], who["core"])
+        mine = ig.at[q, rows_of(k, c)]
+        add_tiles(mine, (mine, core_got.at[q, k]))
+
+    def z_step(q, k):
+        far = depth - 1 - k
+
+        @pl.when((z > 0) & (z < far))
+        def _():
+            mine = ig.at[q, rows_of(far, c)]
+            landed(up_got.at[q, far], up_sem.at[q, far], who["down"])
+            add_tiles(mine, (mine, up_got.at[q, far]))
+
+        sends.start(
+            lambda: ig.at[q, rows_of(far, c)],
+            lambda: up_got.at[q, far],
+            up_sem.at[q, far],
+            who["up"],
+            z < far,
+        )
+
+        @pl.when((z < depth - 1) & (z > k))
+        def _():
+            mine = ig.at[q, rows_of(k, c)]
+            landed(down_got.at[q, k], down_sem.at[q, k], who["up"])
+            add_tiles(mine, (mine, down_got.at[q, k]))
+
+        sends.start(
+            lambda: ig.at[q, rows_of(k, c)],
+            lambda: down_got.at[q, k],
+            down_sem.at[q, k],
+            who["down"],
+            z > k,
+        )
+
+    def z_last(q):
+        mine = ig.at[q, rows_of(z, c)]
+
+        @pl.when(z > 0)
+        def _():
+            landed(up_got.at[q, z], up_sem.at[q, z], who["down"])
+            add_tiles(mine, (mine, up_got.at[q, z]))
+
+        @pl.when(z < depth - 1)
+        def _():
+            landed(down_got.at[q, z], down_sem.at[q, z], who["up"])
+            add_tiles(mine, (mine, down_got.at[q, z]))
+
+        if q == 0:
+            sends.start(lambda: mine, lambda: x_got, ix_sem, who["x"])
+
+    squares[...] = jnp.zeros_like(squares)
+    owned = []
+    for q in range(2):
+        number = jnp.int32(0)
+        for j in range(blocks):
+            number += (owners[j] == y * 2 + owner_x[q]).astype(jnp.int32)
+        owned.append(number)
+
+    def own_chunk(q, i):
+        if i == 0:
+            own_loads[q].wait()
+        landed(y_got.at[q, pl.ds(i * rows, rows)], y_sem.at[q, i], who["y"])
+
+        def one(r, _):
+            valid = jnp.broadcast_to(i * rows + r < owned[q], (half, block_rows))
+            total = y_own[q, i * rows + r].astype(jnp.float32) + y_got[q, i * rows + r].astype(
+                jnp.float32
+            )
+            total = jnp.where(valid, total, 0.0)
+            x_give[q, i * rows + r] = total.astype(jnp.bfloat16)
+            squares[...] += jnp.sum((total * total).reshape(half // 8, 8, block_rows), axis=0)
+            return 0
+
+        lax.fori_loop(0, rows, one, 0)
+        if q == 0:
+            sends.start(
+                lambda: x_give.at[0, pl.ds(i * rows, rows)],
+                lambda: gt.at[pl.ds(i * rows, rows), part(x)],
+                x_sem.at[i],
+                who["x"],
+            )
+        else:
+            copy = pltpu.make_async_copy(
+                x_give.at[1, pl.ds(i * rows, rows)],
+                gt.at[pl.ds(i * rows, rows), part(x)],
+                own_sem.at[1 + i],
+            )
+            copy.start()
+            own_copies.append(copy)
+
+    own_copies = [h_own]
+
+    def bias_sum():
+        landed(b_got.at[0], b_sem.at[0], who["y"])
+        total = bgrad[...] + b_got[0]
+        b_got[1] = total
+        bt[x] = total
+        sends.start(lambda: b_got.at[1], lambda: bt.at[x], b_sem.at[1], who["x"])
+        counted = jnp.broadcast_to(y == 0, (half, LANES))
+        each = jnp.where(counted, total * total, 0.0)
+        squares[:, pl.ds(0, LANES)] += jnp.sum(each.reshape(half // 8, 8, LANES), axis=0)
+
+    bias_sum()
+    for k in range(depth):
+        chip_sum(0, k)
+    z_step(0, 0)
+    own_chunk(0, 0)
+    for k in range(depth):
+        chip_sum(1, k)
+    z_step(0, 1)
+    z_step(1, 0)
+    own_chunk(0, 1)
+    z_step(0, 2)
+    z_step(1, 1)
+    own_chunk(0, 2)
+    z_last(0)
+    own_chunk(0, 3)
+    z_step(1, 2)
+    own_chunk(1, 0)
+    z_last(1)
+    own_chunk(1, 1)
+    own_chunk(1, 2)
+    landed(x_got, ix_sem, who["x"])
+    mine = ig.at[1, rows_of(z, c)]
+    add_tiles(mine, (mine, x_got))
+    copy = pltpu.make_async_copy(mine, ig_out, own_sem.at[1 + CHUNKS])
+    copy.start()
+    own_copies.append(copy)
+    own_chunk(1, 3)
+    total = squares[:, pl.ds(0, LANES)] + squares[:, pl.ds(LANES, LANES)]
+    for step, device in enumerate((who["core"], flip_near, flip_far, who["x"], who["y"])):
+        s_got[0, step] = total
+        sends.start(
+            lambda step=step: s_got.at[0, step],
+            lambda step=step: s_got.at[1, step],
+            s_sem.at[step],
+            device,
+        )
+        landed(s_got.at[1, step], s_sem.at[step], device)
+        total = total + s_got[1, step]
+    norm[...] = jnp.broadcast_to(jnp.sqrt(jnp.sum(total, keepdims=True)), norm.shape)
+    for i in range(CHUNKS):
+        landed(gt.at[pl.ds(i * rows, rows), part(1 - x)], x_sem.at[i], who["x"])
+    landed(h_out.at[part(1 - x)], h_sem, who["x"])
+    landed(bt.at[1 - x], b_sem.at[1], who["x"])
+    for copy in own_copies:
+        copy.wait()
+    sends.finish()
+
+
+def adam_kernel(
+    owners, norm, bt, bw, bm, bv, g, w, m, v,
+    w_new, m_new, v_new, bw_new, bm_new, bv_new,
+):
+    step = pl.program_id(0)
+    per_step, width, block_rows = w.shape
+    half = width // 2
+    blocks = owners.shape[0] - 3
+    me = lax.axis_index("dp")
+    number = jnp.int32(0)
+    for j in range(blocks):
+        number += (owners[j] == me).astype(jnp.int32)
+    factor = 1.0 / jnp.maximum(norm[:1, :1], 1.0)
+    for r in range(per_step):
+        grad = g[r].astype(jnp.float32) * factor
+        valid = jnp.broadcast_to(step * per_step + r < number, (width, block_rows))
+        news = adam_step(w[r], m[r], v[r], grad, 0.1)
+        for ref, new in zip((w_new, m_new, v_new), news):
+            ref[r] = jnp.where(valid, new, 0.0)
+
+    @pl.when(step == 0)
+    def _():
+        lane_of = lax.broadcasted_iota(jnp.int32, (half, width), 1)
+        row_of = lax.broadcasted_iota(jnp.int32, (half, width), 0)
+        row = lax.broadcasted_iota(jnp.int32, (3, width), 0)
+        grads = jnp.zeros((3, width), jnp.float32)
+        valid = jnp.zeros((3, width), jnp.int32)
+        for gate in range(3):
+            owner, rank = bias_rank(owners, blocks, gate)
+            line = jnp.zeros((1, width), jnp.float32)
+            for h in range(2):
+                column = bt[h][:, gate : gate + 1]
+                line += jnp.sum(
+                    jnp.where(lane_of == row_of + h * half, column, 0.0), axis=0, keepdims=True
+                )
+            here = (row == rank) & jnp.broadcast_to(owner == me, (3, width))
+            grads = jnp.where(here, line, grads)
+            valid = jnp.where(here, 1, valid)
+        news = adam_step(bw[...], bm[...], bv[...], grads * factor, 0.0)
+        for ref, new in zip((bw_new, bm_new, bv_new), news):
+            ref[...] = jnp.where(valid > 0, new, 0.0)
+
+
+def paired(
+    inputs, resets, owners, kernel, kernel_first, kernel_second, bias_rows, bias_first, bias_second, cotangent
+):
+    _, width, length = inputs.shape
+    slots, _, block_rows = kernel.shape
+    blocks = owners.shape[0] - 3
+    full = width * lax.axis_size("mp")
+    depth = lax.axis_size("mp") // 2
+    half = width // 2
+    bf16, f32 = jnp.bfloat16, jnp.float32
+    shape = jax.ShapeDtypeStruct
+    hbm = pl.BlockSpec(memory_space=pltpu.MemorySpace.HBM)
+    vmem = pl.BlockSpec(memory_space=pltpu.VMEM)
+    smem = pl.BlockSpec(memory_space=pltpu.SMEM)
+    dma = pltpu.SemaphoreType.DMA
+    wg, xg, cg, rg, bg = pl.pallas_call(
+        gather_kernel,
+        out_shape=(
+            shape((4 * slots, half, block_rows), bf16),
+            shape((2, full, length), bf16),
+            shape((2, half, length), bf16),
+            shape((2, 1, length), jnp.int32),
+            shape((4, 3, width), f32),
+        ),
+        in_specs=[hbm] * 5,
+        out_specs=[hbm] * 5,
+        scratch_shapes=[
+            pltpu.VMEM((slots, width, block_rows), f32),
+            pltpu.VMEM((slots, width, block_rows), bf16),
+            dma((CHUNKS,)),
+            dma((4 + CHUNKS,)),
+            dma((64,)),
+            dma((4, CHUNKS)),
+            dma((2, 2 * depth)),
+            dma,
+            dma,
+            dma((4,)),
+        ],
+        compiler_params=pltpu.CompilerParams(
+            collective_id=0, has_side_effects=True, vmem_limit_bytes=24 * 2**20
+        ),
+        name="gather",
+    )(
+        kernel,
+        inputs.reshape(width, length),
+        cotangent.reshape(width, length),
+        resets,
+        bias_rows,
+    )
+    h, gs, joined, wv, bgrad = pl.pallas_call(
+        layer_kernel,
+        out_shape=(
+            shape((2, half, length), bf16),
+            shape((4 * slots, half, block_rows), bf16),
+            shape((6 * half, 2 * length), bf16),
+            shape((6 * half, full), bf16),
+            shape((half, LANES), f32),
+        ),
+        in_specs=[smem, hbm, hbm, vmem, vmem, vmem],
+        out_specs=[vmem, hbm, hbm, hbm, vmem],
+        scratch_shapes=[
+            pltpu.SMEM((blocks,), jnp.int32),
+            pltpu.SMEM((4,), jnp.int32),
+            pltpu.VMEM((6 * half, full), bf16),
+            pltpu.VMEM((2, full, length), bf16),
+            pltpu.VMEM((6 * half, length), f32),
+            pltpu.VMEM((6 * half, 2 * length), bf16),
+            pltpu.VMEM((full // block_rows, 6 * half, block_rows), bf16),
+            pltpu.VMEM((3 * half, LANES), f32),
+            dma,
+            dma((2,)),
+            dma((2,)),
+        ],
+        compiler_params=pltpu.CompilerParams(vmem_limit_bytes=56 * 2**20),
+        name="layer",
+    )(owners, wg, xg, cg, rg, bg)
+    gt, h_new, ig, bt, norm = pl.pallas_call(
+        reduce_kernel,
+        out_shape=(
+            shape((slots, width, block_rows), bf16),
+            shape((width, length), bf16),
+            shape((width, length), bf16),
+            shape((2, half, LANES), f32),
+            shape((8, LANES), f32),
+        ),
+        in_specs=[smem, hbm, hbm, hbm, hbm, vmem],
+        out_specs=[hbm, hbm, hbm, vmem, vmem],
+        scratch_shapes=[
+            pltpu.VMEM((6 * half, full), bf16),
+            pltpu.VMEM((6 * half, 2 * length), bf16),
+            pltpu.VMEM((2, full, length), bf16),
+            pltpu.VMEM((2, depth, width, length), bf16),
+            pltpu.VMEM((2, depth, width, length), bf16),
+            pltpu.VMEM((2, depth, width, length), bf16),
+            pltpu.VMEM((width, length), bf16),
+            pltpu.VMEM((2, slots, half, block_rows), bf16),
+            pltpu.VMEM((2, slots, half, block_rows), bf16),
+            pltpu.VMEM((2, slots, half, block_rows), bf16),
+            pltpu.VMEM((2, half, LANES), f32),
+            pltpu.VMEM((8, block_rows), f32),
+            pltpu.VMEM((2, 5, 8, LANES), f32),
+            dma((4,)),
+            dma((2 + CHUNKS,)),
+            dma((64,)),
+            dma((2, CHUNKS)),
+            dma((CHUNKS,)),
+            dma((2, depth)),
+            dma((2, depth)),
+            dma((2, depth)),
+            dma,
+            dma,
+            dma((2,)),
+            dma((5,)),
+        ],
+        compiler_params=pltpu.CompilerParams(
+            collective_id=1, has_side_effects=True, vmem_limit_bytes=61 * 2**20
+        ),
+        name="reduce",
+    )(owners, gs, wv, joined, h, bgrad)
+    per_step = 2
+    block = pl.BlockSpec((per_step, width, block_rows), lambda i: (i, 0, 0))
+    whole = lambda *dims: pl.BlockSpec(dims, lambda i: (0,) * len(dims))
+    news = pl.pallas_call(
+        adam_kernel,
+        grid=(slots // per_step,),
+        out_shape=(shape(kernel.shape, f32),) * 3 + (shape(bias_rows.shape, f32),) * 3,
+        in_specs=[smem, whole(8, LANES), whole(2, half, LANES)]
+        + [whole(*bias_rows.shape)] * 3
+        + [block] * 4,
+        out_specs=[block] * 3 + [whole(*bias_rows.shape)] * 3,
+        compiler_params=pltpu.CompilerParams(vmem_limit_bytes=32 * 2**20),
+        name="adam",
+    )(owners, norm, bt, bias_rows, bias_first, bias_second, gt, kernel, kernel_first, kernel_second)
+    kernel_w, kernel_m, kernel_v, bias_w, bias_m, bias_v = news
+    return (h_new[None], ig[None], kernel_w, kernel_m, kernel_v, bias_w, bias_m, bias_v, norm[0, 0])
+
+
 def solution(mesh):
     placed = (
         P("dp", "mp", None),
@@ -171,8 +991,9 @@
         P("dp", "mp"),
         P("dp", "mp", None),
     )
+    fits = mesh.shape["dp"] == 4 and mesh.shape["mp"] == 8
     return jax.shard_map(
-        shards,
+        paired if fits else shards,
         mesh=mesh,
         in_specs=placed,
         out_specs=(

time: 1850 us -> 313 us (0.17)
  local copies, waits for them, and re-layouts: 1120 us -> 27.6 us
  waiting for transfers between devices: 433 us -> 0 us
  Pallas kernels: 0 us -> 281 us
  other arithmetic: 167 us -> 0 us
  blocking collectives: 62.6 us -> 0 us
  matrix products: 36.8 us -> 0 us
    pad x79 -> x0, local copies, waits for them, and re-layouts: 502 us -> none  [pooled(): lax.associative_scan(combine, (decay, (1.0 - forget) * candidate), axis=2)]
    slice x77 -> x1, local copies, waits for them, and re-layouts: 478 us -> 1.19 us  [paired(): norm[0, 0]]
    pallas_call x0 -> x4, Pallas kernels: none -> 281 us  [the longest x1 127 us: paired(): pl.pallas_call(reduce_kernel, out_shape=(shape((slots, width, block_rows)...]
    psum x1 -> x0, waiting for transfers between devices: 267 us -> none  [shards(): total_kernel, total_bias = lax.psum((block_grad, bias_grad), 'dp')]
    all_gather x2 -> x0, waiting for transfers between devices: 140 us -> none  [the longest x1 126 us: shards(): lax.all_gather(kernel.astype(jnp.bfloat16), 'dp', axis=0, tiled=True)]
    psum x2 -> x0, blocking collectives: 53 us -> none  [the longest x1 42.6 us: shards(): grad_norm = jnp.sqrt(lax.psum(squares, ('dp', 'mp')))]
    transpose x2 -> x0, local copies, waits for them, and re-layouts: 44.2 us -> none  [the longest x1 27.9 us: shards(): pair_grad.reshape(2, 3, local_width, full_width).transpose(1, 2, 0, 3)]
    dot_general x3 -> x0, matrix products: 36.8 us -> none  [the longest x1 13.3 us: shards(): jnp.einsum('ok,sol->ksl', rows, joined, preferred_element_type=jnp.float32)]
  transfers between devices with their start and end apart: 4 -> 0, of which waited for: 4 -> 0; matrix products, arithmetic and copies ran while one was open for 5% -> 0% of each run, Pallas kernels for 0% -> 0%
where the time goes in v1:
time: 313 us; the launch traced here: 309 us
  Pallas kernels  281 us (90%)
  local copies, waits for them, and re-layouts  27.6 us (9%)
    pallas_call x1, Pallas kernels, paired(): pl.pallas_call(reduce_kernel, out_shape=(shape((slots, width, block_rows)...  127 us
    pallas_call x1, Pallas kernels, paired(): pl.pallas_call(gather_kernel, out_shape=(shape((4 * slots, half, block_ro...  88.9 us
    pallas_call x1, Pallas kernels, paired(): pl.pallas_call(layer_kernel, out_shape=(shape((2, half, length), bf16), s...  47.4 us
    unnamed x44, local copies, waits for them, and re-layouts  26.4 us
    pallas_call x1, Pallas kernels, paired(): pl.pallas_call(adam_kernel, grid=(slots // per_step,), out_shape=(shape(k...  17.8 us

profile of v1, /device:TPU:0, one launch (start us, length us, event | category | flops | bytes accessed | tf_op | source)
XLA Modules:
  0.0 309.0 jit_solution(17862621476726175247)
XLA Ops:
  0.6 0.0 copy-start
  0.7 3.0 copy-done
  3.7 0.0 copy-start.7
  3.7 1.1 copy-done.7
  4.7 0.0 copy-start.8
  4.7 1.1 copy-done.8
  5.8 0.0 copy-start.10
  5.8 0.7 copy-done.10
  6.5 0.0 copy-start.17
  6.5 0.7 copy-done.17
  7.2 88.9 %gather.1 = (bf16[96,144,256]{2,1,0:T(8,128)(2,1)S(1)}, bf16[2,2304,1024]{2,1,0:T(8,128)(2,1)S(1)}, bf16[2,144,1024]{2,1,0:T(8,128)(2,1)S(1)}, s32[2,1,1024]{2,1,0:T(1,128)S(1)}, f32[4,3,288]{2,1,0:T(4,128)S(1)}) custom-call(f32[24,288,256]{2,1,0:T(8,128)S(1)} %copy-done, bf16[288,1024]{1,0:T(8,128)(2,1)S(1)} %bitcast.5, bf16[288,1024]{1,0:T(8,128)(2,1)S(1)} %bitcast.6, ...), custom_call_target="tpu_custom_call" | custom-call | tf_op jit(solution)/shard_map/gather/pallas_call | solution.py:859
  96.0 0.0 copy-start.2
  96.0 3.7 %copy-done.2 = bf16[2,2304,1024]{2,1,0:T(8,128)(2,1)} copy-done((bf16[2,2304,1024]{2,1,0:T(8,128)(2,1)}, bf16[2,2304,1024]{2,1,0:T(8,128)(2,1)S(1)}, u32[]{:S(2)}) %copy-start.2) | copy-done | bytes 9437208
  99.7 0.0 copy-start.4
  99.7 3.0 copy-done.4
  102.7 0.0 copy-start.6
  102.7 0.8 copy-done.6
  103.5 0.0 copy-start.12
  103.5 0.6 copy-done.12
  104.1 0.0 copy-start.13
  104.1 0.6 copy-done.13
  104.7 47.4 %layer.1 = (bf16[2,144,1024]{2,1,0:T(8,128)(2,1)}, bf16[96,144,256]{2,1,0:T(8,128)(2,1)}, bf16[864,2048]{1,0:T(8,128)(2,1)}, bf16[864,2304]{1,0:T(8,128)(2,1)}, f32[144,128]{1,0:T(8,128)}) custom-call(s32[57]{0:T(128)} %owners.5, bf16[96,144,256]{2,1,0:T(8,128)(2,1)} %copy-done.4, bf16[2,2304,1024]{2,1,0:T(8,128)(2,1)} %copy-done.2, ...), custom_call_target="tpu_custom_call" | custom-call | tf_op jit(solution)/shard_map/layer/pallas_call | solution.py:893
  152.1 0.0 copy-start.11
  152.1 0.0 copy-start.14
  152.1 0.0 copy-start.15
  152.1 0.0 copy-start.16
  152.1 126.7 %reduce.1 = (bf16[24,288,256]{2,1,0:T(8,128)(2,1)}, bf16[288,1024]{1,0:T(8,128)(2,1)}, bf16[288,1024]{1,0:T(8,128)(2,1)}, f32[2,144,128]{2,1,0:T(8,128)}, f32[8,128]{1,0:T(8,128)}) custom-call(s32[57]{0:T(128)} %owners.5, bf16[96,144,256]{2,1,0:T(8,128)(2,1)} %get-tuple-element.35.gs, bf16[864,2304]{1,0:T(8,128)(2,1)} %get-tuple-element.36.w_hbm, ...), custom_call_target="tpu_custom_call" | custom-call | tf_op jit(solution)/shard_map/reduce/pallas_call | solution.py:920
  278.8 1.2 slice.3
  280.0 0.0 copy-done.11
  280.0 0.0 copy-done.14
  280.0 0.0 copy-done.15
  280.0 0.0 copy-done.16
  280.0 0.0 copy-start.1
  280.0 3.0 copy-done.1
  283.0 0.0 copy-start.3
  283.0 3.0 copy-done.3
  286.0 0.0 copy-start.5
  286.0 2.0 copy-done.5
  288.0 0.0 copy-start.9
  288.0 0.9 copy-done.9
  288.9 0.0 copy-start.18
  288.9 0.7 copy-done.18
  289.6 0.0 copy-start.20
  289.6 0.0 copy-start.19
  289.6 17.8 %adam.1 = (f32[24,288,256]{2,1,0:T(8,128)}, f32[24,288,256]{2,1,0:T(8,128)}, f32[24,288,256]{2,1,0:T(8,128)}, f32[3,288]{1,0:T(4,128)}, f32[3,288]{1,0:T(4,128)}, /*index=5*/f32[3,288]{1,0:T(4,128)}) custom-call(s32[57]{0:T(128)S(1)} %copy-done.16, f32[8,128]{1,0:T(8,128)S(1)} %copy-done.18, f32[2,144,128]{2,1,0:T(8,128)S(1)} %copy-done.9, ...), custom_call_target="tpu_custom_call" | custom-call | tf_op jit(solution)/shard_map/adam/pallas_call | solution.py:966
  307.4 0.0 copy-done.20
  307.4 0.8 copy.21
  308.2 0.0 copy-done.19
  308.2 0.8 copy.22
Async XLA Ops:
  0.6 3.0 copy-start
  3.7 1.1 copy-start.7
  4.7 1.1 copy-start.8
  5.8 0.7 copy-start.10
  6.5 0.7 copy-start.17
  96.0 3.7 %copy-start.2 = (bf16[2,2304,1024]{2,1,0:T(8,128)(2,1)}, bf16[2,2304,1024]{2,1,0:T(8,128)(2,1)S(1)}, u32[]{:S(2)}) copy-start(bf16[2,2304,1024]{2,1,0:T(8,128)(2,1)S(1)} %get-tuple-element.31.xg) | copy-start | bytes 28311556
  99.7 3.0 copy-start.4
  102.7 0.8 copy-start.6
  103.5 0.6 copy-start.12
  104.1 0.6 copy-start.13
  152.1 127.9 %copy-start.11 = (f32[3,288]{1,0:T(4,128)S(1)}, f32[3,288]{1,0:T(4,128)}, u32[]{:S(2)}) copy-start(f32[3,288]{1,0:T(4,128)} %bw.1) | copy-start | bytes 10372
  152.1 127.9 %copy-start.14 = (f32[3,288]{1,0:T(4,128)S(1)}, f32[3,288]{1,0:T(4,128)}, u32[]{:S(2)}) copy-start(f32[3,288]{1,0:T(4,128)} %bm.1) | copy-start | bytes 10372
  152.1 127.9 %copy-start.15 = (f32[3,288]{1,0:T(4,128)S(1)}, f32[3,288]{1,0:T(4,128)}, u32[]{:S(2)}) copy-start(f32[3,288]{1,0:T(4,128)} %bv.1) | copy-start | bytes 10372
  152.1 127.9 %copy-start.16 = (s32[57]{0:T(128)S(1)}, s32[57]{0:T(128)}, u32[]{:S(2)}) copy-start(s32[57]{0:T(128)} %owners.5) | copy-start | bytes 688
  280.0 3.0 copy-start.1
  283.0 3.0 copy-start.3
  286.0 2.0 copy-start.5
  288.0 0.9 copy-start.9
  288.9 0.7 copy-start.18
  289.6 17.8 %copy-start.20 = (bf16[288,1024]{1,0:T(8,128)(2,1)S(1)}, bf16[288,1024]{1,0:T(8,128)(2,1)}, u32[]{:S(2)}) copy-start(bf16[288,1024]{1,0:T(8,128)(2,1)} %get-tuple-element.40) | copy-start | bytes 1769476
  289.6 18.6 %copy-start.19 = (bf16[288,1024]{1,0:T(8,128)(2,1)S(1)}, bf16[288,1024]{1,0:T(8,128)(2,1)}, u32[]{:S(2)}) copy-start(bf16[288,1024]{1,0:T(8,128)(2,1)} %get-tuple-element.41) | copy-start | bytes 1769476

commit v2 on v1

--- a/solution.py
+++ b/solution.py
@@ -163,6 +163,8 @@
 MESH_ID = pl.DeviceIdType.MESH
 LANES = 128
 CHUNKS = 4
+PIECES = 3
+VMEM = 61 * 2**20
 
 
 def place():
@@ -182,7 +184,7 @@
     }
 
 
-def greet(who, names, z, depth):
+def greet(who, names, z, depth, more=0):
     barrier = pltpu.get_barrier_semaphore()
     for name in names:
         pl.semaphore_signal(barrier, inc=1, device_id=who[name], device_id_type=MESH_ID)
@@ -196,7 +198,7 @@
         pl.semaphore_signal(barrier, inc=1, device_id=who["down"], device_id_type=MESH_ID)
 
     both = (z < depth - 1).astype(jnp.int32) + (z > 0).astype(jnp.int32)
-    pl.semaphore_wait(barrier, len(names) + both)
+    pl.semaphore_wait(barrier, len(names) + more + both)
 
 
 class Sends:
@@ -541,8 +543,8 @@
 def reduce_kernel(
     owners, gs, w_hbm, j_hbm, h_in, bgrad,
     gt, h_out, ig_out, bt, norm,
-    wv, jv, ig, up_got, down_got, core_got, x_got, y_got, y_own, x_give, b_got, squares, s_got,
-    load_sem, own_sem, send_sem, y_sem, x_sem, core_sem, up_sem, down_sem, ix_sem, h_sem, b_sem, s_sem,
+    wv, jv, ig, up_got, down_got, core_got, x_got, y_got, y_own, b_got, squares, s_got,
+    load_sem, own_sem, send_sem, y_sem, x_sem, core_sem, up_sem, down_sem, z_send, ix_sem, h_sem, b_sem, s_sem,
 ):
     y, x, z, c = place()
     who = partners(y, x, z, c)
@@ -551,9 +553,10 @@
     length = h_out.shape[1]
     full = w_hbm.shape[1]
     depth = full // width // 2
-    rows = slots // CHUNKS
+    rows = slots // PIECES
     blocks = 6 * (full // block_rows)
     tile = 16
+    streams = (1 - x, x)
 
     def part(index):
         return pl.ds(pl.multiple_of(index * half, half), half)
@@ -567,55 +570,42 @@
     ]
     for load in loads:
         load.start()
-    owner_x = (1 - x, x)
     own_loads = []
     for q in range(2):
         copy = pltpu.make_async_copy(
-            gs.at[pl.ds((y * 2 + owner_x[q]) * slots, slots)], y_own.at[q], load_sem.at[2 + q]
+            gs.at[pl.ds((y * 2 + streams[q]) * slots, slots)], y_own.at[q], load_sem.at[2 + q]
         )
         copy.start()
         own_loads.append(copy)
     h_own = pltpu.make_async_copy(h_in.at[x], h_out.at[part(x)], own_sem.at[0])
     h_own.start()
-    greet_extra = jnp.bitwise_xor(z, 2) * 2 + c
+    near = (y * 2 + x, jnp.bitwise_xor(z, 1) * 2 + c)
+    far_off = (y * 2 + x, jnp.bitwise_xor(z, 2) * 2 + c)
     barrier = pltpu.get_barrier_semaphore()
-    flip_near = (y * 2 + x, jnp.bitwise_xor(z, 1) * 2 + c)
-    flip_far = (y * 2 + x, greet_extra)
-    pl.semaphore_signal(barrier, inc=1, device_id=flip_near, device_id_type=MESH_ID)
-    pl.semaphore_signal(barrier, inc=1, device_id=flip_far, device_id_type=MESH_ID)
-    for name in ("x", "y", "core"):
-        pl.semaphore_signal(barrier, inc=1, device_id=who[name], device_id_type=MESH_ID)
-
-    @pl.when(z < depth - 1)
-    def _():
-        pl.semaphore_signal(barrier, inc=1, device_id=who["up"], device_id_type=MESH_ID)
-
-    @pl.when(z > 0)
-    def _():
-        pl.semaphore_signal(barrier, inc=1, device_id=who["down"], device_id_type=MESH_ID)
-
-    both = (z < depth - 1).astype(jnp.int32) + (z > 0).astype(jnp.int32)
-    pl.semaphore_wait(barrier, 5 + both)
+    for device in (near, far_off):
+        pl.semaphore_signal(barrier, inc=1, device_id=device, device_id_type=MESH_ID)
+    greet(who, ("x", "y", "core"), z, depth, 2)
 
     sends = Sends(send_sem)
+
+    def y_send(t):
+        q, i = t // PIECES, t % PIECES
+        sends.start(
+            lambda: gs.at[pl.ds(((1 - y) * 2 + streams[q]) * slots + i * rows, rows)],
+            lambda: y_got.at[q, pl.ds(i * rows, rows)],
+            y_sem.at[q, i],
+            who["y"],
+        )
+
+    y_send(0)
+    y_send(1)
     sends.start(lambda: bgrad, lambda: b_got.at[0], b_sem.at[0], who["y"])
-    for q in range(2):
-        for i in range(CHUNKS):
-            sends.start(
-                lambda q=q, i=i: gs.at[
-                    pl.ds(((1 - y) * 2 + owner_x[q]) * slots + i * rows, rows)
-                ],
-                lambda q=q, i=i: y_got.at[q, pl.ds(i * rows, rows)],
-                y_sem.at[q, i],
-                who["y"],
-            )
     sends.start(lambda: h_in.at[1 - x], lambda: h_out.at[part(x)], h_sem, who["x"])
     for load in loads:
         load.wait()
-    streams = (1 - x, x)
-    for q in range(2):
-
-        def input_grad(k, _, q=q):
+
+    def input_grad(q):
+        def one(k, _):
             columns = pl.ds(pl.multiple_of(k * 256, 256), 256)
             lanes = pl.ds(pl.multiple_of(streams[q] * length, length), length)
             ig[q, columns, :] = lax.dot_general(
@@ -626,90 +616,123 @@
             ).astype(jnp.bfloat16)
             return 0
 
-        lax.fori_loop(0, full // 256, input_grad, 0)
+        lax.fori_loop(0, full // 256, one, 0)
         for k in range(depth):
             sends.start(
-                lambda q=q, k=k: ig.at[q, rows_of(k, 1 - c)],
-                lambda q=q, k=k: core_got.at[q, k],
+                lambda k=k: ig.at[q, rows_of(k, 1 - c)],
+                lambda k=k: core_got.at[q, k],
                 core_sem.at[q, k],
                 who["core"],
             )
 
-    def add_tiles(dst, refs):
+    def add_tiles(refs):
         def one(i, _):
             at = pl.ds(pl.multiple_of(i * tile, tile), tile)
             total = refs[0][at, :].astype(jnp.float32)
             for ref in refs[1:]:
                 total += ref[at, :].astype(jnp.float32)
-            dst[at, :] = total.astype(jnp.bfloat16)
+            refs[0][at, :] = total.astype(jnp.bfloat16)
             return 0
 
         lax.fori_loop(0, width // tile, one, 0)
 
-    def chip_sum(q, k):
-        landed(core_got.at[q, k], core_sem.at[q, k], who["core"])
-        mine = ig.at[q, rows_of(k, c)]
-        add_tiles(mine, (mine, core_got.at[q, k]))
-
-    def z_step(q, k):
-        far = depth - 1 - k
-
-        @pl.when((z > 0) & (z < far))
-        def _():
-            mine = ig.at[q, rows_of(far, c)]
-            landed(up_got.at[q, far], up_sem.at[q, far], who["down"])
-            add_tiles(mine, (mine, up_got.at[q, far]))
-
-        sends.start(
-            lambda: ig.at[q, rows_of(far, c)],
-            lambda: up_got.at[q, far],
-            up_sem.at[q, far],
-            who["up"],
-            z < far,
+    def z_send_of(q, dest, got, recv, device, sem):
+        return pltpu.make_async_remote_copy(
+            src_ref=ig.at[q, rows_of(dest, c)],
+            dst_ref=got.at[q, dest],
+            send_sem=sem,
+            recv_sem=recv.at[q, dest],
+            device_id=device,
+            device_id_type=MESH_ID,
         )
 
-        @pl.when((z < depth - 1) & (z > k))
-        def _():
-            mine = ig.at[q, rows_of(k, c)]
-            landed(down_got.at[q, k], down_sem.at[q, k], who["up"])
-            add_tiles(mine, (mine, down_got.at[q, k]))
-
-        sends.start(
-            lambda: ig.at[q, rows_of(k, c)],
-            lambda: down_got.at[q, k],
-            down_sem.at[q, k],
-            who["down"],
-            z > k,
-        )
+    def z_tick(t):
+        hops = depth - 1
+        for index, (after, got, recv, source, target) in enumerate(
+            (
+                (z, up_got, up_sem, who["down"], who["up"]),
+                (depth - 1 - z, down_got, down_sem, who["up"], who["down"]),
+            )
+        ):
+            item = t - after
+            k = lax.rem(jnp.maximum(item, 0), hops)
+            q = jnp.maximum(item, 0) // hops
+            dest = depth - 1 - k if index == 0 else k
+            on = (item >= 0) & (after < depth - 1 - k)
+
+            @pl.when(on)
+            def _(index=index, after=after, got=got, recv=recv, source=source, target=target, item=item, q=q, dest=dest):
+                landed(core_got.at[q, dest], core_sem.at[q, dest], who["core"])
+                mine = ig.at[q, rows_of(dest, c)]
+
+                @pl.when(after == 0)
+                def _():
+                    add_tiles((mine, core_got.at[q, dest]))
+
+                @pl.when(after > 0)
+                def _():
+                    landed(got.at[q, dest], recv.at[q, dest], source)
+                    add_tiles((mine, core_got.at[q, dest], got.at[q, dest]))
+
+                send = z_send_of(q, dest, got, recv, target, z_send.at[index])
+
+                @pl.when(item > 0)
+                def _():
+                    send.wait_send()
+
+                send.start()
 
     def z_last(q):
+        landed(core_got.at[q, z], core_sem.at[q, z], who["core"])
+        extra = (core_got.at[q, z],)
+        if q == 1:
+            landed(x_got, ix_sem, who["x"])
+            extra += (x_got,)
         mine = ig.at[q, rows_of(z, c)]
 
         @pl.when(z > 0)
         def _():
             landed(up_got.at[q, z], up_sem.at[q, z], who["down"])
-            add_tiles(mine, (mine, up_got.at[q, z]))
 
         @pl.when(z < depth - 1)
         def _():
             landed(down_got.at[q, z], down_sem.at[q, z], who["up"])
-            add_tiles(mine, (mine, down_got.at[q, z]))
+
+        @pl.when(z == 0)
+        def _():
+            add_tiles((mine, *extra, down_got.at[q, z]))
+
+        @pl.when(z == depth - 1)
+        def _():
+            add_tiles((mine, *extra, up_got.at[q, z]))
+
+        @pl.when((z > 0) & (z < depth - 1))
+        def _():
+            add_tiles((mine, *extra, up_got.at[q, z], down_got.at[q, z]))
 
         if q == 0:
             sends.start(lambda: mine, lambda: x_got, ix_sem, who["x"])
+        else:
+            copy = pltpu.make_async_copy(mine, ig_out, own_sem.at[1])
+            copy.start()
+            own_copies.append(copy)
 
     squares[...] = jnp.zeros_like(squares)
     owned = []
     for q in range(2):
         number = jnp.int32(0)
         for j in range(blocks):
-            number += (owners[j] == y * 2 + owner_x[q]).astype(jnp.int32)
+            number += (owners[j] == y * 2 + streams[q]).astype(jnp.int32)
         owned.append(number)
-
-    def own_chunk(q, i):
+    own_copies = [h_own]
+
+    def own_chunk(t):
+        q, i = t // PIECES, t % PIECES
         if i == 0:
             own_loads[q].wait()
         landed(y_got.at[q, pl.ds(i * rows, rows)], y_sem.at[q, i], who["y"])
+        if t + 2 < 2 * PIECES:
+            y_send(t + 2)
 
         def one(r, _):
             valid = jnp.broadcast_to(i * rows + r < owned[q], (half, block_rows))
@@ -717,28 +740,19 @@
                 jnp.float32
             )
             total = jnp.where(valid, total, 0.0)
-            x_give[q, i * rows + r] = total.astype(jnp.bfloat16)
+            y_own[q, i * rows + r] = total.astype(jnp.bfloat16)
             squares[...] += jnp.sum((total * total).reshape(half // 8, 8, block_rows), axis=0)
             return 0
 
         lax.fori_loop(0, rows, one, 0)
+        src = lambda: y_own.at[q, pl.ds(i * rows, rows)]
+        dst = lambda: gt.at[pl.ds(i * rows, rows), part(x)]
         if q == 0:
-            sends.start(
-                lambda: x_give.at[0, pl.ds(i * rows, rows)],
-                lambda: gt.at[pl.ds(i * rows, rows), part(x)],
-                x_sem.at[i],
-                who["x"],
-            )
+            sends.start(src, dst, x_sem.at[i], who["x"])
         else:
-            copy = pltpu.make_async_copy(
-                x_give.at[1, pl.ds(i * rows, rows)],
-                gt.at[pl.ds(i * rows, rows), part(x)],
-                own_sem.at[1 + i],
-            )
+            copy = pltpu.make_async_copy(src(), dst(), own_sem.at[2 + i])
             copy.start()
             own_copies.append(copy)
-
-    own_copies = [h_own]
 
     def bias_sum():
         landed(b_got.at[0], b_sem.at[0], who["y"])
@@ -750,35 +764,28 @@
         each = jnp.where(counted, total * total, 0.0)
         squares[:, pl.ds(0, LANES)] += jnp.sum(each.reshape(half // 8, 8, LANES), axis=0)
 
-    bias_sum()
-    for k in range(depth):
-        chip_sum(0, k)
-    z_step(0, 0)
-    own_chunk(0, 0)
-    for k in range(depth):
-        chip_sum(1, k)
-    z_step(0, 1)
-    z_step(1, 0)
-    own_chunk(0, 1)
-    z_step(0, 2)
-    z_step(1, 1)
-    own_chunk(0, 2)
-    z_last(0)
-    own_chunk(0, 3)
-    z_step(1, 2)
-    own_chunk(1, 0)
-    z_last(1)
-    own_chunk(1, 1)
-    own_chunk(1, 2)
-    landed(x_got, ix_sem, who["x"])
-    mine = ig.at[1, rows_of(z, c)]
-    add_tiles(mine, (mine, x_got))
-    copy = pltpu.make_async_copy(mine, ig_out, own_sem.at[1 + CHUNKS])
-    copy.start()
-    own_copies.append(copy)
-    own_chunk(1, 3)
+    input_grad(0)
+    ticks = 2 * (depth - 1)
+    z_tick(0)
+    input_grad(1)
+    chunks = 2 * PIECES
+    done = 0
+    for t in range(1, ticks + 1):
+        upto = chunks * t // ticks
+        if t == ticks:
+            upto = chunks - 1
+        for i in range(done, upto):
+            own_chunk(i)
+        done = upto
+        if t == 1:
+            bias_sum()
+        if t < ticks:
+            z_tick(t)
+        if t == depth - 1:
+            z_last(0)
+    own_chunk(chunks - 1)
     total = squares[:, pl.ds(0, LANES)] + squares[:, pl.ds(LANES, LANES)]
-    for step, device in enumerate((who["core"], flip_near, flip_far, who["x"], who["y"])):
+    for step, device in enumerate((who["core"], near, far_off, who["x"], who["y"])):
         s_got[0, step] = total
         sends.start(
             lambda step=step: s_got.at[0, step],
@@ -789,10 +796,20 @@
         landed(s_got.at[1, step], s_sem.at[step], device)
         total = total + s_got[1, step]
     norm[...] = jnp.broadcast_to(jnp.sqrt(jnp.sum(total, keepdims=True)), norm.shape)
-    for i in range(CHUNKS):
+    z_last(1)
+    for i in range(PIECES):
         landed(gt.at[pl.ds(i * rows, rows), part(1 - x)], x_sem.at[i], who["x"])
     landed(h_out.at[part(1 - x)], h_sem, who["x"])
     landed(bt.at[1 - x], b_sem.at[1], who["x"])
+
+    @pl.when(z < depth - 1)
+    def _():
+        z_send_of(0, z + 1, up_got, up_sem, who["up"], z_send.at[0]).wait_send()
+
+    @pl.when(z > 0)
+    def _():
+        z_send_of(0, z - 1, down_got, down_sem, who["down"], z_send.at[1]).wait_send()
+
     for copy in own_copies:
         copy.wait()
     sends.finish()
@@ -880,7 +897,7 @@
             dma((4,)),
         ],
         compiler_params=pltpu.CompilerParams(
-            collective_id=0, has_side_effects=True, vmem_limit_bytes=24 * 2**20
+            collective_id=0, has_side_effects=True, vmem_limit_bytes=VMEM
         ),
         name="gather",
     )(
@@ -914,7 +931,7 @@
             dma((2,)),
             dma((2,)),
         ],
-        compiler_params=pltpu.CompilerParams(vmem_limit_bytes=56 * 2**20),
+        compiler_params=pltpu.CompilerParams(vmem_limit_bytes=VMEM),
         name="layer",
     )(owners, wg, xg, cg, rg, bg)
     gt, h_new, ig, bt, norm = pl.pallas_call(
@@ -938,25 +955,25 @@
             pltpu.VMEM((width, length), bf16),
             pltpu.VMEM((2, slots, half, block_rows), bf16),
             pltpu.VMEM((2, slots, half, block_rows), bf16),
-            pltpu.VMEM((2, slots, half, block_rows), bf16),
             pltpu.VMEM((2, half, LANES), f32),
             pltpu.VMEM((8, block_rows), f32),
             pltpu.VMEM((2, 5, 8, LANES), f32),
             dma((4,)),
-            dma((2 + CHUNKS,)),
+            dma((2 + PIECES,)),
             dma((64,)),
-            dma((2, CHUNKS)),
-            dma((CHUNKS,)),
+            dma((2, PIECES)),
+            dma((PIECES,)),
             dma((2, depth)),
             dma((2, depth)),
             dma((2, depth)),
+            dma((2,)),
             dma,
             dma,
             dma((2,)),
             dma((5,)),
         ],
         compiler_params=pltpu.CompilerParams(
-            collective_id=1, has_side_effects=True, vmem_limit_bytes=61 * 2**20
+            collective_id=1, has_side_effects=True, vmem_limit_bytes=VMEM
         ),
         name="reduce",
     )(owners, gs, wv, joined, h, bgrad)
@@ -971,7 +988,7 @@
         + [whole(*bias_rows.shape)] * 3
         + [block] * 4,
         out_specs=[block] * 3 + [whole(*bias_rows.shape)] * 3,
-        compiler_params=pltpu.CompilerParams(vmem_limit_bytes=32 * 2**20),
+        compiler_params=pltpu.CompilerParams(vmem_limit_bytes=VMEM),
         name="adam",
     )(owners, norm, bt, bias_rows, bias_first, bias_second, gt, kernel, kernel_first, kernel_second)
     kernel_w, kernel_m, kernel_v, bias_w, bias_m, bias_v = news

time: 313 us -> 269 us (0.86); the launches traced: 309 us -> 269 us
  local copies, waits for them, and re-layouts: 27.6 us -> 2.83 us
  Pallas kernels: 281 us -> 265 us
    unnamed x44 -> x6, local copies, waits for them, and re-layouts: 26.4 us -> 1.64 us
    pallas_call x1, Pallas kernels: 127 us -> 107 us  [paired(): pl.pallas_call(reduce_kernel, out_shape=(shape((slots, width, block_rows)...]
    pallas_call x1, Pallas kernels: 17.8 us -> 23.1 us  [paired(): pl.pallas_call(adam_kernel, grid=(slots // per_step,), out_shape=(shape(k...]
where the time goes in v2:
time: 269 us
  Pallas kernels  265 us (99%)
  local copies, waits for them, and re-layouts  2.83 us (1%)
    pallas_call x1, Pallas kernels, paired(): pl.pallas_call(reduce_kernel, out_shape=(shape((slots, width, block_rows)...  107 us
    pallas_call x1, Pallas kernels, paired(): pl.pallas_call(gather_kernel, out_shape=(shape((4 * slots, half, block_ro...  88.3 us
    pallas_call x1, Pallas kernels, paired(): pl.pallas_call(layer_kernel, out_shape=(shape((2, half, length), bf16), s...  47.4 us
    pallas_call x1, Pallas kernels, paired(): pl.pallas_call(adam_kernel, grid=(slots // per_step,), out_shape=(shape(k...  23.1 us

profile of v2, /device:TPU:0, one launch (start us, length us, event | category | flops | bytes accessed | tf_op | source)
XLA Modules:
  0.0 269.0 jit_solution(6975446956126249144)
XLA Ops:
  0.6 88.3 %gather.1 = (bf16[96,144,256]{2,1,0:T(8,128)(2,1)}, bf16[2,2304,1024]{2,1,0:T(8,128)(2,1)}, bf16[2,144,1024]{2,1,0:T(8,128)(2,1)}, s32[2,1,1024]{2,1,0:T(1,128)}, f32[4,3,288]{2,1,0:T(4,128)}) custom-call(f32[24,288,256]{2,1,0:T(8,128)} %w.1, bf16[288,1024]{1,0:T(8,128)(2,1)} %bitcast.7, bf16[288,1024]{1,0:T(8,128)(2,1)} %bitcast.8, s32[1,1024]{1,0:T(1,128)} %res_ref.1, ...), custom_call_target="tpu_custom_call" | custom-call | tf_op jit(solution)/shard_map/gather/pallas_call | solution.py:876
  88.9 47.4 %layer.1 = (bf16[2,144,1024]{2,1,0:T(8,128)(2,1)}, bf16[96,144,256]{2,1,0:T(8,128)(2,1)}, bf16[864,2048]{1,0:T(8,128)(2,1)}, bf16[864,2304]{1,0:T(8,128)(2,1)}, f32[144,128]{1,0:T(8,128)}) custom-call(s32[57]{0:T(128)} %owners.5, bf16[96,144,256]{2,1,0:T(8,128)(2,1)} %get-tuple-element.30.wg, bf16[2,2304,1024]{2,1,0:T(8,128)(2,1)} %get-tuple-element.31.xg, ...), custom_call_target="tpu_custom_call" | custom-call | tf_op jit(solution)/shard_map/layer/pallas_call | solution.py:910
  136.3 106.7 %reduce.1 = (bf16[24,288,256]{2,1,0:T(8,128)(2,1)}, bf16[288,1024]{1,0:T(8,128)(2,1)}, bf16[288,1024]{1,0:T(8,128)(2,1)}, f32[2,144,128]{2,1,0:T(8,128)}, f32[8,128]{1,0:T(8,128)}) custom-call(s32[57]{0:T(128)} %owners.5, bf16[96,144,256]{2,1,0:T(8,128)(2,1)} %get-tuple-element.35.gs, bf16[864,2304]{1,0:T(8,128)(2,1)} %get-tuple-element.36.w_hbm, ...), custom_call_target="tpu_custom_call" | custom-call | tf_op jit(solution)/shard_map/reduce/pallas_call | solution.py:937
  243.0 1.2 slice.3
  244.2 0.0 copy-start.1
  244.2 0.0 copy-start
  244.2 23.1 %adam.1 = (f32[24,288,256]{2,1,0:T(8,128)}, f32[24,288,256]{2,1,0:T(8,128)}, f32[24,288,256]{2,1,0:T(8,128)}, f32[3,288]{1,0:T(4,128)}, f32[3,288]{1,0:T(4,128)}, /*index=5*/f32[3,288]{1,0:T(4,128)}) custom-call(s32[57]{0:T(128)} %owners.5, f32[8,128]{1,0:T(8,128)} %get-tuple-element.42.norm, f32[2,144,128]{2,1,0:T(8,128)} %get-tuple-element.43.bt, ...), custom_call_target="tpu_custom_call" | custom-call | tf_op jit(solution)/shard_map/adam/pallas_call | solution.py:983
  267.3 0.0 copy-done.1
  267.3 0.8 copy.21
  268.1 0.0 copy-done
  268.1 0.8 copy.22
Async XLA Ops:
  244.2 23.1 %copy-start.1 = (bf16[288,1024]{1,0:T(8,128)(2,1)S(1)}, bf16[288,1024]{1,0:T(8,128)(2,1)}, u32[]{:S(2)}) copy-start(bf16[288,1024]{1,0:T(8,128)(2,1)} %get-tuple-element.40) | copy-start | bytes 1769476
  244.2 23.9 %copy-start = (bf16[288,1024]{1,0:T(8,128)(2,1)S(1)}, bf16[288,1024]{1,0:T(8,128)(2,1)}, u32[]{:S(2)}) copy-start(bf16[288,1024]{1,0:T(8,128)(2,1)} %get-tuple-element.41) | copy-start | bytes 1769476

commit v3 on v2

--- a/solution.py
+++ b/solution.py
@@ -163,7 +163,7 @@
 MESH_ID = pl.DeviceIdType.MESH
 LANES = 128
 CHUNKS = 4
-PIECES = 3
+BANDS = 3
 VMEM = 61 * 2**20
 
 
@@ -242,15 +242,57 @@
     ).wait_recv()
 
 
+def fill_order(perm):
+    length = perm.shape[0]
+    tile = 16
+    column = lax.broadcasted_iota(jnp.int32, (tile, length), 1)
+    wanted = lax.rem(column, LANES) * (length // LANES) + column // LANES
+    wanted = wanted - lax.broadcasted_iota(jnp.int32, (tile, length), 0)
+
+    def one(i, _):
+        at = pl.ds(pl.multiple_of(i * tile, tile), tile)
+        perm[at, :] = jnp.where(wanted == i * tile, 1.0, 0.0).astype(jnp.bfloat16)
+        return 0
+
+    lax.fori_loop(0, length // tile, one, 0)
+
+
+def reorder(ref, perm):
+    tile = 96 if ref.shape[0] % 96 == 0 else 16
+
+    def one(i, _):
+        at = pl.ds(pl.multiple_of(i * tile, tile), tile)
+        moved = jnp.dot(ref[at, :], perm[...], preferred_element_type=jnp.float32)
+        ref[at, :] = moved.astype(ref.dtype)
+        return 0
+
+    lax.fori_loop(0, ref.shape[0] // tile, one, 0)
+
+
+def restore(src, dst, perm):
+    tile = 96 if src.shape[0] % 96 == 0 else 16
+
+    def one(i, _):
+        at = pl.ds(pl.multiple_of(i * tile, tile), tile)
+        moved = lax.dot_general(
+            src[at, :], perm[...], (((1,), (1,)), ((), ())), preferred_element_type=jnp.float32
+        )
+        dst[at, :] = moved.astype(dst.dtype)
+        return 0
+
+    lax.fori_loop(0, src.shape[0] // tile, one, 0)
+
+
 def gather_kernel(
     w_ref, x_ref, cot_ref, res_ref, bias_ref,
     wg, xg, cg, rg, bg,
-    wf, wb, load_sem, own_sem, send_sem, w_sem, x_sem, c_sem, r_sem, b_sem,
+    wf, wb, perm, xs, cs, rs, load_sem, own_sem, send_sem, w_sem, x_sem, c_sem, r_sem, b_sem,
 ):
     y, x, z, c = place()
     dp, mp = y * 2 + x, z * 2 + c
     who = partners(y, x, z, c)
     slots, width, _ = w_ref.shape
+    length = xg.shape[2]
     half = width // 2
     depth = xg.shape[1] // width // 2
     rows = slots // CHUNKS
@@ -267,17 +309,16 @@
         )
         for i in range(CHUNKS)
     ]
-    for load in loads:
+    takes = [
+        pltpu.make_async_copy(x_ref, xs, load_sem.at[CHUNKS]),
+        pltpu.make_async_copy(cot_ref, cs, load_sem.at[CHUNKS + 1]),
+    ]
+    for load in takes + loads:
         load.start()
-    own = [
-        pltpu.make_async_copy(x_ref, xg.at[x, rows_of(mp)], own_sem.at[0]),
-        pltpu.make_async_copy(cot_ref.at[part(x)], cg.at[x], own_sem.at[1]),
-        pltpu.make_async_copy(res_ref, rg.at[x], own_sem.at[2]),
-        pltpu.make_async_copy(bias_ref, bg.at[dp], own_sem.at[3]),
-    ]
-    for copy in own:
-        copy.start()
     greet(who, ("x", "y", "xy", "core"), z, depth)
+    fill_order(perm)
+    takes[0].wait()
+    reorder(xs, perm)
     sends = Sends(send_sem)
 
     def spread(stream, place_z, src, up, down, core=True):
@@ -293,11 +334,23 @@
             sends.start(src, dst, recv, who["down"], down)
         sends.start(src, dst, recv, who["core"], core)
 
-    spread(x, z, lambda: x_ref, z < depth - 1, z > 0, None)
-    sends.start(lambda: x_ref, lambda: xg.at[x, rows_of(mp)], x_sem.at[x, mp], who["x"])
+    spread(x, z, lambda: xs, z < depth - 1, z > 0, None)
+    sends.start(lambda: xs, lambda: xg.at[x, rows_of(mp)], x_sem.at[x, mp], who["x"])
+    takes[1].wait()
+    reorder(cs, perm)
+    keep = 1.0 - jnp.broadcast_to(res_ref[...], (16, length)).astype(jnp.float32)
+    rs[...] = jnp.dot(keep.astype(jnp.bfloat16), perm[...], preferred_element_type=jnp.float32)[:1]
+    own = [
+        pltpu.make_async_copy(xs, xg.at[x, rows_of(mp)], own_sem.at[0]),
+        pltpu.make_async_copy(cs.at[part(x)], cg.at[x], own_sem.at[1]),
+        pltpu.make_async_copy(rs, rg.at[x], own_sem.at[2]),
+        pltpu.make_async_copy(bias_ref, bg.at[dp], own_sem.at[3]),
+    ]
+    for copy in own:
+        copy.start()
     for name in ("x", "y", "xy"):
         sends.start(lambda: bias_ref, lambda: bg.at[dp], b_sem.at[dp], who[name])
-    sends.start(lambda: res_ref, lambda: rg.at[x], r_sem, who["x"])
+    sends.start(lambda: rs, lambda: rg.at[x], r_sem, who["x"])
     for i in range(CHUNKS):
         loads[i].wait()
 
@@ -317,7 +370,7 @@
         copy = pltpu.make_async_copy(wb.at[pl.ds(i * rows, rows), part(x)], dst(), own_sem.at[4 + i])
         copy.start()
         own.append(copy)
-    sends.start(lambda: cot_ref.at[part(1 - x)], lambda: cg.at[x], c_sem, who["x"])
+    sends.start(lambda: cs.at[part(1 - x)], lambda: cg.at[x], c_sem, who["x"])
 
     def along_z(stream, d):
         @pl.when(z >= d)
@@ -371,19 +424,6 @@
     sends.finish()
 
 
-def slot_table(owners, slot, count, blocks, slots):
-    for d in range(4):
-        count[d] = 0
-
-    def one(i, _):
-        owner = owners[i]
-        slot[i] = owner * slots + count[owner]
-        count[owner] = count[owner] + 1
-        return 0
-
-    lax.fori_loop(0, blocks, one, 0)
-
-
 def bias_rank(owners, blocks, g):
     owner = owners[blocks + g]
     rank = jnp.int32(0)
@@ -392,225 +432,245 @@
     return owner, rank
 
 
-def scan_later(a, b, length):
+def later(values):
+    return [pltpu.roll(values[-1], 1, 1)] + values[:-1]
+
+
+def scan_both(decay, fresh, source):
+    groups = len(decay)
+    held, gain = [fresh[0]], [decay[0]]
+    for v in range(1, groups):
+        held.append(fresh[v] + decay[v] * held[-1])
+        gain.append(decay[v] * gain[-1])
+    back, fall = [source[-1]], [None]
+    for v in range(groups - 2, -1, -1):
+        back.insert(0, source[v] + decay[v + 1] * back[0])
+        fall.insert(0, decay[v + 1] if fall[0] is None else decay[v + 1] * fall[0])
+    ahead = pltpu.roll(decay[0], LANES - 1, 1)
+    level, factor = held[-1], gain[-1]
+    behind, drop = back[0], fall[0] * ahead
     d = 1
-    while d < length:
-        b = b + a * pltpu.roll(b, d, 1)
-        if 2 * d < length:
-            a = a * pltpu.roll(a, d, 1)
+    while d < LANES:
+        level = level + factor * pltpu.roll(level, d, 1)
+        behind = behind + drop * pltpu.roll(behind, LANES - d, 1)
+        if 2 * d < LANES:
+            factor = factor * pltpu.roll(factor, d, 1)
+            drop = drop * pltpu.roll(drop, LANES - d, 1)
         d *= 2
-    return b
-
-
-def scan_earlier(a, b, length):
-    d = 1
-    while d < length:
-        b = b + a * pltpu.roll(b, length - d, 1)
-        if 2 * d < length:
-            a = a * pltpu.roll(a, length - d, 1)
-        d *= 2
-    return b
-
-
-def layer_kernel(
-    owners, wg, xg, cg, rg, bg,
-    h_out, gs, j_out, w_out, bgrad,
-    slot, count, wv, xv, p, joined, gb, bcol, w_sem, x_sem, o_sem,
+    carry = pltpu.roll(level, 1, 1)
+    cells = [held[v] + gain[v] * carry for v in range(groups)]
+    carry = ahead * pltpu.roll(behind, LANES - 1, 1)
+    dc = [back[v] + fall[v] * carry for v in range(groups - 1)] + [back[-1] + carry]
+    return cells, dc
+
+
+def gate_tile(p, pre_at, bias_at, keep, dh_at, h_at, joined_at, add_bias):
+    groups = len(keep)
+    lane = lax.broadcasted_iota(jnp.int32, keep[0].shape, 1)
+
+    def pre(g):
+        now = [pre_at(0, g, v) for v in range(groups)]
+        before = later([pre_at(1, g, v) for v in range(groups)])
+        before[0] = jnp.where(lane == 0, 0.0, before[0])
+        bias = bias_at(g)
+        return [n + b + bias for n, b in zip(now, before)]
+
+    cand = [jnp.tanh(v) for v in pre(0)]
+    forget = [jax.nn.sigmoid(v) for v in pre(1)]
+    gate = [jax.nn.sigmoid(v) for v in pre(2)]
+    decay = [f * k for f, k in zip(forget, keep)]
+    dh = [dh_at(v) for v in range(groups)]
+    cells, dc = scan_both(
+        decay,
+        [(1.0 - f) * z for f, z in zip(forget, cand)],
+        [d * o for d, o in zip(dh, gate)],
+    )
+    for v in range(groups):
+        h_at(v, gate[v] * cells[v])
+    past = later(cells)
+    grads = (
+        [dc[v] * (1.0 - forget[v]) * (1.0 - cand[v] * cand[v]) for v in range(groups)],
+        [
+            dc[v] * (keep[v] * past[v] - cand[v]) * (forget[v] * (1.0 - forget[v]))
+            for v in range(groups)
+        ],
+        [dh[v] * cells[v] * (gate[v] * (1.0 - gate[v])) for v in range(groups)],
+    )
+    for g in range(3):
+        narrow = [value.astype(jnp.bfloat16) for value in grads[g]]
+        wide = [value.astype(jnp.float32) for value in narrow]
+        first = jnp.where(lane == LANES - 1, 0.0, pltpu.roll(wide[0], LANES - 1, 1))
+        ahead = wide[1:] + [first]
+        total = wide[0]
+        for v in range(groups):
+            joined_at(0, g, v, narrow[v])
+            joined_at(1, g, v, ahead[v].astype(jnp.bfloat16))
+            if v:
+                total = total + wide[v]
+        add_bias(jnp.where(lane == g, jnp.sum(total, axis=1, keepdims=True), 0.0))
+
+
+def work_kernel(
+    owners, slot, source, count, wg_in, xg_in, cg_in, rg, bg,
+    gt, h_out, ig_out, bt, norm,
+    wg, wv, xv, cg, hv, p, jv, gb, bcol, bgrad, perm, ig, up_got, down_got, core_got, x_got, b_got, squares, s_got,
+    load_sem, own_sem, send_sem, y_sem, x_sem, core_sem, up_sem, down_sem, z_send, ix_sem, h_sem, b_sem, s_sem,
+    free_sem,
 ):
-    half, block_rows = wg.shape[1], wg.shape[2]
-    slots = wg.shape[0] // 4
-    streams, full, length = xg.shape
+    y, x, z, c = place()
+    who = partners(y, x, z, c)
+    slots, width, block_rows = gt.shape
+    half = width // 2
+    length = h_out.shape[1]
+    full = xv.shape[1]
+    depth = full // width // 2
     per_half = full // block_rows
     blocks = 6 * per_half
-    x = lax.rem(lax.axis_index("dp"), 2)
-    x_loads = [pltpu.make_async_copy(xg.at[s], xv.at[s], x_sem.at[s]) for s in range(2)]
-    slot_table(owners, slot, count, blocks, slots)
-    for h in range(2):
-        for g in range(3):
-
-            def fetch(k, _, h=h, g=g):
-                pltpu.make_async_copy(
-                    wg.at[slot[g * 2 * per_half + h * per_half + k]],
-                    wv.at[
-                        pl.ds((h * 3 + g) * half, half),
-                        pl.ds(pl.multiple_of(k * block_rows, block_rows), block_rows),
-                    ],
-                    w_sem,
-                ).start()
-                return 0
-
-            lax.fori_loop(0, per_half, fetch, 0)
-    for load in x_loads:
+    tile = 16
+    groups = length // LANES
+    band = wg.shape[1]
+    bands = half // band
+    got, give = 0, wg.shape[0] // 2
+    streams = (1 - x, x)
+
+    def part(index):
+        return pl.ds(pl.multiple_of(index * half, half), half)
+
+    def rows_of(place_z, core):
+        return pl.ds(pl.multiple_of((place_z * 2 + core) * width, width), width)
+
+    x_loads = [
+        pltpu.make_async_copy(xg_in.at[streams[q]], xv.at[q], load_sem.at[q]) for q in range(2)
+    ]
+    w_load = pltpu.make_async_copy(wg_in, wg, load_sem.at[2])
+    c_load = pltpu.make_async_copy(cg_in, cg, load_sem.at[3])
+    for load in (w_load, x_loads[0], c_load, x_loads[1]):
         load.start()
-    lane_of = lax.broadcasted_iota(jnp.int32, (half, 2 * half), 1)
-    row_of = lax.broadcasted_iota(jnp.int32, (half, 2 * half), 0)
+    near = (y * 2 + x, jnp.bitwise_xor(z, 1) * 2 + c)
+    far_off = (y * 2 + x, jnp.bitwise_xor(z, 2) * 2 + c)
+    barrier = pltpu.get_barrier_semaphore()
+    for device in (near, far_off):
+        pl.semaphore_signal(barrier, inc=1, device_id=device, device_id_type=MESH_ID)
+    greet(who, ("x", "y", "core"), z, depth, 2)
+
+    sends = Sends(send_sem)
+
+    fill_order(perm)
+    lane_of = lax.broadcasted_iota(jnp.int32, (half, width), 1)
+    row_of = lax.broadcasted_iota(jnp.int32, (half, width), 0)
     diagonal = lane_of == row_of + x * half
     for g in range(3):
         owner, rank = bias_rank(owners, blocks, g)
         held = bg[owner]
-        line = jnp.zeros((1, 2 * half), jnp.float32)
+        line = jnp.zeros((1, width), jnp.float32)
         for r in range(3):
             line = jnp.where(rank == r, held[r : r + 1], line)
         line = line.astype(jnp.bfloat16).astype(jnp.float32)
         column = jnp.sum(jnp.where(diagonal, line, 0.0), axis=1, keepdims=True)
         bcol[pl.ds(g * half, half), :] = jnp.broadcast_to(column, (half, LANES))
     bgrad[...] = jnp.zeros_like(bgrad)
-    pltpu.make_async_copy(wv, wv, w_sem).wait()
-    w_back = pltpu.make_async_copy(wv, w_out, o_sem.at[0])
-    w_back.start()
-    tile = 16
-    moment = lax.broadcasted_iota(jnp.int32, (tile, length), 1)
-    lane = lax.broadcasted_iota(jnp.int32, (tile, LANES), 1)
-    for s in range(2):
-        x_loads[s].wait()
-
-        def project(n, _, s=s):
+    w_load.wait()
+    for h in range(2):
+        for g in range(3):
+
+            def arrange(k, _, h=h, g=g):
+                first = slot[g * 2 * per_half + h * per_half + k] * bands
+                columns = pl.ds(pl.multiple_of(k * block_rows, block_rows), block_rows)
+                for n in range(bands):
+                    wv[pl.ds((n * 6 + h * 3 + g) * band, band), columns] = wg[first + n]
+                return 0
+
+            lax.fori_loop(0, per_half, arrange, 0)
+    pl.semaphore_signal(free_sem, inc=1, device_id=who["y"], device_id_type=MESH_ID)
+
+    def project(q, first, number):
+        def one(n, _):
             columns = pl.ds(pl.multiple_of(n * 256, 256), 256)
-            p[:, columns] = jnp.dot(wv[...], xv[s, :, columns], preferred_element_type=jnp.float32)
+            at = pl.ds(first * 6 * band, number * 6 * band)
+            p[at, columns] = jnp.dot(wv[at, :], xv[q, :, columns], preferred_element_type=jnp.float32)
             return 0
 
-        lax.fori_loop(0, length // 256, project, 0)
-        keep = 1.0 - jnp.broadcast_to(rg[s], (tile, length)).astype(jnp.float32)
-        keep = jnp.where(moment == 0, 0.0, keep)
-
-        def gates(i, _, s=s, keep=keep):
-            base = pl.multiple_of(i * tile, tile)
-
-            def pre(g):
-                now = p[pl.ds(g * half + base, tile), :]
-                before = pltpu.roll(p[pl.ds((3 + g) * half + base, tile), :], 1, 1)
-                return (
-                    now
-                    + jnp.where(moment == 0, 0.0, before)
-                    + bcol[pl.ds(g * half + base, tile), :][:, :1]
-                )
-
-            cand = jnp.tanh(pre(0))
-            forget = jax.nn.sigmoid(pre(1))
-            gate = jax.nn.sigmoid(pre(2))
-            decay = forget * keep
-            cells = scan_later(decay, (1.0 - forget) * cand, length)
-            h_out[s, pl.ds(base, tile), :] = (gate * cells).astype(jnp.bfloat16)
-            dh = cg[s, pl.ds(base, tile), :].astype(jnp.float32)
-            dc = scan_earlier(pltpu.roll(decay, length - 1, 1), dh * gate, length)
-            d_gate = dh * cells * gate * (1.0 - gate)
-            d_cand = dc * (1.0 - forget) * (1.0 - cand * cand)
-            d_forget = (
-                dc * (keep * pltpu.roll(cells, 1, 1) - cand) * forget * (1.0 - forget)
+        lax.fori_loop(0, length // 256, one, 0)
+
+    def gates(q, n):
+        lane = lax.broadcasted_iota(jnp.int32, (tile, LANES), 1)
+        keep = [
+            jnp.broadcast_to(rg[streams[q], :, pl.ds(v * LANES, LANES)], (tile, LANES))
+            for v in range(groups)
+        ]
+        keep[0] = jnp.where(lane == 0, 0.0, keep[0])
+
+        def one(i, _):
+            off = pl.multiple_of(i * tile, tile)
+            at = pl.ds(n * band + off, tile)
+
+            def row(h, g):
+                return pl.ds((n * 6 + h * 3 + g) * band + off, tile)
+
+            def h_at(v, value):
+                hv[at, pl.ds(v * LANES, LANES)] = value.astype(jnp.bfloat16)
+
+            def joined_at(h, g, v, value):
+                jv[row(h, g), pl.ds(q * length + v * LANES, LANES)] = value
+
+            def add_bias(value):
+                bgrad[at, :] += value
+
+            gate_tile(
+                p,
+                lambda h, g, v: p[row(h, g), pl.ds(v * LANES, LANES)],
+                lambda g: bcol[pl.ds(g * half + n * band + off, tile), :],
+                keep,
+                lambda v: cg[streams[q], at, pl.ds(v * LANES, LANES)].astype(jnp.float32),
+                h_at,
+                joined_at,
+                add_bias,
             )
-            total = bgrad[pl.ds(base, tile), :]
-            for g, value in enumerate((d_cand, d_forget, d_gate)):
-                value = value.astype(jnp.bfloat16)
-                wide = value.astype(jnp.float32)
-                joined[pl.ds(g * half + base, tile), pl.ds(s * length, length)] = value
-                ahead = jnp.where(moment == length - 1, 0.0, pltpu.roll(wide, length - 1, 1))
-                joined[pl.ds((3 + g) * half + base, tile), pl.ds(s * length, length)] = ahead.astype(
-                    jnp.bfloat16
-                )
-                total += jnp.where(lane == g, jnp.sum(wide, axis=1, keepdims=True), 0.0)
-            bgrad[pl.ds(base, tile), :] = total
             return 0
 
-        lax.fori_loop(0, half // tile, gates, 0)
-    j_back = pltpu.make_async_copy(joined, j_out, o_sem.at[1])
-    j_back.start()
-
-    def weight_grad(k, _):
-        rows = pl.ds(pl.multiple_of(k * block_rows, block_rows), block_rows)
+        lax.fori_loop(0, band // tile, one, 0)
+
+    def weight_grad(n):
+        at = pl.ds(n * 6 * band, 6 * band)
         both = (((1,), (1,)), ((), ()))
-        total = lax.dot_general(
-            joined[:, pl.ds(0, length)], xv[0, rows, :], both, preferred_element_type=jnp.float32
-        )
-        total += lax.dot_general(
-            joined[:, pl.ds(length, length)], xv[1, rows, :], both, preferred_element_type=jnp.float32
-        )
-        gb[k] = total.astype(jnp.bfloat16)
-        for h in range(2):
-            for g in range(3):
-                pltpu.make_async_copy(
-                    gb.at[k, pl.ds((h * 3 + g) * half, half)],
-                    gs.at[slot[g * 2 * per_half + h * per_half + k]],
-                    w_sem,
-                ).start()
-        return 0
-
-    lax.fori_loop(0, per_half, weight_grad, 0)
-    pltpu.make_async_copy(gb, gb, w_sem).wait()
-    w_back.wait()
-    j_back.wait()
-
-
-def reduce_kernel(
-    owners, gs, w_hbm, j_hbm, h_in, bgrad,
-    gt, h_out, ig_out, bt, norm,
-    wv, jv, ig, up_got, down_got, core_got, x_got, y_got, y_own, b_got, squares, s_got,
-    load_sem, own_sem, send_sem, y_sem, x_sem, core_sem, up_sem, down_sem, z_send, ix_sem, h_sem, b_sem, s_sem,
-):
-    y, x, z, c = place()
-    who = partners(y, x, z, c)
-    slots, width, block_rows = gt.shape
-    half = width // 2
-    length = h_out.shape[1]
-    full = w_hbm.shape[1]
-    depth = full // width // 2
-    rows = slots // PIECES
-    blocks = 6 * (full // block_rows)
-    tile = 16
-    streams = (1 - x, x)
-
-    def part(index):
-        return pl.ds(pl.multiple_of(index * half, half), half)
-
-    def rows_of(place_z, core):
-        return pl.ds(pl.multiple_of((place_z * 2 + core) * width, width), width)
-
-    loads = [
-        pltpu.make_async_copy(w_hbm, wv, load_sem.at[0]),
-        pltpu.make_async_copy(j_hbm, jv, load_sem.at[1]),
-    ]
-    for load in loads:
-        load.start()
-    own_loads = []
-    for q in range(2):
-        copy = pltpu.make_async_copy(
-            gs.at[pl.ds((y * 2 + streams[q]) * slots, slots)], y_own.at[q], load_sem.at[2 + q]
-        )
-        copy.start()
-        own_loads.append(copy)
-    h_own = pltpu.make_async_copy(h_in.at[x], h_out.at[part(x)], own_sem.at[0])
-    h_own.start()
-    near = (y * 2 + x, jnp.bitwise_xor(z, 1) * 2 + c)
-    far_off = (y * 2 + x, jnp.bitwise_xor(z, 2) * 2 + c)
-    barrier = pltpu.get_barrier_semaphore()
-    for device in (near, far_off):
-        pl.semaphore_signal(barrier, inc=1, device_id=device, device_id_type=MESH_ID)
-    greet(who, ("x", "y", "core"), z, depth, 2)
-
-    sends = Sends(send_sem)
+
+        def one(k, _):
+            rows = pl.ds(pl.multiple_of(k * block_rows, block_rows), block_rows)
+            total = lax.dot_general(
+                jv[at, pl.ds(0, length)], xv[0, rows, :], both, preferred_element_type=jnp.float32
+            )
+            total += lax.dot_general(
+                jv[at, pl.ds(length, length)], xv[1, rows, :], both, preferred_element_type=jnp.float32
+            )
+            total = total.astype(jnp.bfloat16)
+            for i in range(6):
+                gb[n, k * 6 + i] = total[i * band : (i + 1) * band]
+            return 0
+
+        lax.fori_loop(0, per_half, one, 0)
+
+        for q in range(2):
+
+            def pack(r, _, q=q):
+                wg[give + (n * 2 + q) * slots + r] = gb[n, source[((1 - y) * 2 + streams[q]) * slots + r]]
+                return 0
+
+            lax.fori_loop(0, slots, pack, 0)
 
     def y_send(t):
-        q, i = t // PIECES, t % PIECES
         sends.start(
-            lambda: gs.at[pl.ds(((1 - y) * 2 + streams[q]) * slots + i * rows, rows)],
-            lambda: y_got.at[q, pl.ds(i * rows, rows)],
-            y_sem.at[q, i],
+            lambda: wg.at[pl.ds(give + t * slots, slots)],
+            lambda: wg.at[pl.ds(got + t * slots, slots)],
+            y_sem.at[t],
             who["y"],
         )
-
-    y_send(0)
-    y_send(1)
-    sends.start(lambda: bgrad, lambda: b_got.at[0], b_sem.at[0], who["y"])
-    sends.start(lambda: h_in.at[1 - x], lambda: h_out.at[part(x)], h_sem, who["x"])
-    for load in loads:
-        load.wait()
 
     def input_grad(q):
         def one(k, _):
             columns = pl.ds(pl.multiple_of(k * 256, 256), 256)
-            lanes = pl.ds(pl.multiple_of(streams[q] * length, length), length)
             ig[q, columns, :] = lax.dot_general(
                 wv[:, columns],
-                jv[:, lanes],
+                jv[:, pl.ds(q * length, length)],
                 (((0,), (0,)), ((), ())),
                 preferred_element_type=jnp.float32,
             ).astype(jnp.bfloat16)
@@ -713,44 +773,38 @@
         if q == 0:
             sends.start(lambda: mine, lambda: x_got, ix_sem, who["x"])
         else:
-            copy = pltpu.make_async_copy(mine, ig_out, own_sem.at[1])
+            restore(mine, x_got, perm)
+            copy = pltpu.make_async_copy(x_got, ig_out, own_sem.at[1])
             copy.start()
             own_copies.append(copy)
 
     squares[...] = jnp.zeros_like(squares)
-    owned = []
-    for q in range(2):
-        number = jnp.int32(0)
-        for j in range(blocks):
-            number += (owners[j] == y * 2 + streams[q]).astype(jnp.int32)
-        owned.append(number)
-    own_copies = [h_own]
+    own_copies = []
 
     def own_chunk(t):
-        q, i = t // PIECES, t % PIECES
-        if i == 0:
-            own_loads[q].wait()
-        landed(y_got.at[q, pl.ds(i * rows, rows)], y_sem.at[q, i], who["y"])
-        if t + 2 < 2 * PIECES:
+        n, q = t // 2, t % 2
+        landed(wg.at[pl.ds(got + t * slots, slots)], y_sem.at[t], who["y"])
+        if t + 2 < 2 * bands:
             y_send(t + 2)
+        mine = y * 2 + streams[q]
 
         def one(r, _):
-            valid = jnp.broadcast_to(i * rows + r < owned[q], (half, block_rows))
-            total = y_own[q, i * rows + r].astype(jnp.float32) + y_got[q, i * rows + r].astype(
-                jnp.float32
-            )
+            valid = jnp.broadcast_to(r < count[mine], (band, block_rows))
+            total = gb[n, source[mine * slots + r]].astype(jnp.float32) + wg[
+                got + t * slots + r
+            ].astype(jnp.float32)
             total = jnp.where(valid, total, 0.0)
-            y_own[q, i * rows + r] = total.astype(jnp.bfloat16)
-            squares[...] += jnp.sum((total * total).reshape(half // 8, 8, block_rows), axis=0)
+            wg[got + t * slots + r] = total.astype(jnp.bfloat16)
+            squares[...] += jnp.sum((total * total).reshape(band // 8, 8, block_rows), axis=0)
             return 0
 
-        lax.fori_loop(0, rows, one, 0)
-        src = lambda: y_own.at[q, pl.ds(i * rows, rows)]
-        dst = lambda: gt.at[pl.ds(i * rows, rows), part(x)]
+        lax.fori_loop(0, slots, one, 0)
+        src = lambda: wg.at[pl.ds(got + t * slots, slots)]
+        dst = lambda: gt.at[:, pl.ds(pl.multiple_of(x * half + n * band, 16), band)]
         if q == 0:
-            sends.start(src, dst, x_sem.at[i], who["x"])
+            sends.start(src, dst, x_sem.at[n], who["x"])
         else:
-            copy = pltpu.make_async_copy(src(), dst(), own_sem.at[2 + i])
+            copy = pltpu.make_async_copy(src(), dst(), own_sem.at[2 + n])
             copy.start()
             own_copies.append(copy)
 
@@ -764,26 +818,47 @@
         each = jnp.where(counted, total * total, 0.0)
         squares[:, pl.ds(0, LANES)] += jnp.sum(each.reshape(half // 8, 8, LANES), axis=0)
 
+    x_loads[0].wait()
+    c_load.wait()
+    project(0, 0, bands)
+    for n in range(bands):
+        gates(0, n)
     input_grad(0)
+    restore(hv, cg.at[streams[0]], perm)
+    sends.start(lambda: cg.at[1 - x], lambda: h_out.at[part(x)], h_sem, who["x"])
+    x_loads[1].wait()
     ticks = 2 * (depth - 1)
-    z_tick(0)
+    chunks = 2 * bands
+    for n in range(bands):
+        project(1, n, 1)
+        if n == 0:
+            z_tick(0)
+        gates(1, n)
+        weight_grad(n)
+        if n == 0:
+            pl.semaphore_wait(free_sem, 1)
+            y_send(0)
+            y_send(1)
+    sends.start(lambda: bgrad, lambda: b_got.at[0], b_sem.at[0], who["y"])
+    z_tick(1)
     input_grad(1)
-    chunks = 2 * PIECES
-    done = 0
-    for t in range(1, ticks + 1):
-        upto = chunks * t // ticks
-        if t == ticks:
-            upto = chunks - 1
-        for i in range(done, upto):
-            own_chunk(i)
-        done = upto
-        if t == 1:
-            bias_sum()
+    restore(hv, cg.at[streams[1]], perm)
+    h_own = pltpu.make_async_copy(cg.at[x], h_out.at[part(x)], own_sem.at[0])
+    h_own.start()
+    own_copies.append(h_own)
+    own_chunk(0)
+    z_tick(2)
+    bias_sum()
+    done = 1
+    for t in range(depth - 1, ticks + 1):
         if t < ticks:
             z_tick(t)
         if t == depth - 1:
             z_last(0)
-    own_chunk(chunks - 1)
+        upto = min(chunks, max(done, 1 + (chunks - 1) * (t - depth + 2) // (ticks - depth + 2)))
+        for i in range(done, upto):
+            own_chunk(i)
+        done = upto
     total = squares[:, pl.ds(0, LANES)] + squares[:, pl.ds(LANES, LANES)]
     for step, device in enumerate((who["core"], near, far_off, who["x"], who["y"])):
         s_got[0, step] = total
@@ -797,8 +872,8 @@
         total = total + s_got[1, step]
     norm[...] = jnp.broadcast_to(jnp.sqrt(jnp.sum(total, keepdims=True)), norm.shape)
     z_last(1)
-    for i in range(PIECES):
-        landed(gt.at[pl.ds(i * rows, rows), part(1 - x)], x_sem.at[i], who["x"])
+    for n in range(bands):
+        landed(gt.at[:, pl.ds(pl.multiple_of((1 - x) * half + n * band, 16), band)], x_sem.at[n], who["x"])
     landed(h_out.at[part(1 - x)], h_sem, who["x"])
     landed(bt.at[1 - x], b_sem.at[1], who["x"])
 
@@ -858,6 +933,18 @@
             ref[...] = jnp.where(valid > 0, new, 0.0)
 
 
+def tables(owned, slots):
+    blocks = owned.shape[0]
+    per_half = blocks // 6
+    slot = owned * slots + earlier_count(owned)
+    number = jnp.arange(blocks, dtype=jnp.int32)
+    stands = lax.rem(number, per_half) * 6 + lax.rem(number // per_half, 2) * 3 + number // (2 * per_half)
+    hits = slot[None, :] == jnp.arange(4 * slots, dtype=jnp.int32)[:, None]
+    source = jnp.sum(jnp.where(hits, stands[None, :], 0), axis=1)
+    count = jnp.sum((owned[None, :] == jnp.arange(4, dtype=jnp.int32)[:, None]).astype(jnp.int32), axis=1)
+    return slot, source, count
+
+
 def paired(
     inputs, resets, owners, kernel, kernel_first, kernel_second, bias_rows, bias_first, bias_second, cotangent
 ):
@@ -879,15 +966,19 @@
             shape((4 * slots, half, block_rows), bf16),
             shape((2, full, length), bf16),
             shape((2, half, length), bf16),
-            shape((2, 1, length), jnp.int32),
+            shape((2, 1, length), f32),
             shape((4, 3, width), f32),
         ),
-        in_specs=[hbm] * 5,
+        in_specs=[hbm] * 3 + [vmem, hbm],
         out_specs=[hbm] * 5,
         scratch_shapes=[
             pltpu.VMEM((slots, width, block_rows), f32),
             pltpu.VMEM((slots, width, block_rows), bf16),
-            dma((CHUNKS,)),
+            pltpu.VMEM((length, length), bf16),
+            pltpu.VMEM((width, length), bf16),
+            pltpu.VMEM((width, length), bf16),
+            pltpu.VMEM((1, length), f32),
+            dma((CHUNKS + 2,)),
             dma((4 + CHUNKS,)),
             dma((64,)),
             dma((4, CHUNKS)),
@@ -907,35 +998,10 @@
         resets,
         bias_rows,
     )
-    h, gs, joined, wv, bgrad = pl.pallas_call(
-        layer_kernel,
-        out_shape=(
-            shape((2, half, length), bf16),
-            shape((4 * slots, half, block_rows), bf16),
-            shape((6 * half, 2 * length), bf16),
-            shape((6 * half, full), bf16),
-            shape((half, LANES), f32),
-        ),
-        in_specs=[smem, hbm, hbm, vmem, vmem, vmem],
-        out_specs=[vmem, hbm, hbm, hbm, vmem],
-        scratch_shapes=[
-            pltpu.SMEM((blocks,), jnp.int32),
-            pltpu.SMEM((4,), jnp.int32),
-            pltpu.VMEM((6 * half, full), bf16),
-            pltpu.VMEM((2, full, length), bf16),
-            pltpu.VMEM((6 * half, length), f32),
-            pltpu.VMEM((6 * half, 2 * length), bf16),
-            pltpu.VMEM((full // block_rows, 6 * half, block_rows), bf16),
-            pltpu.VMEM((3 * half, LANES), f32),
-            dma,
-            dma((2,)),
-            dma((2,)),
-        ],
-        compiler_params=pltpu.CompilerParams(vmem_limit_bytes=VMEM),
-        name="layer",
-    )(owners, wg, xg, cg, rg, bg)
+    band = half // BANDS
+    slot, source, count = tables(owners[:blocks], slots)
     gt, h_new, ig, bt, norm = pl.pallas_call(
-        reduce_kernel,
+        work_kernel,
         out_shape=(
             shape((slots, width, block_rows), bf16),
             shape((width, length), bf16),
@@ -943,26 +1009,33 @@
             shape((2, half, LANES), f32),
             shape((8, LANES), f32),
         ),
-        in_specs=[smem, hbm, hbm, hbm, hbm, vmem],
+        in_specs=[smem] * 4 + [hbm] * 3 + [vmem] * 2,
         out_specs=[hbm, hbm, hbm, vmem, vmem],
         scratch_shapes=[
+            pltpu.VMEM((4 * slots * BANDS, band, block_rows), bf16),
             pltpu.VMEM((6 * half, full), bf16),
+            pltpu.VMEM((2, full, length), bf16),
+            pltpu.VMEM((2, half, length), bf16),
+            pltpu.VMEM((half, length), bf16),
+            pltpu.VMEM((6 * half, length), f32),
             pltpu.VMEM((6 * half, 2 * length), bf16),
+            pltpu.VMEM((BANDS, blocks, band, block_rows), bf16),
+            pltpu.VMEM((3 * half, LANES), f32),
+            pltpu.VMEM((half, LANES), f32),
+            pltpu.VMEM((length, length), bf16),
             pltpu.VMEM((2, full, length), bf16),
             pltpu.VMEM((2, depth, width, length), bf16),
             pltpu.VMEM((2, depth, width, length), bf16),
             pltpu.VMEM((2, depth, width, length), bf16),
             pltpu.VMEM((width, length), bf16),
-            pltpu.VMEM((2, slots, half, block_rows), bf16),
-            pltpu.VMEM((2, slots, half, block_rows), bf16),
             pltpu.VMEM((2, half, LANES), f32),
             pltpu.VMEM((8, block_rows), f32),
             pltpu.VMEM((2, 5, 8, LANES), f32),
             dma((4,)),
-            dma((2 + PIECES,)),
+            dma((2 + BANDS,)),
             dma((64,)),
-            dma((2, PIECES)),
-            dma((PIECES,)),
+            dma((2 * BANDS,)),
+            dma((BANDS,)),
             dma((2, depth)),
             dma((2, depth)),
             dma((2, depth)),
@@ -971,12 +1044,15 @@
             dma,
             dma((2,)),
             dma((5,)),
+            pltpu.SemaphoreType.REGULAR,
         ],
         compiler_params=pltpu.CompilerParams(
             collective_id=1, has_side_effects=True, vmem_limit_bytes=VMEM
         ),
-        name="reduce",
-    )(owners, gs, wv, joined, h, bgrad)
+        name="work",
+    )(
+        owners, slot, source, count, wg.reshape(4 * slots * BANDS, band, block_rows), xg, cg, rg, bg
+    )
     per_step = 2
     block = pl.BlockSpec((per_step, width, block_rows), lambda i: (i, 0, 0))
     whole = lambda *dims: pl.BlockSpec(dims, lambda i: (0,) * len(dims))

time: 269 us -> 261 us (0.970)
  Pallas kernels: 265 us -> 253 us
  other arithmetic: 0 us -> 3.48 us
    pallas_call x2 -> x1, Pallas kernels: 154 us -> 140 us  [paired(): pl.pallas_call(work_kernel, out_shape=(shape((slots, width, block_rows),...]
    reduce_sum x0 -> x3, other arithmetic: none -> 2.8 us  [the longest x1 1.28 us: tables(): jnp.sum((owned[None, :] == jnp.arange(4, dtype=jnp.int32)[:, None]).astyp...]
where the time goes in v3:
time: 261 us; the launch traced here: 260 us
  Pallas kernels  253 us (97%)
  other arithmetic  3.48 us (1%)
  local copies, waits for them, and re-layouts  2.84 us (1%)
    pallas_call x1, Pallas kernels, paired(): pl.pallas_call(work_kernel, out_shape=(shape((slots, width, block_rows),...  140 us
    pallas_call x1, Pallas kernels, paired(): pl.pallas_call(gather_kernel, out_shape=(shape((4 * slots, half, block_ro...  90.6 us
    pallas_call x1, Pallas kernels, paired(): pl.pallas_call(adam_kernel, grid=(slots // per_step,), out_shape=(shape(k...  23.1 us

profile of v3, /device:TPU:0, one launch (start us, length us, event | category | flops | bytes accessed | tf_op | source)
XLA Modules:
  0.0 260.2 jit_solution(4185691304532069335)
XLA Ops:
  0.6 0.9 convert_reduce_fusion
  1.6 0.7 fusion.3
  2.2 0.0 copy-start.2
  2.2 0.6 select_reduce_fusion.source
  2.9 1.3 convert_reduce_fusion.1.count
  4.1 90.6 %gather.1 = (bf16[96,144,256]{2,1,0:T(8,128)(2,1)}, bf16[2,2304,1024]{2,1,0:T(8,128)(2,1)}, bf16[2,144,1024]{2,1,0:T(8,128)(2,1)}, f32[2,1,1024]{2,1,0:T(1,128)}, f32[4,3,288]{2,1,0:T(4,128)}) custom-call(f32[24,288,256]{2,1,0:T(8,128)} %w.1, bf16[288,1024]{1,0:T(8,128)(2,1)} %bitcast.10, bf16[288,1024]{1,0:T(8,128)(2,1)} %bitcast.11, s32[1,1024]{1,0:T(1,128)} %res_ref.1, ...), custom_call_target="tpu_custom_call" | custom-call | tf_op jit(solution)/shard_map/gather/pallas_call | solution.py:963
  94.7 0.0 copy-done.2
  94.7 139.5 %work.1 = (bf16[24,288,256]{2,1,0:T(8,128)(2,1)}, bf16[288,1024]{1,0:T(8,128)(2,1)}, bf16[288,1024]{1,0:T(8,128)(2,1)}, f32[2,144,128]{2,1,0:T(8,128)}, f32[8,128]{1,0:T(8,128)}) custom-call(s32[57]{0:T(128)} %owners.3, s32[54]{0:T(128)} %copy-done.2, s32[96]{0:T(128)} %select_reduce_fusion.source, s32[4]{0:T(128)} %convert_reduce_fusion.1.count, ...), custom_call_target="tpu_custom_call" | custom-call | tf_op jit(solution)/shard_map/work/pallas_call | solution.py:1003
  234.3 0.0 copy-start.1
  234.3 0.0 copy-start
  234.3 23.1 %adam.1 = (f32[24,288,256]{2,1,0:T(8,128)}, f32[24,288,256]{2,1,0:T(8,128)}, f32[24,288,256]{2,1,0:T(8,128)}, f32[3,288]{1,0:T(4,128)}, f32[3,288]{1,0:T(4,128)}, /*index=5*/f32[3,288]{1,0:T(4,128)}) custom-call(s32[57]{0:T(128)} %owners.3, f32[8,128]{1,0:T(8,128)} %get-tuple-element.32.norm, f32[2,144,128]{2,1,0:T(8,128)} %get-tuple-element.33.bt, ...), custom_call_target="tpu_custom_call" | custom-call | tf_op jit(solution)/shard_map/adam/pallas_call | solution.py:1059
  257.4 1.2 slice.7
  258.6 0.0 copy-done.1
  258.6 0.8 copy.21
  259.4 0.0 copy-done
  259.4 0.8 copy.22
Async XLA Ops:
  2.2 92.5 %copy-start.2 = (s32[54]{0:T(128)}, s32[54]{0:T(128)S(1)}, u32[]{:S(2)}) copy-start(s32[54]{0:T(128)S(1)} %get-tuple-element.42.slot) | copy-start | bytes 652
  234.3 24.3 %copy-start.1 = (bf16[288,1024]{1,0:T(8,128)(2,1)S(1)}, bf16[288,1024]{1,0:T(8,128)(2,1)}, u32[]{:S(2)}) copy-start(bf16[288,1024]{1,0:T(8,128)(2,1)} %get-tuple-element.30) | copy-start | bytes 1769476
  234.3 25.1 %copy-start = (bf16[288,1024]{1,0:T(8,128)(2,1)S(1)}, bf16[288,1024]{1,0:T(8,128)(2,1)}, u32[]{:S(2)}) copy-start(bf16[288,1024]{1,0:T(8,128)(2,1)} %get-tuple-element.31) | copy-start | bytes 1769476

commit v4 on v3

v4 whole, which is shorter than its diff:
```python
import jax
import jax.numpy as jnp
from jax import lax
from jax.experimental import pallas as pl
from jax.experimental.pallas import tpu as pltpu
from jax.sharding import PartitionSpec as P

D = 2304
STEP = 10


def earlier_count(owned):
    number = owned.shape[0]
    places = jnp.arange(number, dtype=jnp.int32)
    earlier = (owned[:, None] == owned[None, :]) & (places[None, :] < places[:, None])
    return jnp.sum(earlier.astype(jnp.int32), axis=1)


def slot_sources(slot, count):
    places = jnp.arange(slot.shape[0], dtype=jnp.int32)
    hits = slot[None, :] == jnp.arange(count, dtype=jnp.int32)[:, None]
    source = jnp.sum(jnp.where(hits, places[None, :], 0), axis=1)
    return (source, jnp.any(hits, axis=1).astype(jnp.float32))


def shift_later(values):
    return jnp.pad(values, ((0, 0), (0, 0), (1, 0)))[:, :, :-1]


def shift_earlier(values):
    return jnp.pad(values, ((0, 0), (0, 0), (0, 1)))[:, :, 1:]


def combine(earlier, later):
    return (earlier[0] * later[0], later[0] * earlier[1] + later[1])


def pooled(preact, keeping):
    channels = preact.shape[1] // 3
    candidate = jnp.tanh(preact[:, :channels])
    forget = jax.nn.sigmoid(preact[:, channels : 2 * channels])
    output_gate = jax.nn.sigmoid(preact[:, 2 * channels :])
    decay = forget * keeping[:, None, :]
    _, cells = lax.associative_scan(combine, (decay, (1.0 - forget) * candidate), axis=2)
    return output_gate * cells


def adam_step(weights, first, second, grad, decay_rate):
    rate = (2.0 * D) ** (-0.5)
    first_new = 0.9 * first + 0.1 * grad
    second_new = 0.999 * second + 0.001 * grad * grad
    first_hat = first_new / (1.0 - 0.9**STEP)
    second_hat = second_new / (1.0 - 0.999**STEP)
    weights_new = weights - rate * (
        first_hat / (jnp.sqrt(second_hat) + 1e-08) + decay_rate * weights
    )
    return (weights_new, first_new, second_new)


def shards(
    inputs,
    resets,
    owners,
    kernel,
    kernel_first,
    kernel_second,
    bias_rows,
    bias_first,
    bias_second,
    cotangent,
):
    streams, local_width, length = inputs.shape
    slots_own, _, block_rows = kernel.shape
    block_count = owners.shape[0] - 3
    dp_size = lax.axis_size("dp")
    dp_index = lax.axis_index("dp")
    kernel_owner = owners[:block_count]
    bias_owner = owners[block_count:]
    kernel_slot = kernel_owner * slots_own + earlier_count(kernel_owner)
    bias_slot = bias_owner * 3 + earlier_count(bias_owner)
    all_kernel, all_bias = (
        lax.all_gather(kernel.astype(jnp.bfloat16), "dp", axis=0, tiled=True),
        lax.all_gather(bias_rows.astype(jnp.bfloat16), "dp", axis=0, tiled=True),
    )
    per_gate = block_count // 3
    double_width = per_gate * block_rows
    full_width = double_width // 2
    gate_cols = 3 * local_width
    arranged = (
        all_kernel[kernel_slot]
        .reshape(3, per_gate, local_width, block_rows)
        .transpose(0, 2, 1, 3)
        .reshape(gate_cols, double_width)
    )
    paired_t = jnp.concatenate([arranged[:, :full_width], arranged[:, full_width:]], axis=0)
    bias_vec = all_bias[bias_slot].astype(jnp.float32).reshape(gate_cols)
    rows = paired_t
    projected = jnp.einsum(
        "ok,skl->sol",
        rows,
        lax.all_gather(inputs, "mp", axis=1, tiled=True),
        preferred_element_type=jnp.float32,
    )
    preact = (
        projected[:, :gate_cols] + shift_later(projected[:, gate_cols:]) + bias_vec[None, :, None]
    )
    keeping = (1 - resets).astype(jnp.float32)
    result, pullback = jax.vjp(lambda values: pooled(values, keeping), preact)
    pre_grad = pullback(cotangent.astype(jnp.float32))[0].astype(jnp.bfloat16)
    joined = jnp.concatenate([pre_grad, shift_earlier(pre_grad)], axis=1)
    bias_grad = jnp.sum(pre_grad.astype(jnp.float32), axis=(0, 2)).reshape(3, local_width)
    pair_grad = jnp.einsum(
        "sol,skl->ok",
        joined,
        lax.all_gather(inputs, "mp", axis=1, tiled=True),
        preferred_element_type=jnp.float32,
    )
    rows = paired_t
    term_rows = lax.psum_scatter(
        jnp.einsum("ok,sol->ksl", rows, joined, preferred_element_type=jnp.float32),
        "mp",
        scatter_dimension=0,
        tiled=True,
    )
    input_grads = jnp.transpose(term_rows.astype(jnp.bfloat16), (1, 0, 2))
    block_grad = pair_grad.reshape(2, 3, local_width, full_width).transpose(1, 2, 0, 3)
    block_grad = (
        block_grad.reshape(3, local_width, per_gate, block_rows)
        .transpose(0, 2, 1, 3)
        .reshape(block_count, local_width, block_rows)
    )
    kernel_source, kernel_valid = slot_sources(kernel_slot, dp_size * slots_own)
    bias_source, bias_valid = slot_sources(bias_slot, dp_size * 3)
    own_kernel_valid = lax.dynamic_slice_in_dim(kernel_valid, dp_index * slots_own, slots_own)
    own_bias_valid = lax.dynamic_slice_in_dim(bias_valid, dp_index * 3, 3)
    total_kernel, total_bias = lax.psum((block_grad, bias_grad), "dp")
    own_kernel_source = lax.dynamic_slice_in_dim(kernel_source, dp_index * slots_own, slots_own)
    own_bias_source = lax.dynamic_slice_in_dim(bias_source, dp_index * 3, 3)
    own_kernel = total_kernel[own_kernel_source] * own_kernel_valid[:, None, None]
    own_bias = total_bias[own_bias_source] * own_bias_valid[:, None]
    squares = jnp.sum(own_kernel * own_kernel) + jnp.sum(own_bias * own_bias)
    grad_norm = jnp.sqrt(lax.psum(squares, ("dp", "mp")))
    factor = 1.0 / jnp.maximum(grad_norm, 1.0)
    kernel_w, kernel_m, kernel_v = adam_step(
        kernel, kernel_first, kernel_second, own_kernel * factor, 0.1
    )
    bias_w, bias_m, bias_v = adam_step(bias_rows, bias_first, bias_second, own_bias * factor, 0.0)
    kernel_mask = own_kernel_valid[:, None, None] > 0.5
    bias_mask = own_bias_valid[:, None] > 0.5
    return (
        result.astype(jnp.bfloat16),
        input_grads,
        jnp.where(kernel_mask, kernel_w, 0.0),
        jnp.where(kernel_mask, kernel_m, 0.0),
        jnp.where(kernel_mask, kernel_v, 0.0),
        jnp.where(bias_mask, bias_w, 0.0),
        jnp.where(bias_mask, bias_m, 0.0),
        jnp.where(bias_mask, bias_v, 0.0),
        grad_norm,
    )


MESH_ID = pl.DeviceIdType.MESH
LANES = 128
BANDS = 3
DEEP = 8
STAGES = 4
VMEM = 61 * 2**20


def place():
    dp, mp = lax.axis_index("dp"), lax.axis_index("mp")
    return dp // 2, lax.rem(dp, 2), mp // 2, lax.rem(mp, 2)


def partners(y, x, z, c):
    dp, mp = y * 2 + x, z * 2 + c
    return {
        "x": (y * 2 + 1 - x, mp),
        "y": ((1 - y) * 2 + x, mp),
        "xy": ((1 - y) * 2 + 1 - x, mp),
        "core": (dp, z * 2 + 1 - c),
        "up": (dp, mp + 2),
        "down": (dp, mp - 2),
    }


def greet(devices):
    barrier = pltpu.get_barrier_semaphore()
    for device in devices:
        pl.semaphore_signal(barrier, inc=1, device_id=device, device_id_type=MESH_ID)
    pl.semaphore_wait(barrier, len(devices))


class Sends:
    def __init__(self, sems):
        self.sems, self.number, self.made = sems, 0, {}

    def start(self, src, dst, recv, device, when=None):
        slot = self.number
        self.number += 1

        def build():
            return pltpu.make_async_remote_copy(
                src_ref=src(),
                dst_ref=dst(),
                send_sem=self.sems.at[slot],
                recv_sem=recv,
                device_id=device,
                device_id_type=MESH_ID,
            )

        if when is None:
            build().start()
        else:
            pl.when(when)(lambda: build().start())
        self.made[slot] = (build, when)
        return slot

    def wait(self, slots):
        for slot in slots:
            build, when = self.made.pop(slot)
            if when is None:
                build().wait_send()
            else:
                pl.when(when)(lambda build=build: build().wait_send())

    def finish(self):
        self.wait(list(self.made))


def landed(ref, sem, device):
    pltpu.make_async_remote_copy(
        src_ref=ref, dst_ref=ref, send_sem=sem, recv_sem=sem, device_id=device, device_id_type=MESH_ID
    ).wait_recv()


def fill_order(perm):
    length = perm.shape[0]
    tile = 16
    column = lax.broadcasted_iota(jnp.int32, (tile, length), 1)
    wanted = lax.rem(column, LANES) * (length // LANES) + column // LANES
    wanted = wanted - lax.broadcasted_iota(jnp.int32, (tile, length), 0)

    def one(i, _):
        at = pl.ds(pl.multiple_of(i * tile, tile), tile)
        perm[at, :] = jnp.where(wanted == i * tile, 1.0, 0.0).astype(jnp.bfloat16)
        return 0

    lax.fori_loop(0, length // tile, one, 0)


def reorder(src, dst, perm):
    def one(i, _):
        at = pl.ds(pl.multiple_of(i * 256, 256), 256)
        moved = jnp.dot(src[...], perm[:, at], preferred_element_type=jnp.float32)
        dst[:, at] = moved.astype(dst.dtype)
        return 0

    lax.fori_loop(0, perm.shape[1] // 256, one, 0)


def restore(src, dst, perm):
    def one(i, _):
        at = pl.ds(pl.multiple_of(i * 256, 256), 256)
        moved = lax.dot_general(
            src[...], perm[at, :], (((1,), (1,)), ((), ())), preferred_element_type=jnp.float32
        )
        dst[:, at] = moved.astype(dst.dtype)
        return 0

    lax.fori_loop(0, perm.shape[0] // 256, one, 0)


def bias_rank(owners, blocks, g):
    owner = owners[blocks + g]
    rank = jnp.int32(0)
    for h in range(g):
        rank += (owners[blocks + h] == owner).astype(jnp.int32)
    return owner, rank


def sigmoid(v):
    return 0.5 * jnp.tanh(0.5 * v) + 0.5


def later(values):
    return [pltpu.roll(values[-1], 1, 1)] + values[:-1]


def scan_both(decay, fresh, source):
    groups = len(decay)
    held, gain = [fresh[0]], [decay[0]]
    for v in range(1, groups):
        held.append(fresh[v] + decay[v] * held[-1])
        gain.append(decay[v] * gain[-1])
    back, fall = [source[-1]], [None]
    for v in range(groups - 2, -1, -1):
        back.insert(0, source[v] + decay[v + 1] * back[0])
        fall.insert(0, decay[v + 1] if fall[0] is None else decay[v + 1] * fall[0])
    ahead = pltpu.roll(decay[0], LANES - 1, 1)
    level, factor = held[-1], gain[-1]
    behind, drop = back[0], fall[0] * ahead
    d = 1
    while d < LANES:
        level = level + factor * pltpu.roll(level, d, 1)
        behind = behind + drop * pltpu.roll(behind, LANES - d, 1)
        if 2 * d < LANES:
            factor = factor * pltpu.roll(factor, d, 1)
            drop = drop * pltpu.roll(drop, LANES - d, 1)
        d *= 2
    carry = pltpu.roll(level, 1, 1)
    cells = [held[v] + gain[v] * carry for v in range(groups)]
    carry = ahead * pltpu.roll(behind, LANES - 1, 1)
    dc = [back[v] + fall[v] * carry for v in range(groups - 1)] + [back[-1] + carry]
    return cells, dc


def gate_tile(p, pre_at, bias_at, keep, dh_at, h_at, joined_at, add_bias):
    groups = len(keep)
    lane = lax.broadcasted_iota(jnp.int32, keep[0].shape, 1)

    def pre(g):
        now = [pre_at(0, g, v) for v in range(groups)]
        before = later([pre_at(1, g, v) for v in range(groups)])
        before[0] = jnp.where(lane == 0, 0.0, before[0])
        bias = bias_at(g)
        return [n + b + bias for n, b in zip(now, before)]

    cand = [jnp.tanh(v) for v in pre(0)]
    forget = [sigmoid(v) for v in pre(1)]
    gate = [sigmoid(v) for v in pre(2)]
    decay = [f * k for f, k in zip(forget, keep)]
    dh = [dh_at(v) for v in range(groups)]
    cells, dc = scan_both(
        decay,
        [(1.0 - f) * z for f, z in zip(forget, cand)],
        [d * o for d, o in zip(dh, gate)],
    )
    for v in range(groups):
        h_at(v, gate[v] * cells[v])
    past = later(cells)
    grads = (
        [dc[v] * (1.0 - forget[v]) * (1.0 - cand[v] * cand[v]) for v in range(groups)],
        [
            dc[v] * (keep[v] * past[v] - cand[v]) * (forget[v] * (1.0 - forget[v]))
            for v in range(groups)
        ],
        [dh[v] * cells[v] * (gate[v] * (1.0 - gate[v])) for v in range(groups)],
    )
    for g in range(3):
        narrow = [value.astype(jnp.bfloat16) for value in grads[g]]
        wide = [value.astype(jnp.float32) for value in narrow]
        first = jnp.where(lane == LANES - 1, 0.0, pltpu.roll(wide[0], LANES - 1, 1))
        ahead = wide[1:] + [first]
        total = wide[0]
        for v in range(groups):
            joined_at(0, g, v, narrow[v])
            joined_at(1, g, v, ahead[v].astype(jnp.bfloat16))
            if v:
                total = total + wide[v]
        add_bias(jnp.where(lane == g, jnp.sum(total, axis=1, keepdims=True), 0.0))


def fill_tables(owners, table, table_v, sem, blocks, slots):
    per_half = blocks // 6
    down = lax.broadcasted_iota(jnp.int32, (64, LANES), 0)
    along = lax.broadcasted_iota(jnp.int32, (64, LANES), 1)

    def spell(j, both):
        owner = owners[j]
        return jnp.where(down == j, owner, both[0]), jnp.where(along == j, owner, both[1])

    start = (jnp.full((64, LANES), -1, jnp.int32), jnp.full((64, LANES), -2, jnp.int32))
    rows, columns = lax.fori_loop(0, blocks, spell, start)
    rank = jnp.sum(jnp.where((rows == columns) & (down < along), 1, 0), axis=0, keepdims=True)
    table_v[pl.ds(0, 1), :] = columns[:1] * slots + rank
    table_v[pl.ds(1, 1), :] = jnp.sum(jnp.where(rows == along, 1, 0), axis=0, keepdims=True)
    first = pltpu.make_async_copy(table_v.at[pl.ds(0, 8)], table.at[pl.ds(0, 8)], sem.at[0])
    first.start()
    first.wait()

    def place_of(j, held):
        stands = lax.rem(j, per_half) * 6 + lax.rem(j // per_half, 2) * 3 + j // (2 * per_half)
        return jnp.where(along[:1] == table[0, j], stands, held)

    table_v[pl.ds(8, 1), :] = lax.fori_loop(0, blocks, place_of, jnp.zeros((1, LANES), jnp.int32))
    second = pltpu.make_async_copy(table_v.at[pl.ds(8, 8)], table.at[pl.ds(8, 8)], sem.at[1])
    second.start()
    second.wait()


def layer_kernel(
    owners, w_ref, x_ref, cot_ref, res_ref, bias_ref,
    gt, h_out, ig_out, bt, norm,
    table, table_v, wf, wg0, wg1, wg2, wv, xv, cg, rg, bg, hv, p, jv, gb, bcol, bgrad, perm,
    ig, up_got, down_got, core_got, x_got, b_got, squares, s_got, t_got,
    load_sem, table_sem, own_sem, send_sem, w_sem, xg_sem, c_sem, r_sem, bg_sem,
    y_sem, x_sem, core_sem, up_sem, down_sem, z_send, ix_sem, h_sem, b_sem, s_sem, t_sem, free_sem,
):
    y, x, z, c = place()
    dp, mp = y * 2 + x, z * 2 + c
    who = partners(y, x, z, c)
    slots, width, block_rows = gt.shape
    half = width // 2
    length = h_out.shape[1]
    full = xv.shape[1]
    depth = full // width // 2
    per_half = full // block_rows
    blocks = 6 * per_half
    tile = 16
    groups = length // LANES
    wg = (wg0, wg1, wg2)
    band = wg0.shape[1]
    bands = half // band
    owner_x = (1 - x, x)
    mp_peers = [(dp, lax.rem(mp + r, 2 * depth)) for r in range(1, 2 * depth)]
    dp_peers = [who["x"], who["y"], who["xy"]]

    def part(index):
        return pl.ds(pl.multiple_of(index * half, half), half)

    def rows_of(place_z, core):
        return pl.ds(pl.multiple_of((place_z * 2 + core) * width, width), width)

    def piece(n, owner):
        return wg[n].at[pl.ds(owner * slots, slots)]

    def reused(t, give):
        row = (t + (2 * bands if give else 0)) * slots
        return wg[row // (4 * slots)], row % (4 * slots)

    def reused_at(t, give):
        ref, row = reused(t, give)
        return ref.at[pl.ds(row, slots)]

    mine = xv.at[1, rows_of(z, c)]
    x_held = jv.at[pl.ds(0, width), pl.ds(0, length)]
    c_held = [jv.at[pl.ds(width + i * half, half), pl.ds(0, length)] for i in range(2)]
    x_load = pltpu.make_async_copy(x_ref, x_held, load_sem.at[0])
    c_loads = [
        pltpu.make_async_copy(cot_ref.at[part(x)], c_held[0], load_sem.at[1]),
        pltpu.make_async_copy(cot_ref.at[part(1 - x)], c_held[1], load_sem.at[2]),
    ]

    def w_load(i):
        at = pl.multiple_of((x if i % 2 == 0 else 1 - x) * half + (i // 2) * band, 16)
        return pltpu.make_async_copy(
            w_ref.at[:, pl.ds(at, band)], wf.at[i % 2], load_sem.at[3 + i % 2]
        )

    x_load.start()
    w_load(0).start()
    w_load(1).start()
    for load in c_loads:
        load.start()
    greet(mp_peers + dp_peers)
    sends = Sends(send_sem)
    fill_order(perm)
    x_load.wait()
    reorder(x_held, mine, perm)

    def slice_of(q, place_z, core):
        return xv.at[q, rows_of(place_z, core)]

    def spread(q, place_z, up, down, core):
        ref = lambda: slice_of(q, place_z, c)
        recv = xg_sem.at[q, place_z * 2 + c]
        for name, when in (("up", up), ("down", down), ("core", core)):
            if when is not False:
                sends.start(ref, ref, recv, who[name], when)

    spread(1, z, z < depth - 1, z > 0, None)
    sends.start(lambda: mine, lambda: xv.at[0, rows_of(z, c)], xg_sem.at[0, mp], who["x"])
    y_pieces, x_pieces = [], []

    def y_piece(n):
        ref = lambda: piece(n, dp)
        y_pieces.append(sends.start(ref, ref, w_sem.at[n, dp], who["y"]))

    def x_piece(n):
        x_pieces.append(
            sends.start(
                lambda: gb.at[n, pl.ds(0, slots)],
                lambda: piece(n, dp),
                w_sem.at[n, dp],
                who["x"],
            )
        )

    for i in range(2 * bands):
        n = i // 2
        w_load(i).wait()

        def cast(r, _, i=i, n=n):
            value = wf[i % 2, r].astype(jnp.bfloat16)
            if i % 2 == 0:
                wg[n][dp * slots + r] = value
            else:
                gb[n, r] = value
            return 0

        lax.fori_loop(0, slots, cast, 0)
        if i + 2 < 2 * bands:
            w_load(i + 2).start()
        if i == 0:
            y_piece(0)
    for name in ("x", "y", "xy"):
        sends.start(lambda: bias_ref, lambda: bg.at[dp], bg_sem.at[dp], who[name])
    bg[dp] = bias_ref[...]
    for load in c_loads:
        load.wait()
    reorder(c_held[0], cg.at[1], perm)
    reorder(c_held[1], hv.at[0], perm)
    keep_row = 1.0 - jnp.broadcast_to(res_ref[...], (16, length)).astype(jnp.float32)
    rg[1] = jnp.dot(keep_row.astype(jnp.bfloat16), perm[...], preferred_element_type=jnp.float32)[:1]
    sends.start(lambda: rg.at[1], lambda: rg.at[0], r_sem, who["x"])
    fill_tables(owners, table, table_v, table_sem, blocks, slots)
    for owner in (y * 2 + 1 - x, (1 - y) * 2 + x, (1 - y) * 2 + 1 - x):
        landed(bg.at[owner], bg_sem.at[owner], who["x"])
    lane_of = lax.broadcasted_iota(jnp.int32, (half, width), 1)
    row_of = lax.broadcasted_iota(jnp.int32, (half, width), 0)
    diagonal = lane_of == row_of + x * half
    for g in range(3):
        owner, rank = bias_rank(owners, blocks, g)
        held = bg[owner]
        line = jnp.zeros((1, width), jnp.float32)
        for r in range(3):
            line = jnp.where(rank == r, held[r : r + 1], line)
        line = line.astype(jnp.bfloat16).astype(jnp.float32)
        column = jnp.sum(jnp.where(diagonal, line, 0.0), axis=1, keepdims=True)
        bcol[pl.ds(g * half, half), :] = jnp.broadcast_to(column, (half, LANES))
    bgrad[...] = jnp.zeros_like(bgrad)
    squares[...] = jnp.zeros_like(squares)

    def along_z(q, d):
        for at, on, on_z, device, up in (
            (z - d, z >= d, z < depth - 1, who["down"], True),
            (z + d, z + d < depth, z > 0, who["up"], False),
        ):

            @pl.when(on)
            def _(at=at, device=device):
                landed(slice_of(q, at, c), xg_sem.at[q, at * 2 + c], device)

            further = on & on_z
            spread(q, at, further if up else False, False if up else further, on)

    def pass_on(n):
        owner = y * 2 + 1 - x
        ref = lambda: piece(n, owner)
        landed(ref(), w_sem.at[n, owner], who["x"])
        if n + 1 < bands:
            x_piece(n + 1)
        y_pieces.append(sends.start(ref, ref, w_sem.at[n, owner], who["y"]))

    def arrange(n):
        for owner in ((1 - y) * 2 + x, (1 - y) * 2 + 1 - x):
            landed(piece(n, owner), w_sem.at[n, owner], who["y"])
        for h in range(2):
            for g in range(3):

                def one(k, _, h=h, g=g):
                    columns = pl.ds(pl.multiple_of(k * block_rows, block_rows), block_rows)
                    first = table[0, g * 2 * per_half + h * per_half + k]
                    wv[pl.ds((n * 6 + h * 3 + g) * band, band), columns] = wg[n][first]
                    return 0

                lax.fori_loop(0, per_half, one, 0)

    def from_core(q):
        for k in range(depth):
            landed(slice_of(q, k, 1 - c), xg_sem.at[q, k * 2 + 1 - c], who["core"])

    def project(q, first, number):
        def one(n, _):
            columns = pl.ds(pl.multiple_of(n * 256, 256), 256)
            at = pl.ds(first * 6 * band, number * 6 * band)
            p[at, columns] = jnp.dot(wv[at, :], xv[q, :, columns], preferred_element_type=jnp.float32)
            return 0

        lax.fori_loop(0, length // 256, one, 0)

    def gates(q, n):
        lane = lax.broadcasted_iota(jnp.int32, (tile, LANES), 1)
        keep = [
            jnp.broadcast_to(rg[q, :, pl.ds(v * LANES, LANES)], (tile, LANES))
            for v in range(groups)
        ]
        keep[0] = jnp.where(lane == 0, 0.0, keep[0])

        def one(i, _):
            off = pl.multiple_of(i * tile, tile)
            at = pl.ds(n * band + off, tile)

            def row(h, g):
                return pl.ds((n * 6 + h * 3 + g) * band + off, tile)

            def h_at(v, value):
                hv[q, at, pl.ds(v * LANES, LANES)] = value.astype(jnp.bfloat16)

            def joined_at(h, g, v, value):
                jv[row(h, g), pl.ds(q * length + v * LANES, LANES)] = value

            def add_bias(value):
                bgrad[at, :] += value

            gate_tile(
                p,
                lambda h, g, v: p[row(h, g), pl.ds(v * LANES, LANES)],
                lambda g: bcol[pl.ds(g * half + n * band + off, tile), :],
                keep,
                lambda v: cg[q, at, pl.ds(v * LANES, LANES)].astype(jnp.float32),
                h_at,
                joined_at,
                add_bias,
            )
            return 0

        lax.fori_loop(0, band // tile, one, 0)

    def weight_grad(n):
        at = pl.ds(n * 6 * band, 6 * band)
        both = (((1,), (1,)), ((), ()))

        def one(k, _):
            rows = pl.ds(pl.multiple_of(k * block_rows, block_rows), block_rows)
            total = lax.dot_general(
                jv[at, pl.ds(0, length)], xv[0, rows, :], both, preferred_element_type=jnp.float32
            )
            total += lax.dot_general(
                jv[at, pl.ds(length, length)], xv[1, rows, :], both, preferred_element_type=jnp.float32
            )
            total = total.astype(jnp.bfloat16)
            for i in range(6):
                gb[n, k * 6 + i] = total[i * band : (i + 1) * band]
            return 0

        lax.fori_loop(0, per_half, one, 0)

        for q in range(2):

            def pack(r, _, q=q):
                ref, row = reused(n * 2 + q, True)
                ref[row + r] = gb[n, table[8, ((1 - y) * 2 + owner_x[q]) * slots + r]]
                return 0

            lax.fori_loop(0, slots, pack, 0)

    def y_send(t):
        sends.start(
            lambda: reused_at(t, True),
            lambda: reused_at(t, False),
            y_sem.at[t],
            who["y"],
        )

    def input_grad(q):
        def one(k, _):
            columns = pl.ds(pl.multiple_of(k * 256, 256), 256)
            ig[q, columns, :] = lax.dot_general(
                wv[:, columns],
                jv[:, pl.ds(q * length, length)],
                (((0,), (0,)), ((), ())),
                preferred_element_type=jnp.float32,
            ).astype(jnp.bfloat16)
            return 0

        lax.fori_loop(0, full // 256, one, 0)
        for k in range(depth):
            sends.start(
                lambda k=k: ig.at[q, rows_of(k, 1 - c)],
                lambda k=k: core_got.at[q, k],
                core_sem.at[q, k],
                who["core"],
            )

    def add_tiles(refs):
        def one(i, _):
            at = pl.ds(pl.multiple_of(i * tile, tile), tile)
            total = refs[0][at, :].astype(jnp.float32)
            for ref in refs[1:]:
                total += ref[at, :].astype(jnp.float32)
            refs[0][at, :] = total.astype(jnp.bfloat16)
            return 0

        lax.fori_loop(0, width // tile, one, 0)

    def z_send_of(q, dest, got, recv, device, sem):
        return pltpu.make_async_remote_copy(
            src_ref=ig.at[q, rows_of(dest, c)],
            dst_ref=got.at[q, dest],
            send_sem=sem,
            recv_sem=recv.at[q, dest],
            device_id=device,
            device_id_type=MESH_ID,
        )

    mid = depth // 2 - 1
    up_items = [(0, d) for d in range(depth - 1, 0, -1) if d != mid]
    up_items += [(1, d) for d in range(depth - 1, 0, -1)]
    down_items = [(0, d) for d in range(depth - 1) if d != mid]
    down_items += [(1, d) for d in range(depth - 1)]

    def z_tick(t):
        for index, (items, after, got, recv, source, target) in enumerate(
            (
                (up_items, z, up_got, up_sem, who["down"], who["up"]),
                (down_items, depth - 1 - z, down_got, down_sem, who["up"], who["down"]),
            )
        ):
            item = t - after
            q = jnp.int32(0)
            dest = jnp.int32(0)
            earlier = jnp.int32(0)
            on = item < 0
            for i, (q_of, dest_of) in enumerate(items):
                goes = z < dest_of if index == 0 else z > dest_of
                q = jnp.where(item == i, q_of, q)
                dest = jnp.where(item == i, dest_of, dest)
                earlier += (goes & (item > i)).astype(jnp.int32)
                on = (on & (item != i)) | (goes & (item == i))
            on = on & (item >= 0) & (item < len(items))

            @pl.when(on)
            def _(index=index, after=after, got=got, recv=recv, source=source, target=target, q=q, dest=dest, earlier=earlier):
                landed(core_got.at[q, dest], core_sem.at[q, dest], who["core"])
                mine = ig.at[q, rows_of(dest, c)]

                @pl.when(after == 0)
                def _():
                    add_tiles((mine, core_got.at[q, dest]))

                @pl.when(after > 0)
                def _():
                    landed(got.at[q, dest], recv.at[q, dest], source)
                    add_tiles((mine, core_got.at[q, dest], got.at[q, dest]))

                send = z_send_of(q, dest, got, recv, target, z_send.at[index, lax.rem(earlier, 2)])

                @pl.when(earlier > 1)
                def _():
                    send.wait_send()

                send.start()

    def x_first():
        mine = ig.at[0, rows_of(mid, c)]
        landed(core_got.at[0, mid], core_sem.at[0, mid], who["core"])
        add_tiles((mine, core_got.at[0, mid]))
        sends.start(lambda: mine, lambda: up_got.at[0, mid], up_sem.at[0, mid], who["x"])

    def x_first_got():
        landed(up_got.at[0, mid], up_sem.at[0, mid], who["x"])
        add_tiles((ig.at[1, rows_of(mid, c)], up_got.at[0, mid]))

    def z_last(q):
        mine = ig.at[q, rows_of(z, c)]
        core = core_got.at[q, z]

        def joint(when, extra, above, below):
            @pl.when(when)
            def _():
                landed(core, core_sem.at[q, z], who["core"])
                refs = (mine, core)
                if extra:
                    landed(x_got, ix_sem, who["x"])
                    refs += (x_got,)
                if below:
                    landed(up_got.at[q, z], up_sem.at[q, z], who["down"])
                    refs += (up_got.at[q, z],)
                if above:
                    landed(down_got.at[q, z], down_sem.at[q, z], who["up"])
                    refs += (down_got.at[q, z],)
                add_tiles(refs)

        extra = q == 1
        joint(z == 0, extra, True, False)
        joint(z == depth - 1, extra, False, True)
        joint((z > 0) & (z < depth - 1) & (z != mid), extra, True, True)
        if q == 1:
            joint(z == mid, False, True, True)
            restore(mine, x_got, perm)
            copy = pltpu.make_async_copy(x_got, ig_out, own_sem.at[1])
            copy.start()
            own_copies.append(copy)
        else:
            sends.start(lambda: mine, lambda: x_got, ix_sem, who["x"], z != mid)

    own_copies = []

    def own_chunk(t):
        n, q = t // 2, t % 2
        landed(reused_at(t, False), y_sem.at[t], who["y"])
        ref, row = reused(t, False)
        if t + 2 < 2 * bands:
            y_send(t + 2)
        owner = y * 2 + owner_x[q]

        def one(r, _):
            valid = jnp.broadcast_to(r < table[1, owner], (band, block_rows))
            total = gb[n, table[8, owner * slots + r]].astype(jnp.float32)
            total += ref[row + r].astype(jnp.float32)
            total = jnp.where(valid, total, 0.0)
            ref[row + r] = total.astype(jnp.bfloat16)
            squares[...] += jnp.sum((total * total).reshape(band // 8, 8, block_rows), axis=0)
            return 0

        lax.fori_loop(0, slots, one, 0)
        src = lambda: reused_at(t, False)
        dst = lambda: gt.at[:, pl.ds(pl.multiple_of(x * half + n * band, 16), band)]
        if q == 0:
            sends.start(src, dst, x_sem.at[n], who["x"])
        else:
            copy = pltpu.make_async_copy(src(), dst(), own_sem.at[2 + n])
            copy.start()
            own_copies.append(copy)

    def bias_sum():
        landed(b_got.at[0], b_sem.at[0], who["y"])
        total = bgrad[...] + b_got[0]
        b_got[1] = total
        bt[x] = total
        sends.start(lambda: b_got.at[1], lambda: bt.at[x], b_sem.at[1], who["x"])
        counted = jnp.broadcast_to(y == 0, (half, LANES))
        each = jnp.where(counted, total * total, 0.0)
        squares[:, pl.ds(0, LANES)] += jnp.sum(each.reshape(half // 8, 8, LANES), axis=0)

    landed(xv.at[0, rows_of(z, c)], xg_sem.at[0, mp], who["x"])
    spread(0, z, z < depth - 1, z > 0, None)
    cot_sent = sends.start(lambda: hv.at[0], lambda: cg.at[0], c_sem, who["x"])
    x_piece(0)
    y_piece(1)
    for d in range(1, depth):
        along_z(0, d)
        if d == 1:
            y_piece(2)
        if d <= 2:
            pass_on(d - 1)
    along_z(1, 1)
    landed(cg.at[0], c_sem, who["x"])
    landed(rg.at[0], r_sem, who["x"])
    sends.wait([cot_sent])
    from_core(0)
    def layer_part(q, n):
        project(q, n, 1)
        gates(q, n)

    def give_part(n):
        weight_grad(n)
        if n == 0:
            pl.semaphore_wait(free_sem, 1)
            y_send(0)
            y_send(1)

    chunks = 2 * bands
    ticks = 2 * depth - 3
    arrange(0)
    layer_part(0, 0)
    pass_on(2)
    along_z(1, 2)
    arrange(1)
    layer_part(0, 1)
    along_z(1, 3)
    arrange(2)
    sends.wait(y_pieces + x_pieces)
    pl.semaphore_signal(free_sem, inc=1, device_id=who["y"], device_id_type=MESH_ID)
    from_core(1)
    layer_part(1, 0)
    give_part(0)
    layer_part(0, 2)
    input_grad(0)
    project(1, 1, 1)
    x_first()
    z_tick(0)
    gates(1, 1)
    give_part(1)
    z_tick(1)
    layer_part(1, 2)
    give_part(2)
    sends.start(lambda: bgrad, lambda: b_got.at[0], b_sem.at[0], who["y"])
    own_chunk(0)
    input_grad(1)
    x_first_got()
    z_tick(2)
    for q in (0, 1):
        restore(hv.at[q], cg.at[q], perm)
    sends.start(lambda: cg.at[0], lambda: h_out.at[part(x)], h_sem, who["x"])
    h_own = pltpu.make_async_copy(cg.at[1], h_out.at[part(x)], own_sem.at[0])
    h_own.start()
    own_copies.append(h_own)
    bias_sum()
    own_chunk(1)
    own_chunk(2)
    z_last(0)
    for t in range(depth - 1, ticks):
        z_tick(t)
        own_chunk(t)
    for t in range(ticks, chunks):
        own_chunk(t)
    total = squares[:, pl.ds(0, LANES)] + squares[:, pl.ds(LANES, LANES)]
    s_got[mp] = total
    for device in mp_peers:
        sends.start(lambda: s_got.at[mp], lambda: s_got.at[mp], s_sem.at[mp], device)
    for device in mp_peers:
        landed(s_got.at[device[1]], s_sem.at[device[1]], device)
    total = s_got[0]
    for k in range(1, 2 * depth):
        total = total + s_got[k]
    t_got[dp] = total
    for device in dp_peers:
        sends.start(lambda: t_got.at[dp], lambda: t_got.at[dp], t_sem.at[dp], device)
    z_last(1)
    for device in dp_peers:
        landed(t_got.at[device[0]], t_sem.at[device[0]], device)
    total = t_got[0]
    for k in range(1, 4):
        total = total + t_got[k]
    norm[...] = jnp.broadcast_to(jnp.sqrt(jnp.sum(total, keepdims=True)), norm.shape)
    for n in range(bands):
        landed(gt.at[:, pl.ds(pl.multiple_of((1 - x) * half + n * band, 16), band)], x_sem.at[n], who["x"])
    landed(h_out.at[part(1 - x)], h_sem, who["x"])
    landed(bt.at[1 - x], b_sem.at[1], who["x"])

    @pl.when(z < depth - 1)
    def _():
        for k in range(2):
            z_send_of(1, z + 1, up_got, up_sem, who["up"], z_send.at[0, k]).wait_send()

    @pl.when(z > 0)
    def _():
        for k in range(2):
            z_send_of(1, z - 1, down_got, down_sem, who["down"], z_send.at[1, k]).wait_send()

    for copy in own_copies:
        copy.wait()
    sends.finish()


def adam_turn(weights, first, second, grad, decay_rate):
    rate = (2.0 * D) ** (-0.5)
    first_new = 0.9 * first + 0.1 * grad
    second_new = 0.999 * second + (0.001 * grad) * grad
    second_hat = second_new * (1.0 / (1.0 - 0.999**STEP))
    root = second_hat * lax.rsqrt(jnp.maximum(second_hat, 1e-37)) + 1e-08
    turn = pl.reciprocal(root, approx=True)
    turn = turn * (2.0 - root * turn)
    step = (first_new * (rate / (1.0 - 0.9**STEP))) * turn
    return (weights * (1.0 - rate * decay_rate) - step, first_new, second_new)


def adam_kernel(
    owners, norm, bt, bw, bm, bv, g, w, m, v,
    w_new, m_new, v_new, bw_new, bm_new, bv_new,
    g_held, held, made, in_sem, out_sem,
):
    deep, rows, width, block_rows = g_held.shape
    stages = made.shape[1]
    turns = g.shape[0] // rows
    half = width // 2
    blocks = owners.shape[0] - 3
    me = lax.axis_index("dp")

    def taken(i):
        slot = lax.rem(i, deep)
        at = pl.ds(i * rows, rows)
        copies = [pltpu.make_async_copy(g.at[at], g_held.at[slot], in_sem.at[slot, 3])]
        for k, ref in enumerate((w, m, v)):
            copies.append(pltpu.make_async_copy(ref.at[at], held.at[k, slot], in_sem.at[slot, k]))
        return copies

    def given(i):
        slot = lax.rem(i, stages)
        at = pl.ds(i * rows, rows)
        return [
            pltpu.make_async_copy(made.at[k, slot], ref.at[at], out_sem.at[slot, k])
            for k, ref in enumerate((w_new, m_new, v_new))
        ]

    for i in range(min(deep, turns)):
        for copy in taken(jnp.int32(i)):
            copy.start()
    number = jnp.int32(0)
    for j in range(blocks):
        number += (owners[j] == me).astype(jnp.int32)
    factor = 1.0 / jnp.maximum(norm[:1, :1], 1.0)
    lane_of = lax.broadcasted_iota(jnp.int32, (half, width), 1)
    row_of = lax.broadcasted_iota(jnp.int32, (half, width), 0)
    row = lax.broadcasted_iota(jnp.int32, (3, width), 0)
    grads = jnp.zeros((3, width), jnp.float32)
    filled = jnp.zeros((3, width), jnp.int32)
    for gate in range(3):
        owner, rank = bias_rank(owners, blocks, gate)
        line = jnp.zeros((1, width), jnp.float32)
        for h in range(2):
            column = bt[h][:, gate : gate + 1]
            line += jnp.sum(
                jnp.where(lane_of == row_of + h * half, column, 0.0), axis=0, keepdims=True
            )
        here = (row == rank) & jnp.broadcast_to(owner == me, (3, width))
        grads = jnp.where(here, line, grads)
        filled = jnp.where(here, 1, filled)
    news = adam_step(bw[...], bm[...], bv[...], grads * factor, 0.0)
    for ref, new in zip((bw_new, bm_new, bv_new), news):
        ref[...] = jnp.where(filled > 0, new, 0.0)

    def turn(i, _):
        slot, stage = lax.rem(i, deep), lax.rem(i, stages)
        for copy in taken(i):
            copy.wait()

        @pl.when(i >= stages)
        def _():
            for copy in given(i - stages):
                copy.wait()

        for r in range(rows):
            grad = g_held[slot, r].astype(jnp.float32) * factor
            valid = jnp.broadcast_to(i * rows + r < number, (width, block_rows))
            news = adam_turn(held[0, slot, r], held[1, slot, r], held[2, slot, r], grad, 0.1)
            for k, new in enumerate(news):
                made[k, stage, r] = jnp.where(valid, new, 0.0)
        for copy in given(i):
            copy.start()

        @pl.when(i + deep < turns)
        def _():
            for copy in taken(i + deep):
                copy.start()

        return 0

    lax.fori_loop(0, turns, turn, 0)
    for i in range(max(0, turns - stages), turns):
        for copy in given(jnp.int32(i)):
            copy.wait()


def paired(
    inputs, resets, owners, kernel, kernel_first, kernel_second, bias_rows, bias_first, bias_second, cotangent
):
    _, width, length = inputs.shape
    slots, _, block_rows = kernel.shape
    blocks = owners.shape[0] - 3
    full = width * lax.axis_size("mp")
    depth = lax.axis_size("mp") // 2
    half = width // 2
    bf16, f32 = jnp.bfloat16, jnp.float32
    shape = jax.ShapeDtypeStruct
    hbm = pl.BlockSpec(memory_space=pltpu.MemorySpace.HBM)
    vmem = pl.BlockSpec(memory_space=pltpu.VMEM)
    smem = pl.BlockSpec(memory_space=pltpu.SMEM)
    dma = pltpu.SemaphoreType.DMA
    band = half // BANDS
    gt, h_new, ig, bt, norm = pl.pallas_call(
        layer_kernel,
        out_shape=(
            shape((slots, width, block_rows), bf16),
            shape((width, length), bf16),
            shape((width, length), bf16),
            shape((2, half, LANES), f32),
            shape((8, LANES), f32),
        ),
        in_specs=[smem] + [hbm] * 3 + [vmem] * 2,
        out_specs=[hbm, hbm, hbm, vmem, vmem],
        scratch_shapes=[
            pltpu.SMEM((16, LANES), jnp.int32),
            pltpu.VMEM((16, LANES), jnp.int32),
            pltpu.VMEM((2, slots, band, block_rows), f32),
            pltpu.VMEM((4 * slots, band, block_rows), bf16),
            pltpu.VMEM((4 * slots, band, block_rows), bf16),
            pltpu.VMEM((4 * slots, band, block_rows), bf16),
            pltpu.VMEM((6 * half, full), bf16),
            pltpu.VMEM((2, full, length), bf16),
            pltpu.VMEM((2, half, length), bf16),
            pltpu.VMEM((2, 1, length), f32),
            pltpu.VMEM((4, 3, width), f32),
            pltpu.VMEM((2, half, length), bf16),
            pltpu.VMEM((6 * half, length), f32),
            pltpu.VMEM((6 * half, 2 * length), bf16),
            pltpu.VMEM((BANDS, blocks, band, block_rows), bf16),
            pltpu.VMEM((3 * half, LANES), f32),
            pltpu.VMEM((half, LANES), f32),
            pltpu.VMEM((length, length), bf16),
            pltpu.VMEM((2, full, length), bf16),
            pltpu.VMEM((2, depth, width, length), bf16),
            pltpu.VMEM((2, depth, width, length), bf16),
            pltpu.VMEM((2, depth, width, length), bf16),
            pltpu.VMEM((width, length), bf16),
            pltpu.VMEM((2, half, LANES), f32),
            pltpu.VMEM((8, block_rows), f32),
            pltpu.VMEM((2 * depth, 8, LANES), f32),
            pltpu.VMEM((4, 8, LANES), f32),
            dma((5,)),
            dma((2,)),
            dma((2 + BANDS,)),
            dma((96,)),
            dma((BANDS, 4)),
            dma((2, 2 * depth)),
            dma,
            dma,
            dma((4,)),
            dma((2 * BANDS,)),
            dma((BANDS,)),
            dma((2, depth)),
            dma((2, depth)),
            dma((2, depth)),
            dma((2, 2)),
            dma,
            dma,
            dma((2,)),
            dma((2 * depth,)),
            dma((4,)),
            pltpu.SemaphoreType.REGULAR,
        ],
        compiler_params=pltpu.CompilerParams(
            collective_id=0, has_side_effects=True, vmem_limit_bytes=VMEM
        ),
        name="layer",
    )(
        owners,
        kernel,
        inputs.reshape(width, length),
        cotangent.reshape(width, length),
        resets,
        bias_rows,
    )
    rows = 1
    news = pl.pallas_call(
        adam_kernel,
        out_shape=(shape(kernel.shape, f32),) * 3 + (shape(bias_rows.shape, f32),) * 3,
        in_specs=[smem] + [vmem] * 5 + [hbm] * 4,
        out_specs=[hbm] * 3 + [vmem] * 3,
        scratch_shapes=[
            pltpu.VMEM((DEEP, rows, width, block_rows), bf16),
            pltpu.VMEM((3, DEEP, rows, width, block_rows), f32),
            pltpu.VMEM((3, STAGES, rows, width, block_rows), f32),
            dma((DEEP, 4)),
            dma((STAGES, 3)),
        ],
        compiler_params=pltpu.CompilerParams(vmem_limit_bytes=VMEM),
        name="adam",
    )(owners, norm, bt, bias_rows, bias_first, bias_second, gt, kernel, kernel_first, kernel_second)
    kernel_w, kernel_m, kernel_v, bias_w, bias_m, bias_v = news
    return (h_new[None], ig[None], kernel_w, kernel_m, kernel_v, bias_w, bias_m, bias_v, norm[0, 0])


def solution(mesh):
    placed = (
        P("dp", "mp", None),
        P("dp", None),
        P(),
        P("dp", "mp", None),
        P("dp", "mp", None),
        P("dp", "mp", None),
        P("dp", "mp"),
        P("dp", "mp"),
        P("dp", "mp"),
        P("dp", "mp", None),
    )
    fits = mesh.shape["dp"] == 4 and mesh.shape["mp"] == 8
    return jax.shard_map(
        paired if fits else shards,
        mesh=mesh,
        in_specs=placed,
        out_specs=(
            P("dp", "mp", None),
            P("dp", "mp", None),
            P("dp", "mp", None),
            P("dp", "mp", None),
            P("dp", "mp", None),
            P("dp", "mp"),
            P("dp", "mp"),
            P("dp", "mp"),
            P(),
        ),
        check_vma=False,
    )
```

time: 261 us -> 225 us (0.86)
  Pallas kernels: 253 us -> 221 us
  other arithmetic: 3.48 us -> 0 us
    pallas_call x3 -> x2, Pallas kernels: 253 us -> 221 us  [the longest x1 203 us: paired(): pl.pallas_call(layer_kernel, out_shape=(shape((slots, width, block_rows),...]
    reduce_sum x3 -> x0, other arithmetic: 2.8 us -> none  [the longest x1 1.28 us: tables(): jnp.sum((owned[None, :] == jnp.arange(4, dtype=jnp.int32)[:, None]).astyp...]
where the time goes in v4:
time: 225 us; the launch traced here: 224 us
  Pallas kernels  221 us (98%)
  local copies, waits for them, and re-layouts  2.83 us (1%)
    pallas_call x1, Pallas kernels, paired(): pl.pallas_call(layer_kernel, out_shape=(shape((slots, width, block_rows),...  203 us
    pallas_call x1, Pallas kernels, paired(): pl.pallas_call(adam_kernel, out_shape=(shape(kernel.shape, f32),) * 3 + (...  17.8 us

profile of v4, /device:TPU:0, one launch (start us, length us, event | category | flops | bytes accessed | tf_op | source)
XLA Modules:
  0.0 224.3 jit_solution(6478344446540642651)
XLA Ops:
  0.6 203.0 %layer.1 = (bf16[24,288,256]{2,1,0:T(8,128)(2,1)}, bf16[288,1024]{1,0:T(8,128)(2,1)}, bf16[288,1024]{1,0:T(8,128)(2,1)}, f32[2,144,128]{2,1,0:T(8,128)}, f32[8,128]{1,0:T(8,128)}) custom-call(s32[57]{0:T(128)} %owners.3, f32[24,288,256]{2,1,0:T(8,128)} %w.1, bf16[288,1024]{1,0:T(8,128)(2,1)} %bitcast.5, bf16[288,1024]{1,0:T(8,128)(2,1)} %bitcast.6, ...), custom_call_target="tpu_custom_call" | custom-call | tf_op jit(solution)/shard_map/layer/pallas_call | solution.py:1055
  203.6 0.0 copy-start.1
  203.6 0.0 copy-start
  203.6 17.8 %adam.1 = (f32[24,288,256]{2,1,0:T(8,128)}, f32[24,288,256]{2,1,0:T(8,128)}, f32[24,288,256]{2,1,0:T(8,128)}, f32[3,288]{1,0:T(4,128)}, f32[3,288]{1,0:T(4,128)}, /*index=5*/f32[3,288]{1,0:T(4,128)}) custom-call(s32[57]{0:T(128)} %owners.3, f32[8,128]{1,0:T(8,128)} %get-tuple-element.22.norm, f32[2,144,128]{2,1,0:T(8,128)} %get-tuple-element.23.bt, ...), custom_call_target="tpu_custom_call" | custom-call | tf_op jit(solution)/shard_map/adam/pallas_call | solution.py:1129
  221.5 1.2 slice.3
  222.7 0.0 copy-done.1
  222.7 0.8 copy.21
  223.5 0.0 copy-done
  223.5 0.8 copy.22
Async XLA Ops:
  203.6 19.1 %copy-start.1 = (bf16[288,1024]{1,0:T(8,128)(2,1)S(1)}, bf16[288,1024]{1,0:T(8,128)(2,1)}, u32[]{:S(2)}) copy-start(bf16[288,1024]{1,0:T(8,128)(2,1)} %get-tuple-element.20) | copy-start | bytes 1769476
  203.6 19.9 %copy-start = (bf16[288,1024]{1,0:T(8,128)(2,1)S(1)}, bf16[288,1024]{1,0:T(8,128)(2,1)}, u32[]{:S(2)}) copy-start(bf16[288,1024]{1,0:T(8,128)(2,1)} %get-tuple-element.21) | copy-start | bytes 1769476

commit v5 on v4

--- a/solution.py
+++ b/solution.py
@@ -163,6 +163,8 @@
 MESH_ID = pl.DeviceIdType.MESH
 LANES = 128
 BANDS = 3
+IM = 768
+IN = 512
 DEEP = 8
 STAGES = 4
 VMEM = 61 * 2**20
@@ -316,7 +318,7 @@
     return cells, dc
 
 
-def gate_tile(p, pre_at, bias_at, keep, dh_at, h_at, joined_at, add_bias):
+def gate_tile(pre_at, bias_at, keep, dh_at, h_at, joined_at, add_bias):
     groups = len(keep)
     lane = lax.broadcasted_iota(jnp.int32, keep[0].shape, 1)
 
@@ -572,52 +574,47 @@
         for k in range(depth):
             landed(slice_of(q, k, 1 - c), xg_sem.at[q, k * 2 + 1 - c], who["core"])
 
-    def project(q, first, number):
-        def one(n, _):
-            columns = pl.ds(pl.multiple_of(n * 256, 256), 256)
-            at = pl.ds(first * 6 * band, number * 6 * band)
-            p[at, columns] = jnp.dot(wv[at, :], xv[q, :, columns], preferred_element_type=jnp.float32)
+    def project(q, n):
+        rows = pl.ds(n * 6 * band, 6 * band)
+
+        def one(i, _):
+            columns = pl.ds(pl.multiple_of(i * 256, 256), 256)
+            p[:, columns] = jnp.dot(wv[rows, :], xv[q, :, columns], preferred_element_type=jnp.float32)
             return 0
 
         lax.fori_loop(0, length // 256, one, 0)
 
     def gates(q, n):
-        lane = lax.broadcasted_iota(jnp.int32, (tile, LANES), 1)
+        lane = lax.broadcasted_iota(jnp.int32, (band, LANES), 1)
         keep = [
-            jnp.broadcast_to(rg[q, :, pl.ds(v * LANES, LANES)], (tile, LANES))
+            jnp.broadcast_to(rg[q, :, pl.ds(v * LANES, LANES)], (band, LANES))
             for v in range(groups)
         ]
         keep[0] = jnp.where(lane == 0, 0.0, keep[0])
 
-        def one(i, _):
-            off = pl.multiple_of(i * tile, tile)
-            at = pl.ds(n * band + off, tile)
-
-            def row(h, g):
-                return pl.ds((n * 6 + h * 3 + g) * band + off, tile)
-
-            def h_at(v, value):
-                hv[q, at, pl.ds(v * LANES, LANES)] = value.astype(jnp.bfloat16)
-
-            def joined_at(h, g, v, value):
-                jv[row(h, g), pl.ds(q * length + v * LANES, LANES)] = value
-
-            def add_bias(value):
-                bgrad[at, :] += value
-
-            gate_tile(
-                p,
-                lambda h, g, v: p[row(h, g), pl.ds(v * LANES, LANES)],
-                lambda g: bcol[pl.ds(g * half + n * band + off, tile), :],
-                keep,
-                lambda v: cg[q, at, pl.ds(v * LANES, LANES)].astype(jnp.float32),
-                h_at,
-                joined_at,
-                add_bias,
-            )
-            return 0
-
-        lax.fori_loop(0, band // tile, one, 0)
+        at = pl.ds(n * band, band)
+
+        def row(h, g):
+            return pl.ds((n * 6 + h * 3 + g) * band, band)
+
+        def h_at(v, value):
+            hv[q, at, pl.ds(v * LANES, LANES)] = value.astype(jnp.bfloat16)
+
+        def joined_at(h, g, v, value):
+            jv[row(h, g), pl.ds(q * length + v * LANES, LANES)] = value
+
+        def add_bias(value):
+            bgrad[at, :] += value
+
+        gate_tile(
+            lambda h, g, v: p[pl.ds((h * 3 + g) * band, band), pl.ds(v * LANES, LANES)],
+            lambda g: bcol[pl.ds(g * half + n * band, band), :],
+            keep,
+            lambda v: cg[q, at, pl.ds(v * LANES, LANES)].astype(jnp.float32),
+            h_at,
+            joined_at,
+            add_bias,
+        )
 
     def weight_grad(n):
         at = pl.ds(n * 6 * band, 6 * band)
@@ -656,17 +653,18 @@
         )
 
     def input_grad(q):
-        def one(k, _):
-            columns = pl.ds(pl.multiple_of(k * 256, 256), 256)
-            ig[q, columns, :] = lax.dot_general(
+        def one(i, _):
+            columns = pl.ds(pl.multiple_of(i // (length // IN) * IM, IM), IM)
+            lanes = pl.multiple_of(lax.rem(i, length // IN) * IN, IN)
+            ig[q, columns, pl.ds(lanes, IN)] = lax.dot_general(
                 wv[:, columns],
-                jv[:, pl.ds(q * length, length)],
+                jv[:, pl.ds(q * length + lanes, IN)],
                 (((0,), (0,)), ((), ())),
                 preferred_element_type=jnp.float32,
             ).astype(jnp.bfloat16)
             return 0
 
-        lax.fori_loop(0, full // 256, one, 0)
+        lax.fori_loop(0, (full // IM) * (length // IN), one, 0)
         for k in range(depth):
             sends.start(
                 lambda k=k: ig.at[q, rows_of(k, 1 - c)],
@@ -702,7 +700,7 @@
     down_items = [(0, d) for d in range(depth - 1) if d != mid]
     down_items += [(1, d) for d in range(depth - 1)]
 
-    def z_tick(t):
+    def z_tick(t, first=True, rest=True):
         for index, (items, after, got, recv, source, target) in enumerate(
             (
                 (up_items, z, up_got, up_sem, who["down"], who["up"]),
@@ -721,6 +719,8 @@
                 earlier += (goes & (item > i)).astype(jnp.int32)
                 on = (on & (item != i)) | (goes & (item == i))
             on = on & (item >= 0) & (item < len(items))
+            if not (first and rest):
+                on = on & ((after == 0) if first else (after > 0))
 
             @pl.when(on)
             def _(index=index, after=after, got=got, recv=recv, source=source, target=target, q=q, dest=dest, earlier=earlier):
@@ -793,8 +793,8 @@
         n, q = t // 2, t % 2
         landed(reused_at(t, False), y_sem.at[t], who["y"])
         ref, row = reused(t, False)
-        if t + 2 < 2 * bands:
-            y_send(t + 2)
+        if t + 3 < 2 * bands and t != 1:
+            y_send(t + 3)
         owner = y * 2 + owner_x[q]
 
         def one(r, _):
@@ -843,7 +843,7 @@
     sends.wait([cot_sent])
     from_core(0)
     def layer_part(q, n):
-        project(q, n, 1)
+        project(q, n)
         gates(q, n)
 
     def give_part(n):
@@ -870,19 +870,23 @@
     give_part(0)
     layer_part(0, 2)
     input_grad(0)
-    project(1, 1, 1)
+    project(1, 1)
     x_first()
     z_tick(0)
     gates(1, 1)
     give_part(1)
-    z_tick(1)
+    y_send(2)
+    z_tick(1, rest=False)
     layer_part(1, 2)
+    sends.start(lambda: bgrad, lambda: b_got.at[0], b_sem.at[0], who["y"])
+    z_tick(1, first=False)
+    input_grad(1)
+    own_chunk(0)
     give_part(2)
-    sends.start(lambda: bgrad, lambda: b_got.at[0], b_sem.at[0], who["y"])
-    own_chunk(0)
-    input_grad(1)
+    y_send(4)
     x_first_got()
     z_tick(2)
+    own_chunk(1)
     for q in (0, 1):
         restore(hv.at[q], cg.at[q], perm)
     sends.start(lambda: cg.at[0], lambda: h_out.at[part(x)], h_sem, who["x"])
@@ -890,7 +894,6 @@
     h_own.start()
     own_copies.append(h_own)
     bias_sum()
-    own_chunk(1)
     own_chunk(2)
     z_last(0)
     for t in range(depth - 1, ticks):
@@ -1076,7 +1079,7 @@
             pltpu.VMEM((2, 1, length), f32),
             pltpu.VMEM((4, 3, width), f32),
             pltpu.VMEM((2, half, length), bf16),
-            pltpu.VMEM((6 * half, length), f32),
+            pltpu.VMEM((6 * band, length), f32),
             pltpu.VMEM((6 * half, 2 * length), bf16),
             pltpu.VMEM((BANDS, blocks, band, block_rows), bf16),
             pltpu.VMEM((3 * half, LANES), f32),

time: 225 us -> 215 us (0.956)
  Pallas kernels: 221 us -> 210 us
    pallas_call x1, Pallas kernels: 203 us -> 192 us  [paired(): pl.pallas_call(layer_kernel, out_shape=(shape((slots, width, block_rows),...]
where the time goes in v5:
time: 215 us; the launch traced here: 213 us
  Pallas kernels  210 us (98%)
  local copies, waits for them, and re-layouts  2.83 us (1%)
    pallas_call x1, Pallas kernels, paired(): pl.pallas_call(layer_kernel, out_shape=(shape((slots, width, block_rows),...  192 us
    pallas_call x1, Pallas kernels, paired(): pl.pallas_call(adam_kernel, out_shape=(shape(kernel.shape, f32),) * 3 + (...  17.8 us

profile of v5, /device:TPU:0, one launch (start us, length us, event | category | flops | bytes accessed | tf_op | source)
XLA Modules:
  0.0 213.1 jit_solution(11819791027302500115)
XLA Ops:
  0.6 191.8 %layer.1 = (bf16[24,288,256]{2,1,0:T(8,128)(2,1)}, bf16[288,1024]{1,0:T(8,128)(2,1)}, bf16[288,1024]{1,0:T(8,128)(2,1)}, f32[2,144,128]{2,1,0:T(8,128)}, f32[8,128]{1,0:T(8,128)}) custom-call(s32[57]{0:T(128)} %owners.3, f32[24,288,256]{2,1,0:T(8,128)} %w.1, bf16[288,1024]{1,0:T(8,128)(2,1)} %bitcast.5, bf16[288,1024]{1,0:T(8,128)(2,1)} %bitcast.6, ...), custom_call_target="tpu_custom_call" | custom-call | tf_op jit(solution)/shard_map/layer/pallas_call | solution.py:1058
  192.4 0.0 copy-start.1
  192.4 0.0 copy-start
  192.5 17.8 %adam.1 = (f32[24,288,256]{2,1,0:T(8,128)}, f32[24,288,256]{2,1,0:T(8,128)}, f32[24,288,256]{2,1,0:T(8,128)}, f32[3,288]{1,0:T(4,128)}, f32[3,288]{1,0:T(4,128)}, /*index=5*/f32[3,288]{1,0:T(4,128)}) custom-call(s32[57]{0:T(128)} %owners.3, f32[8,128]{1,0:T(8,128)} %get-tuple-element.22.norm, f32[2,144,128]{2,1,0:T(8,128)} %get-tuple-element.23.bt, ...), custom_call_target="tpu_custom_call" | custom-call | tf_op jit(solution)/shard_map/adam/pallas_call | solution.py:1132
  210.3 1.2 slice.3
  211.5 0.0 copy-done.1
  211.5 0.8 copy.21
  212.3 0.0 copy-done
  212.3 0.8 copy.22
Async XLA Ops:
  192.4 19.1 %copy-start.1 = (bf16[288,1024]{1,0:T(8,128)(2,1)S(1)}, bf16[288,1024]{1,0:T(8,128)(2,1)}, u32[]{:S(2)}) copy-start(bf16[288,1024]{1,0:T(8,128)(2,1)} %get-tuple-element.20) | copy-start | bytes 1769476
  192.4 19.9 %copy-start = (bf16[288,1024]{1,0:T(8,128)(2,1)S(1)}, bf16[288,1024]{1,0:T(8,128)(2,1)}, u32[]{:S(2)}) copy-start(bf16[288,1024]{1,0:T(8,128)(2,1)} %get-tuple-element.21) | copy-start | bytes 1769476

commit v6 on v5

--- a/solution.py
+++ b/solution.py
@@ -163,8 +163,7 @@
 MESH_ID = pl.DeviceIdType.MESH
 LANES = 128
 BANDS = 3
-IM = 768
-IN = 512
+IM = 256
 DEEP = 8
 STAGES = 4
 VMEM = 61 * 2**20
@@ -416,6 +415,7 @@
     band = wg0.shape[1]
     bands = half // band
     owner_x = (1 - x, x)
+    mid = depth // 2 - 1
     mp_peers = [(dp, lax.rem(mp + r, 2 * depth)) for r in range(1, 2 * depth)]
     dp_peers = [who["x"], who["y"], who["xy"]]
 
@@ -451,17 +451,13 @@
             w_ref.at[:, pl.ds(at, band)], wf.at[i % 2], load_sem.at[3 + i % 2]
         )
 
+    w_load(0).start()
     x_load.start()
-    w_load(0).start()
     w_load(1).start()
     for load in c_loads:
         load.start()
     greet(mp_peers + dp_peers)
     sends = Sends(send_sem)
-    fill_order(perm)
-    x_load.wait()
-    reorder(x_held, mine, perm)
-
     def slice_of(q, place_z, core):
         return xv.at[q, rows_of(place_z, core)]
 
@@ -472,8 +468,6 @@
             if when is not False:
                 sends.start(ref, ref, recv, who[name], when)
 
-    spread(1, z, z < depth - 1, z > 0, None)
-    sends.start(lambda: mine, lambda: xv.at[0, rows_of(z, c)], xg_sem.at[0, mp], who["x"])
     y_pieces, x_pieces = [], []
 
     def y_piece(n):
@@ -490,11 +484,11 @@
             )
         )
 
-    for i in range(2 * bands):
+    def take_weights(i):
         n = i // 2
         w_load(i).wait()
 
-        def cast(r, _, i=i, n=n):
+        def cast(r, _):
             value = wf[i % 2, r].astype(jnp.bfloat16)
             if i % 2 == 0:
                 wg[n][dp * slots + r] = value
@@ -505,8 +499,16 @@
         lax.fori_loop(0, slots, cast, 0)
         if i + 2 < 2 * bands:
             w_load(i + 2).start()
-        if i == 0:
-            y_piece(0)
+
+    fill_order(perm)
+    take_weights(0)
+    y_piece(0)
+    x_load.wait()
+    reorder(x_held, mine, perm)
+    spread(1, z, z < depth - 1, z > 0, None)
+    sends.start(lambda: mine, lambda: xv.at[0, rows_of(z, c)], xg_sem.at[0, mp], who["x"])
+    for i in range(1, 2 * bands):
+        take_weights(i)
     for name in ("x", "y", "xy"):
         sends.start(lambda: bias_ref, lambda: bg.at[dp], bg_sem.at[dp], who[name])
     bg[dp] = bias_ref[...]
@@ -540,6 +542,8 @@
             (z - d, z >= d, z < depth - 1, who["down"], True),
             (z + d, z + d < depth, z > 0, who["up"], False),
         ):
+            if q == 0:
+                on = on & (at != mid)
 
             @pl.when(on)
             def _(at=at, device=device):
@@ -578,11 +582,11 @@
         rows = pl.ds(n * 6 * band, 6 * band)
 
         def one(i, _):
-            columns = pl.ds(pl.multiple_of(i * 256, 256), 256)
+            columns = pl.ds(pl.multiple_of(i * 512, 512), 512)
             p[:, columns] = jnp.dot(wv[rows, :], xv[q, :, columns], preferred_element_type=jnp.float32)
             return 0
 
-        lax.fori_loop(0, length // 256, one, 0)
+        lax.fori_loop(0, length // 512, one, 0)
 
     def gates(q, n):
         lane = lax.broadcasted_iota(jnp.int32, (band, LANES), 1)
@@ -653,25 +657,26 @@
         )
 
     def input_grad(q):
-        def one(i, _):
-            columns = pl.ds(pl.multiple_of(i // (length // IN) * IM, IM), IM)
-            lanes = pl.multiple_of(lax.rem(i, length // IN) * IN, IN)
-            ig[q, columns, pl.ds(lanes, IN)] = lax.dot_general(
-                wv[:, columns],
-                jv[:, pl.ds(q * length + lanes, IN)],
+        number = full // IM
+        order = sorted(range(number), key=lambda k: min(k, number - 1 - k))
+        waiting = list(range(depth))
+        for place_of, k in enumerate(order):
+            ig[q, pl.ds(k * IM, IM), :] = lax.dot_general(
+                wv[:, pl.ds(k * IM, IM)],
+                jv[:, pl.ds(q * length, length)],
                 (((0,), (0,)), ((), ())),
                 preferred_element_type=jnp.float32,
             ).astype(jnp.bfloat16)
-            return 0
-
-        lax.fori_loop(0, (full // IM) * (length // IN), one, 0)
-        for k in range(depth):
-            sends.start(
-                lambda k=k: ig.at[q, rows_of(k, 1 - c)],
-                lambda k=k: core_got.at[q, k],
-                core_sem.at[q, k],
-                who["core"],
-            )
+            for d in list(waiting):
+                needs = set(range(2 * d * width // IM, ((2 * d + 2) * width - 1) // IM + 1))
+                if needs <= set(order[: place_of + 1]):
+                    waiting.remove(d)
+                    sends.start(
+                        lambda d=d: ig.at[q, rows_of(d, 1 - c)],
+                        lambda d=d: core_got.at[q, d],
+                        core_sem.at[q, d],
+                        who["core"],
+                    )
 
     def add_tiles(refs):
         def one(i, _):
@@ -694,7 +699,6 @@
             device_id_type=MESH_ID,
         )
 
-    mid = depth // 2 - 1
     up_items = [(0, d) for d in range(depth - 1, 0, -1) if d != mid]
     up_items += [(1, d) for d in range(depth - 1, 0, -1)]
     down_items = [(0, d) for d in range(depth - 1) if d != mid]
@@ -710,20 +714,18 @@
             item = t - after
             q = jnp.int32(0)
             dest = jnp.int32(0)
-            earlier = jnp.int32(0)
             on = item < 0
             for i, (q_of, dest_of) in enumerate(items):
                 goes = z < dest_of if index == 0 else z > dest_of
                 q = jnp.where(item == i, q_of, q)
                 dest = jnp.where(item == i, dest_of, dest)
-                earlier += (goes & (item > i)).astype(jnp.int32)
                 on = (on & (item != i)) | (goes & (item == i))
             on = on & (item >= 0) & (item < len(items))
             if not (first and rest):
                 on = on & ((after == 0) if first else (after > 0))
 
             @pl.when(on)
-            def _(index=index, after=after, got=got, recv=recv, source=source, target=target, q=q, dest=dest, earlier=earlier):
+            def _(index=index, after=after, got=got, recv=recv, source=source, target=target, q=q, dest=dest):
                 landed(core_got.at[q, dest], core_sem.at[q, dest], who["core"])
                 mine = ig.at[q, rows_of(dest, c)]
 
@@ -736,13 +738,7 @@
                     landed(got.at[q, dest], recv.at[q, dest], source)
                     add_tiles((mine, core_got.at[q, dest], got.at[q, dest]))
 
-                send = z_send_of(q, dest, got, recv, target, z_send.at[index, lax.rem(earlier, 2)])
-
-                @pl.when(earlier > 1)
-                def _():
-                    send.wait_send()
-
-                send.start()
+                z_send_of(q, dest, got, recv, target, z_send.at[index, q, dest]).start()
 
     def x_first():
         mine = ig.at[0, rows_of(mid, c)]
@@ -788,13 +784,14 @@
             sends.start(lambda: mine, lambda: x_got, ix_sem, who["x"], z != mid)
 
     own_copies = []
+    next_piece = {2: 3, 4: 5}
 
     def own_chunk(t):
         n, q = t // 2, t % 2
         landed(reused_at(t, False), y_sem.at[t], who["y"])
         ref, row = reused(t, False)
-        if t + 3 < 2 * bands and t != 1:
-            y_send(t + 3)
+        if t in next_piece:
+            y_send(next_piece[t])
         owner = y * 2 + owner_x[q]
 
         def one(r, _):
@@ -827,21 +824,32 @@
         squares[:, pl.ds(0, LANES)] += jnp.sum(each.reshape(half // 8, 8, LANES), axis=0)
 
     landed(xv.at[0, rows_of(z, c)], xg_sem.at[0, mp], who["x"])
-    spread(0, z, z < depth - 1, z > 0, None)
+    spread(0, z, (z < depth - 1) & (z != mid), (z > 0) & (z != mid), None)
     cot_sent = sends.start(lambda: hv.at[0], lambda: cg.at[0], c_sem, who["x"])
     x_piece(0)
     y_piece(1)
+    along_z(1, 1)
     for d in range(1, depth):
         along_z(0, d)
         if d == 1:
             y_piece(2)
         if d <= 2:
             pass_on(d - 1)
-    along_z(1, 1)
+            if d + 1 < depth - 1:
+                along_z(1, d + 1)
+    pass_on(2)
+    sends.start(
+        lambda: slice_of(1, mid, c),
+        lambda: slice_of(0, mid, c),
+        xg_sem.at[0, mid * 2 + c],
+        who["x"],
+        z != mid,
+    )
+    along_z(1, depth - 1)
     landed(cg.at[0], c_sem, who["x"])
     landed(rg.at[0], r_sem, who["x"])
     sends.wait([cot_sent])
-    from_core(0)
+    from_core(1)
     def layer_part(q, n):
         project(q, n)
         gates(q, n)
@@ -853,34 +861,36 @@
             y_send(0)
             y_send(1)
 
-    chunks = 2 * bands
     ticks = 2 * depth - 3
     arrange(0)
+    layer_part(1, 0)
+    arrange(1)
+    sends.wait([y_pieces[k] for k in (0, 1, 3, 4)] + x_pieces)
+    pl.semaphore_signal(free_sem, inc=1, device_id=who["y"], device_id_type=MESH_ID)
+    layer_part(1, 1)
+
+    @pl.when(z != mid)
+    def _():
+        landed(slice_of(0, mid, c), xg_sem.at[0, mid * 2 + c], who["x"])
+
+    spread(0, mid, False, False, z != mid)
+    from_core(0)
     layer_part(0, 0)
-    pass_on(2)
-    along_z(1, 2)
-    arrange(1)
+    give_part(0)
     layer_part(0, 1)
-    along_z(1, 3)
     arrange(2)
-    sends.wait(y_pieces + x_pieces)
-    pl.semaphore_signal(free_sem, inc=1, device_id=who["y"], device_id_type=MESH_ID)
-    from_core(1)
-    layer_part(1, 0)
-    give_part(0)
+    sends.wait([y_pieces[k] for k in (2, 5)])
     layer_part(0, 2)
     input_grad(0)
-    project(1, 1)
+    z_tick(0)
     x_first()
-    z_tick(0)
-    gates(1, 1)
     give_part(1)
     y_send(2)
     z_tick(1, rest=False)
     layer_part(1, 2)
     sends.start(lambda: bgrad, lambda: b_got.at[0], b_sem.at[0], who["y"])
+    input_grad(1)
     z_tick(1, first=False)
-    input_grad(1)
     own_chunk(0)
     give_part(2)
     y_send(4)
@@ -896,10 +906,12 @@
     bias_sum()
     own_chunk(2)
     z_last(0)
+    left = [4, 3, 5]
     for t in range(depth - 1, ticks):
         z_tick(t)
-        own_chunk(t)
-    for t in range(ticks, chunks):
+        if left:
+            own_chunk(left.pop(0))
+    for t in left:
         own_chunk(t)
     total = squares[:, pl.ds(0, LANES)] + squares[:, pl.ds(LANES, LANES)]
     s_got[mp] = total
@@ -925,15 +937,14 @@
     landed(h_out.at[part(1 - x)], h_sem, who["x"])
     landed(bt.at[1 - x], b_sem.at[1], who["x"])
 
-    @pl.when(z < depth - 1)
-    def _():
-        for k in range(2):
-            z_send_of(1, z + 1, up_got, up_sem, who["up"], z_send.at[0, k]).wait_send()
-
-    @pl.when(z > 0)
-    def _():
-        for k in range(2):
-            z_send_of(1, z - 1, down_got, down_sem, who["down"], z_send.at[1, k]).wait_send()
+    for index, (items, got, recv, target) in enumerate(
+        ((up_items, up_got, up_sem, who["up"]), (down_items, down_got, down_sem, who["down"]))
+    ):
+        for q, dest in items:
+
+            @pl.when(z < dest if index == 0 else z > dest)
+            def _(index=index, got=got, recv=recv, target=target, q=q, dest=dest):
+                z_send_of(q, dest, got, recv, target, z_send.at[index, q, dest]).wait_send()
 
     for copy in own_copies:
         copy.wait()
@@ -953,9 +964,9 @@
 
 
 def adam_kernel(
-    owners, norm, bt, bw, bm, bv, g, w, m, v,
-    w_new, m_new, v_new, bw_new, bm_new, bv_new,
-    g_held, held, made, in_sem, out_sem,
+    owners, norm, bt, bw, bm, bv, g, w, m, v, h_in, ig_in,
+    w_new, m_new, v_new, bw_new, bm_new, bv_new, h_out, ig_out, norm_out,
+    g_held, held, made, kept, in_sem, out_sem, pass_sem,
 ):
     deep, rows, width, block_rows = g_held.shape
     stages = made.shape[1]
@@ -983,6 +994,16 @@
     for i in range(min(deep, turns)):
         for copy in taken(jnp.int32(i)):
             copy.start()
+    come = [
+        pltpu.make_async_copy(ref, kept.at[k], pass_sem.at[k]) for k, ref in enumerate((h_in, ig_in))
+    ]
+    leave = [
+        pltpu.make_async_copy(kept.at[k], ref, pass_sem.at[2 + k])
+        for k, ref in enumerate((h_out, ig_out))
+    ]
+    for copy in come:
+        copy.start()
+    norm_out[...] = norm[:1, :1]
     number = jnp.int32(0)
     for j in range(blocks):
         number += (owners[j] == me).astype(jnp.int32)
@@ -1031,12 +1052,20 @@
             for copy in taken(i + deep):
                 copy.start()
 
+        @pl.when(i == turns // 2)
+        def _():
+            for k in range(2):
+                come[k].wait()
+                leave[k].start()
+
         return 0
 
     lax.fori_loop(0, turns, turn, 0)
     for i in range(max(0, turns - stages), turns):
         for copy in given(jnp.int32(i)):
             copy.wait()
+    for copy in leave:
+        copy.wait()
 
 
 def paired(
@@ -1108,7 +1137,7 @@
             dma((2, depth)),
             dma((2, depth)),
             dma((2, depth)),
-            dma((2, 2)),
+            dma((2, 2, depth)),
             dma,
             dma,
             dma((2,)),
@@ -1131,21 +1160,28 @@
     rows = 1
     news = pl.pallas_call(
         adam_kernel,
-        out_shape=(shape(kernel.shape, f32),) * 3 + (shape(bias_rows.shape, f32),) * 3,
-        in_specs=[smem] + [vmem] * 5 + [hbm] * 4,
-        out_specs=[hbm] * 3 + [vmem] * 3,
+        out_shape=(shape(kernel.shape, f32),) * 3
+        + (shape(bias_rows.shape, f32),) * 3
+        + (shape((width, length), bf16),) * 2
+        + (shape((1, 1), f32),),
+        in_specs=[smem] + [vmem] * 5 + [hbm] * 6,
+        out_specs=[hbm] * 3 + [vmem] * 3 + [hbm] * 2 + [vmem],
         scratch_shapes=[
             pltpu.VMEM((DEEP, rows, width, block_rows), bf16),
             pltpu.VMEM((3, DEEP, rows, width, block_rows), f32),
             pltpu.VMEM((3, STAGES, rows, width, block_rows), f32),
+            pltpu.VMEM((2, width, length), bf16),
             dma((DEEP, 4)),
             dma((STAGES, 3)),
+            dma((4,)),
         ],
         compiler_params=pltpu.CompilerParams(vmem_limit_bytes=VMEM),
         name="adam",
-    )(owners, norm, bt, bias_rows, bias_first, bias_second, gt, kernel, kernel_first, kernel_second)
-    kernel_w, kernel_m, kernel_v, bias_w, bias_m, bias_v = news
-    return (h_new[None], ig[None], kernel_w, kernel_m, kernel_v, bias_w, bias_m, bias_v, norm[0, 0])
+    )(
+        owners, norm, bt, bias_rows, bias_first, bias_second, gt, kernel, kernel_first, kernel_second, h_new, ig
+    )
+    *updated, h_last, ig_last, norm_last = news
+    return (h_last[None], ig_last[None], *updated, norm_last[0, 0])
 
 
 def solution(mesh):

time: 215 us -> 212 us (0.986)
  local copies, waits for them, and re-layouts: 2.83 us -> 0 us
where the time goes in v6:
time: 212 us; the launch traced here: 210 us
  Pallas kernels  209 us (99%)
    pallas_call x1, Pallas kernels, paired(): pl.pallas_call(layer_kernel, out_shape=(shape((slots, width, block_rows),...  190 us
    pallas_call x1, Pallas kernels, paired(): pl.pallas_call(adam_kernel, out_shape=(shape(kernel.shape, f32),) * 3 + (...  18.9 us

profile of v6, /device:TPU:0, one launch (start us, length us, event | category | flops | bytes accessed | tf_op | source)
XLA Modules:
  0.0 209.9 jit_solution(12713307572578180050)
XLA Ops:
  0.6 190.2 %layer.1 = (bf16[24,288,256]{2,1,0:T(8,128)(2,1)}, bf16[288,1024]{1,0:T(8,128)(2,1)}, bf16[288,1024]{1,0:T(8,128)(2,1)}, f32[2,144,128]{2,1,0:T(8,128)}, f32[8,128]{1,0:T(8,128)}) custom-call(s32[57]{0:T(128)} %owners.3, f32[24,288,256]{2,1,0:T(8,128)} %w.1, bf16[288,1024]{1,0:T(8,128)(2,1)} %bitcast.5, bf16[288,1024]{1,0:T(8,128)(2,1)} %bitcast.6, ...), custom_call_target="tpu_custom_call" | custom-call | tf_op jit(solution)/shard_map/layer/pallas_call | solution.py:1087
  190.9 18.9 %adam.1 = (f32[24,288,256]{2,1,0:T(8,128)}, f32[24,288,256]{2,1,0:T(8,128)}, f32[24,288,256]{2,1,0:T(8,128)}, f32[3,288]{1,0:T(4,128)}, f32[3,288]{1,0:T(4,128)}...) custom-call(s32[57]{0:T(128)} %owners.3, ...), custom_call_target="tpu_custom_call" | custom-call | tf_op jit(solution)/shard_map/adam/pallas_call | solution.py:1161

commit v7 on v6

--- a/solution.py
+++ b/solution.py
@@ -581,12 +581,7 @@
     def project(q, n):
         rows = pl.ds(n * 6 * band, 6 * band)
 
-        def one(i, _):
-            columns = pl.ds(pl.multiple_of(i * 512, 512), 512)
-            p[:, columns] = jnp.dot(wv[rows, :], xv[q, :, columns], preferred_element_type=jnp.float32)
-            return 0
-
-        lax.fori_loop(0, length // 512, one, 0)
+        p[...] = jnp.dot(wv[rows, :], xv[q], preferred_element_type=jnp.float32)
 
     def gates(q, n):
         lane = lax.broadcasted_iota(jnp.int32, (band, LANES), 1)
@@ -894,8 +889,10 @@
     own_chunk(0)
     give_part(2)
     y_send(4)
+    z_tick(2, rest=False)
     x_first_got()
-    z_tick(2)
+    z_tick(2, first=False)
+    z_tick(3, rest=False)
     own_chunk(1)
     for q in (0, 1):
         restore(hv.at[q], cg.at[q], perm)
@@ -908,7 +905,7 @@
     z_last(0)
     left = [4, 3, 5]
     for t in range(depth - 1, ticks):
-        z_tick(t)
+        z_tick(t, first=t > depth - 1)
         if left:
             own_chunk(left.pop(0))
     for t in left:

time: 212 us -> 211 us (level)
  no operation moved by 1% of the time
where the time goes in v7:
time: 211 us; the launch traced here: 209 us
  Pallas kernels  209 us (99%)
    pallas_call x1, Pallas kernels, paired(): pl.pallas_call(layer_kernel, out_shape=(shape((slots, width, block_rows),...  190 us
    pallas_call x1, Pallas kernels, paired(): pl.pallas_call(adam_kernel, out_shape=(shape(kernel.shape, f32),) * 3 + (...  18.9 us

profile of v7, /device:TPU:0, one launch (start us, length us, event | category | flops | bytes accessed | tf_op | source)
XLA Modules:
  0.0 209.4 jit_solution(2656174515942053189)
XLA Ops:
  0.6 189.7 %layer.1 = (bf16[24,288,256]{2,1,0:T(8,128)(2,1)}, bf16[288,1024]{1,0:T(8,128)(2,1)}, bf16[288,1024]{1,0:T(8,128)(2,1)}, f32[2,144,128]{2,1,0:T(8,128)}, f32[8,128]{1,0:T(8,128)}) custom-call(s32[57]{0:T(128)} %owners.3, f32[24,288,256]{2,1,0:T(8,128)} %w.1, bf16[288,1024]{1,0:T(8,128)(2,1)} %bitcast.5, bf16[288,1024]{1,0:T(8,128)(2,1)} %bitcast.6, ...), custom_call_target="tpu_custom_call" | custom-call | tf_op jit(solution)/shard_map/layer/pallas_call | solution.py:1084
  190.3 18.9 %adam.1 = (f32[24,288,256]{2,1,0:T(8,128)}, f32[24,288,256]{2,1,0:T(8,128)}, f32[24,288,256]{2,1,0:T(8,128)}, f32[3,288]{1,0:T(4,128)}, f32[3,288]{1,0:T(4,128)}...) custom-call(s32[57]{0:T(128)} %owners.3, ...), custom_call_target="tpu_custom_call" | custom-call | tf_op jit(solution)/shard_map/adam/pallas_call | solution.py:1158
